TPU v7x, 32 devices: a whole 2x2x4 slice. The times are simulated.
32 devices in a mesh: seq: 4 (over y, x), fsdp: 8 (over z, core).
Axes of the slice: x: 2, y: 2, z: 4, core: 2. Of those that a mesh axis runs over, the one named last changes fastest.
Arguments:
- tokens: bfloat16 [8, 2048, 1024], P('fsdp', 'seq'), may hold values from -17 to 17
- segments: int32 [8, 2048], P('fsdp'), may hold values from 0 to 10, as said below
- valid_mask: int32 [8, 2048], P('fsdp', 'seq'), may hold values 0 or 1
- norm_gains: float32 [2, 2, 1024], replicated, may hold values from 0.5 to 1.5
- head_gain: float32 [2, 128], replicated, may hold values from 0.5 to 1.5
- conv_weight: float32 [2, 4, 3072], replicated, may hold values from -3 to 3
- beta_weight: bfloat16 [2, 1024, 8], replicated, may hold values from -0.1875 to 0.1875
- qkv_weight: bfloat16 [2, 1024, 3072], P(None, 'fsdp'), may hold values from -0.1875 to 0.1875
- out_weight: bfloat16 [2, 1024, 1024], P(None, 'fsdp'), may hold values from -0.1875 to 0.1875
- gate_up_weight: bfloat16 [2, 1024, 5632], P(None, 'fsdp'), may hold values from -0.1875 to 0.1875
- down_weight: bfloat16 [2, 2816, 1024], P(None, 'fsdp'), may hold values from -0.109375 to 0.109375
- cotangent: bfloat16 [8, 2048, 1024], P('fsdp', 'seq'), may hold values from -17 to 17
Outputs:
- mixed: bfloat16 [8, 2048, 1024], P('fsdp', 'seq')
- d_tokens: float32 [8, 2048, 1024], P('fsdp', 'seq')
- d_norm_gains: float32 [2, 2, 1024], replicated
- d_head_gain: float32 [2, 128], replicated
- d_conv_weight: float32 [2, 4, 3072], replicated
- d_beta_weight: float32 [2, 1024, 8], replicated
- d_qkv_weight: float32 [2, 1024, 3072], P(None, 'fsdp')
- d_out_weight: float32 [2, 1024, 1024], P(None, 'fsdp')
- d_gate_up_weight: float32 [2, 1024, 5632], P(None, 'fsdp')
- d_down_weight: float32 [2, 2816, 1024], P(None, 'fsdp')
- rms_stats: float32 [2, 3], replicated
Inputs may be any that keep to these rules, and one draw needn't show every extreme that they name: `segments`: segment numbers start at 0 and rise by one at each document boundary; documents run 200 to 1024 tokens, except the last of a sequence, which may be cut shorter.
All inputs are finite; a program needn't handle non-finite values. No bound on the sum of `valid_mask` on one device may be relied on, other than what follows from the above.
Results may differ from a plain program's by a relative error of at most 0.025.
Values may be sent and summed in bfloat16 or wider, within the bound.
No kernel may reach another device: no remote copies, remote signals or barrier semaphores. Data moves between devices by JAX's collectives and lax.ppermute only.
A program may use at most 384 MiB of HBM per device.

v0:
```python
from functools import partial

import jax
import jax.numpy as jnp
from jax import lax
from jax.sharding import PartitionSpec as P

D = 1024
H = 8
HD = 128
KW = 4
STRETCH = 64
LAYERS = 2


highest = lax.Precision.HIGHEST
epsilon_norm = 1e-05
epsilon_unit = 1e-06


def shifted(block, axis, distance):
    devices = range(lax.axis_size(axis))
    route = [(i - distance, i) for i in devices if i - distance in devices]
    return lax.ppermute(block, axis, route)


def matmul(left, right):
    return jnp.dot(left, right, precision=highest, preferred_element_type=jnp.float32)


def root_norm(values, gain):
    return (
        values * lax.rsqrt(jnp.mean(values * values, axis=-1, keepdims=True) + epsilon_norm) * gain
    )


def short_filter(extended, doc_ext, filt):
    taps = filt.shape[0]
    row_count = extended.shape[0] - taps + 1
    current = doc_ext[taps - 1 :]
    summed = jnp.zeros((row_count, extended.shape[1]), jnp.float32)
    for offset in range(taps):
        same_doc = (doc_ext[offset : offset + row_count] == current).astype(jnp.float32)
        summed = summed + filt[offset] * extended[offset : offset + row_count] * same_doc[:, None]
    return jax.nn.silu(summed)


def delta_head(query, keys, values, strength, doc_ids, block_size):
    length, head_width = query.shape
    query = (
        query
        * lax.rsqrt(jnp.sum(query * query, axis=-1, keepdims=True) + epsilon_unit)
        * head_width ** (-0.5)
    )
    keys = keys * lax.rsqrt(jnp.sum(keys * keys, axis=-1, keepdims=True) + epsilon_unit)
    blocks = length // block_size
    ends = doc_ids[block_size - 1 :: block_size]
    before = jnp.concatenate([jnp.full((1,), -1, jnp.int32), ends[: blocks - 1]])
    row_index = lax.broadcasted_iota(jnp.int32, (block_size, block_size), 0)
    col_index = lax.broadcasted_iota(jnp.int32, (block_size, block_size), 1)
    identity = jnp.eye(block_size, dtype=jnp.float32)

    def advance(memory, block_items):
        query_b, keys_b, values_b, strength_b, doc_b, prior_doc = block_items
        same_doc = doc_b[:, None] == doc_b[None, :]
        lower_mask = (same_doc & (col_index < row_index)).astype(jnp.float32)
        upto_mask = (same_doc & (col_index <= row_index)).astype(jnp.float32)
        carry_on = (doc_b == prior_doc).astype(jnp.float32)
        tail_doc = (doc_b == doc_b[block_size - 1]).astype(jnp.float32)
        keys_scaled = keys_b * strength_b[:, None]
        system = identity + matmul(keys_scaled, keys_b.T) * lower_mask
        solved = jax.scipy.linalg.solve_triangular(
            system,
            jnp.concatenate([keys_scaled, values_b * strength_b[:, None]], axis=1),
            lower=True,
        )
        key_mix = solved[:, :head_width]
        value_mix = solved[:, head_width:]
        deltas = value_mix - carry_on[:, None] * matmul(key_mix, memory)
        output = carry_on[:, None] * matmul(query_b, memory) + matmul(
            matmul(query_b, keys_b.T) * upto_mask, deltas
        )
        memory = carry_on[block_size - 1] * memory + matmul(keys_b.T, tail_doc[:, None] * deltas)
        return (memory, output)

    block_items = (
        query.reshape(blocks, block_size, head_width),
        keys.reshape(blocks, block_size, head_width),
        values.reshape(blocks, block_size, head_width),
        strength.reshape(blocks, block_size),
        doc_ids.reshape(blocks, block_size),
        before,
    )
    last_memory, outputs = lax.scan(
        jax.checkpoint(advance), jnp.zeros((head_width, head_width), jnp.float32), block_items
    )
    return outputs.reshape(length, head_width)


def mix_heads(heads_all, logits_all, gain, doc_ids):
    mixed_heads = jax.vmap(
        partial(delta_head, doc_ids=doc_ids, block_size=STRETCH), in_axes=1, out_axes=1
    )(heads_all[:, 0], heads_all[:, 1], heads_all[:, 2], jax.nn.sigmoid(logits_all[:, 0, :, 0]))
    return root_norm(mixed_heads, gain)


def swiglu_act(gate_up):
    half_width = gate_up.shape[1] // 2
    return jax.nn.silu(gate_up[:, :half_width]) * gate_up[:, half_width:]


def contract_last(left, right):
    return lax.dot_general(
        left, right, (((1,), (1,)), ((), ())), preferred_element_type=jnp.float32
    )


def contract_first(left, right):
    return lax.dot_general(
        left, right, (((0,), (0,)), ((), ())), preferred_element_type=jnp.float32
    )


def fetch_rows(weights):
    return (
        lax.all_gather(weights[0], "fsdp", axis=0, tiled=True),
        lax.all_gather(weights[1], "fsdp", axis=0, tiled=True),
    )


def reduce_rows(left, right):
    return lax.psum_scatter(
        contract_first(left, right).astype(jnp.bfloat16), "fsdp", scatter_dimension=0, tiled=True
    ).astype(jnp.float32)


def on_device(
    tokens,
    segments,
    valid_mask,
    norm_gains,
    head_gain,
    conv_weight,
    beta_weight,
    qkv_weight,
    out_weight,
    gate_up_weight,
    down_weight,
    cotangent,
):
    tok_rows = tokens.shape[1]
    doc_ids = segments[0]
    doc_pad = jnp.concatenate([jnp.full((KW - 1,), -1, jnp.int32), doc_ids])
    piece_start = lax.axis_index("seq") * tok_rows
    doc_ext = lax.dynamic_slice_in_dim(doc_pad, piece_start, tok_rows + KW - 1)
    valid_rows = valid_mask[0].astype(jnp.float32)
    stream = tokens[0].astype(jnp.float32)
    square_sums = []
    stored = []
    for layer_at in range(LAYERS):
        qkv_full, out_full = fetch_rows((qkv_weight[layer_at], out_weight[layer_at]))
        gate_up_full, down_full = fetch_rows((gate_up_weight[layer_at], down_weight[layer_at]))
        square_sums.append(jnp.sum(jnp.sum(stream * stream, axis=1) * valid_rows))
        normed_one, pull_one = jax.vjp(root_norm, stream, norm_gains[layer_at, 0])
        normed_one = normed_one.astype(jnp.bfloat16)
        projected = jnp.dot(normed_one, qkv_full, preferred_element_type=jnp.float32).astype(
            jnp.bfloat16
        )
        logits = jnp.dot(
            normed_one, beta_weight[layer_at], preferred_element_type=jnp.float32
        ).astype(jnp.bfloat16)
        rim_rows = shifted(projected[tok_rows - KW + 1 :], "seq", 1)
        extended = jnp.concatenate([rim_rows, projected], axis=0).astype(jnp.float32)
        filtered, pull_filter = jax.vjp(
            lambda padded, taps_now: short_filter(padded, doc_ext, taps_now),
            extended,
            conv_weight[layer_at],
        )
        outgoing = filtered.astype(jnp.bfloat16).reshape(tok_rows, 3, H, HD)
        heads_all, logits_all = (
            lax.all_to_all(outgoing, "seq", split_axis=2, concat_axis=0, tiled=True),
            lax.all_to_all(
                logits.reshape(tok_rows, 1, H, 1), "seq", split_axis=2, concat_axis=0, tiled=True
            ),
        )
        head_out, pull_mix = jax.vjp(
            partial(mix_heads, doc_ids=doc_ids),
            heads_all.astype(jnp.float32),
            logits_all.astype(jnp.float32),
            head_gain[layer_at],
        )
        head_low = head_out.astype(jnp.bfloat16)
        attended = lax.all_to_all(head_low, "seq", split_axis=0, concat_axis=1, tiled=True).reshape(
            tok_rows, D
        )
        branch = jnp.dot(attended, out_full, preferred_element_type=jnp.float32)
        square_sums.append(jnp.sum(jnp.sum(branch * branch, axis=1) * valid_rows))
        stream = stream + branch
        normed_two, pull_two = jax.vjp(root_norm, stream, norm_gains[layer_at, 1])
        normed_two = normed_two.astype(jnp.bfloat16)
        gate_up = jnp.dot(normed_two, gate_up_full, preferred_element_type=jnp.float32)
        activated, pull_act = jax.vjp(swiglu_act, gate_up)
        activated = activated.astype(jnp.bfloat16)
        branch = jnp.dot(activated, down_full, preferred_element_type=jnp.float32)
        square_sums.append(jnp.sum(jnp.sum(branch * branch, axis=1) * valid_rows))
        stream = stream + branch
        stored.append(
            (
                qkv_full,
                out_full,
                gate_up_full,
                down_full,
                pull_one,
                normed_one,
                pull_filter,
                pull_mix,
                attended,
                pull_two,
                normed_two,
                pull_act,
                activated,
            )
        )
    stream_grad = cotangent[0].astype(jnp.float32) * valid_rows[:, None]
    gain_list = []
    head_list = []
    filter_list = []
    beta_list = []
    qkv_list = []
    out_list = []
    gate_list = []
    down_list = []
    for layer_at in reversed(range(LAYERS)):
        (
            qkv_full,
            out_full,
            gate_up_full,
            down_full,
            pull_one,
            normed_one,
            pull_filter,
            pull_mix,
            attended,
            pull_two,
            normed_two,
            pull_act,
            activated,
        ) = stored[layer_at]
        qkv_full, out_full = fetch_rows((qkv_weight[layer_at], out_weight[layer_at]))
        gate_up_full, down_full = fetch_rows((gate_up_weight[layer_at], down_weight[layer_at]))
        branch_low = stream_grad.astype(jnp.bfloat16)
        grad_down = reduce_rows(activated, branch_low)
        (grad_gate_up,) = pull_act(contract_last(branch_low, down_full))
        grad_gate_up = grad_gate_up.astype(jnp.bfloat16)
        grad_gate = reduce_rows(normed_two, grad_gate_up)
        grad_state, gain_two = pull_two(contract_last(grad_gate_up, gate_up_full))
        stream_grad = stream_grad + grad_state
        branch_low = stream_grad.astype(jnp.bfloat16)
        grad_out = reduce_rows(attended, branch_low)
        grad_heads = (
            contract_last(branch_low, out_full).astype(jnp.bfloat16).reshape(tok_rows, H, HD)
        )
        grad_heads = lax.all_to_all(grad_heads, "seq", split_axis=1, concat_axis=0, tiled=True)
        grad_mix, grad_logits, gain_head = pull_mix(grad_heads.astype(jnp.float32))
        back_mix, back_logits = (
            lax.all_to_all(
                grad_mix.astype(jnp.bfloat16), "seq", split_axis=0, concat_axis=2, tiled=True
            ),
            lax.all_to_all(
                grad_logits.astype(jnp.bfloat16), "seq", split_axis=0, concat_axis=2, tiled=True
            ),
        )
        grad_ext, grad_filter = pull_filter(back_mix.reshape(tok_rows, 3 * D).astype(jnp.float32))
        returned = shifted(grad_ext[: KW - 1].astype(jnp.bfloat16), "seq", -1).astype(jnp.float32)
        grad_proj = grad_ext[KW - 1 :]
        grad_proj = jnp.concatenate(
            [grad_proj[: tok_rows - KW + 1], grad_proj[tok_rows - KW + 1 :] + returned], axis=0
        ).astype(jnp.bfloat16)
        grad_logit_rows = back_logits.reshape(tok_rows, H)
        grad_qkv = reduce_rows(normed_one, grad_proj)
        grad_beta = contract_first(normed_one, grad_logit_rows)
        grad_normed = contract_last(grad_proj, qkv_full) + contract_last(
            grad_logit_rows, beta_weight[layer_at]
        )
        grad_state, gain_one = pull_one(grad_normed)
        stream_grad = stream_grad + grad_state
        grad_qkv, grad_out, grad_gate, grad_down = (
            lax.psum(grad_qkv.astype(jnp.bfloat16), "seq").astype(jnp.float32),
            lax.psum(grad_out.astype(jnp.bfloat16), "seq").astype(jnp.float32),
            lax.psum(grad_gate.astype(jnp.bfloat16), "seq").astype(jnp.float32),
            lax.psum(grad_down.astype(jnp.bfloat16), "seq").astype(jnp.float32),
        )
        gain_list.append(jnp.stack([gain_one, gain_two]))
        head_list.append(gain_head)
        filter_list.append(grad_filter)
        beta_list.append(grad_beta)
        qkv_list.append(grad_qkv)
        out_list.append(grad_out)
        gate_list.append(grad_gate)
        down_list.append(grad_down)
    stats_sum, valid_count, gains_sum, head_sum, filter_sum, beta_sum = lax.psum(
        (
            jnp.stack(square_sums),
            jnp.sum(valid_rows),
            jnp.stack(gain_list[::-1]),
            jnp.stack(head_list[::-1]),
            jnp.stack(filter_list[::-1]),
            jnp.stack(beta_list[::-1]),
        ),
        ("seq", "fsdp"),
    )
    rms_stats = jnp.sqrt(stats_sum / (jnp.maximum(valid_count, 1.0) * D)).reshape(LAYERS, 3)
    return (
        stream.astype(jnp.bfloat16)[None],
        stream_grad[None],
        gains_sum,
        head_sum,
        filter_sum,
        beta_sum,
        jnp.stack(qkv_list[::-1]),
        jnp.stack(out_list[::-1]),
        jnp.stack(gate_list[::-1]),
        jnp.stack(down_list[::-1]),
        rms_stats,
    )


def solution(mesh):
    return jax.shard_map(
        on_device,
        mesh=mesh,
        in_specs=(
            P("fsdp", "seq", None),
            P("fsdp", None),
            P("fsdp", "seq"),
            P(),
            P(),
            P(),
            P(),
            P(None, "fsdp", None),
            P(None, "fsdp", None),
            P(None, "fsdp", None),
            P(None, "fsdp", None),
            P("fsdp", "seq", None),
        ),
        out_specs=(
            P("fsdp", "seq", None),
            P("fsdp", "seq", None),
            P(),
            P(),
            P(),
            P(),
            P(None, "fsdp", None),
            P(None, "fsdp", None),
            P(None, "fsdp", None),
            P(None, "fsdp", None),
            P(),
        ),
        check_vma=False,
    )
```

profile of v0, /device:TPU:0, one launch (start us, length us, event | category | flops | bytes accessed | tf_op | source)
XLA Modules:
  0.0 4554.3 jit_solution(11951980701082770093)
XLA Ops:
  25.8 52.0 %all-gather.17.cloned.1.call-done = bf16[1,1024,3072]{2,1,0:T(8,128)(2,1)} async-done(((bf16[1,128,3072]{2,1,0:T(8,128)(2,1)}), bf16[1,1024,3072]{2,1,0:T(8,128)(2,1)}) %all-gather.17.cloned.1.call-update) | async-done | bytes 6291472 | tf_op jit(solution)/shard_map/all_gather | solution.py:126
  109.7 32.9 all-to-all-done
  157.3 791.4 %while.76 = (s32[]{:T(128)}, f32[2,128,128]{2,1,0:T(8,128)S(1)}, f32[32,2,64,128]{3,2,0,1:T(8,128)S(1)}, f32[32,2,128,128]{3,2,1,0:T(8,128)}, s32[32,64]{1,0:T(8...) while((s32[]{:T(128)}, f32[2,128,128]{2,1,0:T(8,128)S(1)}, ...), condition=%wide.region_4.0_spmd.clone, body=%wide.region_3.0_spmd.clone.sunk | while | flops 138830080 | bytes 2522550 | solution.py:94
  959.5 17.1 all_to_all.132
  1040.6 34.0 all-to-all-done.3
  1089.5 704.4 %while.77 = (s32[]{:T(128)}, f32[2,128,128]{2,1,0:T(8,128)S(1)}, f32[32,2,64,128]{3,2,0,1:T(8,128)S(1)}, f32[32,2,128,128]{3,2,1,0:T(8,128)}, s32[32,64]{1,0:T(8...) while((s32[]{:T(128)}, f32[2,128,128]{2,1,0:T(8,128)S(1)}, ...), condition=%wide.region_11.13_spmd.clone, body=%wide.region_10.12_spmd.clone.sunk | while | flops 138830080 | bytes 2506166 | solution.py:94
  1855.5 14.6 multiply_reduce_fusion.16
  1907.7 823.3 %while.78 = (s32[]{:T(128)}, f32[2,128,128]{2,1,0:T(8,128)S(1)}, f32[32,2,64,128]{3,2,0,1:T(8,128)S(1)}, f32[32,2,64,128]{3,2,0,1:T(8,128)}, f32[32,2,64,128]{3,...) while((s32[]{:T(128)}, f32[2,128,128]{2,1,0:T(8,128)S(1)}, ...), condition=%wide.region_19.22_spmd.clone, body=%wide.region_16.21_spmd.clone.sunk | while | flops 359374976 | bytes 6644227 | solution.py:94
  2760.7 28.4 copy.332
  2803.0 25.3 all-to-all-done.7
  2845.9 16.5 multiply_reduce_fusion.7
  2906.8 13.5 multiply_reduce_fusion.18
  2975.9 849.5 %while.79 = (s32[]{:T(128)}, f32[2,128,128]{2,1,0:T(8,128)S(1)}, f32[32,2,64,128]{3,2,0,1:T(8,128)S(1)}, f32[32,2,64,128]{3,2,0,1:T(8,128)}, f32[32,2,64,128]{3,...) while((s32[]{:T(128)}, f32[2,128,128]{2,1,0:T(8,128)S(1)}, ...), condition=%wide.region_28.31_spmd.clone, body=%wide.region_25.30_spmd.clone.sunk | while | flops 359374976 | bytes 6644227 | solution.py:94
  3835.5 28.6 copy.349
  3864.1 38.3 all_to_all.133
  3920.0 15.2 multiply_reduce_fusion.11
  3963.6 14.0 convolution_convert_fusion
  3979.1 13.9 convolution_convert_fusion.1
  3993.3 36.3 reduce-scatter.9.cloned.1.call-done
  4029.6 119.9 %reduce-scatter.19.cloned.1.call-done = bf16[128,5632]{1,0:T(8,128)(2,1)} async-done(((bf16[1024,5632]{1,0:T(8,128)(2,1)}), bf16[128,5632]{1,0:T(8,128)(2,1)}) %reduce-scatter.19.cloned.1.call-update) | async-done | bytes 1441808 | tf_op jit(solution)/shard_map/reduce_scatter | solution.py:132
  4149.4 119.9 %reduce-scatter.17.cloned.1.call-done = bf16[128,5632]{1,0:T(8,128)(2,1)} async-done(((bf16[1024,5632]{1,0:T(8,128)(2,1)}), bf16[128,5632]{1,0:T(8,128)(2,1)}) %reduce-scatter.17.cloned.1.call-update) | async-done | bytes 1441808 | tf_op jit(solution)/shard_map/reduce_scatter | solution.py:132
  4313.3 37.4 all-reduce.31
  4355.7 60.0 %all-reduce.39.cloned.1.call-done = (bf16[1,128,3072]{2,1,0:T(8,128)(2,1)}, bf16[1,128,3072]{2,1,0:T(8,128)(2,1)}, bf16[1,128,1024]{2,1,0:T(8,128)(2,1)}, bf16[1...) async-done(((bf16[1,128,3072]{2,1,0:T(8,128)(2,1)}, ...) | async-done | bytes 6422544 | tf_op jit(solution)/shard_map/psum | solution.py:288
  4424.9 119.3 %all-reduce.37.cloned.1.call-done = (f32[2,4,3072]{2,1,0:T(4,128)}, f32[2,1024,8]{1,2,0:T(8,128)}) async-done(((f32[2,4,3072]{2,1,0:T(4,128)}, f32[2,1024,8]{1,2,0:T(8,128)}), (f32[2,4,3072]{2,1,0:T(4,128)}, f32[2,1024,8]{1,2,0:T(8,128)})) %all-reduce.37.cloned.1.call-update) | async-done | bytes 163856 | tf_op jit(solution)/shard_map/psum | solution.py:301
  (4189 shorter events, 3679.4 us)
Async XLA Ops:
  7.2 70.6 %all-gather.17.cloned.1.call-start = ((), (), s32[]{:S(2)}) async-start(), calls=%async_computation.28 | async-start | bytes 7077888 | tf_op jit(solution)/shard_map/all_gather | solution.py:126
  10.0 968.1 %all-gather.19.cloned.1.call-start = ((), (), s32[]{:S(2)}) async-start(), calls=%async_computation.29 | async-start | bytes 2359296 | tf_op jit(solution)/shard_map/all_gather | solution.py:127
  10.9 971.2 %all-gather.21.cloned.1.call-start = ((), (), s32[]{:S(2)}) async-start(), calls=%async_computation.30 | async-start | bytes 12976128 | tf_op jit(solution)/shard_map/all_gather | solution.py:126
  12.8 986.3 %all-gather.23.cloned.1.call-start = ((), (), s32[]{:S(2)}) async-start(), calls=%async_computation.31 | async-start | bytes 6488064 | tf_op jit(solution)/shard_map/all_gather | solution.py:127
  15.5 992.2 %all-gather.25.cloned.1.call-start = ((), (), s32[]{:S(2)}) async-start(), calls=%async_computation.32 | async-start | bytes 7077888 | tf_op jit(solution)/shard_map/all_gather | solution.py:126
  19.2 80.9 %all-to-all-start.1 = ((bf16[4,2,512]{2,1,0:T(2,128)(2,1)}), bf16[4,2,512]{2,1,0:T(2,128)(2,1)S(1)}, u32[]{:S(2)}, u32[]{:S(2)}) async-start(bf16[4,2,512]{2,1,0:T(2,128)(2,1)} %reshape.807), calls=%async_computation.1 | async-start | bytes 16384 | tf_op jit(solution)/shard_map/all_to_all | solution.py:182
  24.4 1800.2 %all-gather.27.cloned.1.call-start = ((), (), s32[]{:S(2)}) async-start(), calls=%async_computation.33 | async-start | bytes 2359296 | tf_op jit(solution)/shard_map/all_gather | solution.py:127
  100.2 42.4 all-to-all-start
  105.0 1725.4 %all-gather.29.cloned.1.call-start = ((), (), s32[]{:S(2)}) async-start(), calls=%async_computation.34 | async-start | bytes 12976128 | tf_op jit(solution)/shard_map/all_gather | solution.py:126
  1035.0 39.6 all-to-all-start.3
  1039.7 803.0 %all-gather.31.cloned.1.call-start = ((), (), s32[]{:S(2)}) async-start(), calls=%async_computation.35 | async-start | bytes 6488064 | tf_op jit(solution)/shard_map/all_gather | solution.py:127
  2751.3 37.8 all-to-all-start.8
  2789.1 39.2 all-to-all-start.7
  2793.2 1199.9 %reduce-scatter.15.cloned.1.call-start = ((), (), s32[]{:S(2)}) async-start(), calls=%async_computation.23 | async-start | bytes 2359296 | tf_op jit(solution)/shard_map/reduce_scatter | solution.py:132
  2798.2 1195.0 %reduce-scatter.13.cloned.1.call-start = ((), (), s32[]{:S(2)}) async-start(), calls=%async_computation.22 | async-start | bytes 2359296 | tf_op jit(solution)/shard_map/reduce_scatter | solution.py:132
  2927.1 1066.1 %reduce-scatter.23.cloned.1.call-start = ((), (), s32[]{:S(2)}) async-start(), calls=%async_computation.27 | async-start | bytes 6488064 | tf_op jit(solution)/shard_map/reduce_scatter | solution.py:132
  2934.3 1059.0 %reduce-scatter.21.cloned.1.call-start = ((), (), s32[]{:S(2)}) async-start(), calls=%async_computation.26 | async-start | bytes 6488064 | tf_op jit(solution)/shard_map/reduce_scatter | solution.py:132
  2948.8 17.8 all-to-all-start.9
  2954.1 1039.1 %reduce-scatter.11.cloned.1.call-start = ((), (), s32[]{:S(2)}) async-start(), calls=%async_computation.21 | async-start | bytes 7077888 | tf_op jit(solution)/shard_map/reduce_scatter | solution.py:132
  2961.5 1068.0 %reduce-scatter.9.cloned.1.call-start = ((), (), s32[]{:S(2)}) async-start(), calls=%async_computation.20 | async-start | bytes 7077888 | tf_op jit(solution)/shard_map/reduce_scatter | solution.py:132
  3962.0 187.4 %reduce-scatter.19.cloned.1.call-start = ((), (), s32[]{:S(2)}) async-start(), calls=%async_computation.25 | async-start | bytes 12976128 | tf_op jit(solution)/shard_map/reduce_scatter | solution.py:132
  3977.6 291.7 %reduce-scatter.17.cloned.1.call-start = ((), (), s32[]{:S(2)}) async-start(), calls=%async_computation.24 | async-start | bytes 12976128 | tf_op jit(solution)/shard_map/reduce_scatter | solution.py:132
  3993.1 422.7 %all-reduce.39.cloned.1.call-start = ((), (), s32[]{:S(2)}) async-start(), calls=%async_computation.37 | async-start | bytes 12845056 | tf_op jit(solution)/shard_map/psum | solution.py:288
  4288.3 255.9 %all-reduce.37.cloned.1.call-start = ((), (), s32[]{:S(2)}) async-start(), calls=%async_computation.36 | async-start | bytes 327680 | tf_op jit(solution)/shard_map/psum | solution.py:301
  (133 other events, 4913.3 us)
Sparse Core Ops, SparseCore 0:
  10.2 67.4 all-gather.16
  79.4 27.6 all-gather.18
  109.3 107.7 all-gather.20
  218.6 58.6 all-gather.22
  279.4 63.4 all-gather.24
  344.3 28.0 all-gather.26
  374.6 107.5 all-gather.28
  1042.1 59.1 all-gather.30
  2798.3 34.3 reduce-scatter.14
  2927.2 35.5 reduce-scatter.12
  2965.2 63.4 reduce-scatter.22
  3030.8 63.3 reduce-scatter.20
  3096.5 68.0 reduce-scatter.10
  3962.1 67.4 reduce-scatter.8
  4031.7 117.6 reduce-scatter.18
  4151.6 117.6 reduce-scatter.16
  4273.8 141.9 all-reduce.38
  4421.8 122.3 all-reduce.36
where the time goes:
time: 4600 us; the launch traced here: 4550 us
  other arithmetic  1850 us (40%)
  matrix products  1060 us (23%)
  local copies, waits for them, and re-layouts  824 us (18%)
  waiting for transfers between devices  645 us (14%)
  blocking collectives  92.9 us (2%)
  starting transfers between devices  52.3 us (1%)
    another operation x192, other arithmetic, advance(): jax.scipy.linalg.solve_triangular(system, jnp.concatenate([keys_scaled, v...  1280 us
    dot_general x1344, matrix products, matmul(): jnp.dot(left, right, precision=highest, preferred_element_type=jnp.float32)  736 us
    squeeze x384, local copies, waits for them, and re-layouts, delta_head(): lax.scan(jax.checkpoint(advance), jnp.zeros((head_width, head_width), jnp...  290 us
    reduce_scatter x8, waiting for transfers between devices, reduce_rows(): lax.psum_scatter(contract_first(left, right).astype(jnp.bfloat16), 'fsdp'...  276 us
    dynamic_slice x128, local copies, waits for them, and re-layouts, delta_head(): lax.scan(jax.checkpoint(advance), jnp.zeros((head_width, head_width), jnp...  160 us
    convert_element_type x128, other arithmetic, advance(): tail_doc = (doc_b == doc_b[block_size - 1]).astype(jnp.float32)  121 us
    psum x1, waiting for transfers between devices, on_device(): lax.psum((jnp.stack(square_sums), jnp.sum(valid_rows), jnp.stack(gain_lis...  119 us
    another operation x256, matrix products, advance(): jax.scipy.linalg.solve_triangular(system, jnp.concatenate([keys_scaled, v...  98.3 us

commit v1 on v0

v1 whole, which is shorter than its diff:
```python
from functools import partial
import jax
import jax.numpy as jnp
from jax import lax
from jax.experimental import pallas as pl
from jax.experimental.pallas import tpu as pltpu
from jax.sharding import PartitionSpec as P

D = 1024
H = 8
HD = 128
KW = 4
CHUNK = 128
HALO = 8
f32 = jnp.float32
bf16 = jnp.bfloat16
EPS_NORM = 1e-05
EPS_UNIT = 1e-06
VMEM_LIMIT = 48 * 1024 * 1024


def dot_nn(a, b):
    return lax.dot_general(a.astype(bf16), b.astype(bf16), (((1,), (0,)), ((), ())), preferred_element_type=f32)


def dot_nt(a, b):
    return lax.dot_general(a.astype(bf16), b.astype(bf16), (((1,), (1,)), ((), ())), preferred_element_type=f32)


def dot_tn(a, b):
    return lax.dot_general(a.astype(bf16), b.astype(bf16), (((0,), (0,)), ((), ())), preferred_element_type=f32)


def sigmoid(x):
    return 1.0 / (1.0 + jnp.exp(-x))


def conv_masks(dcol_ref, rows):
    here = dcol_ref[pl.ds(HALO, rows), :]
    return [
        jnp.broadcast_to((dcol_ref[pl.ds(HALO - KW + 1 + i, rows), :] == here).astype(f32), (rows, HD))
        for i in range(KW - 1)
    ]


def conv_sum(x_ref, halo_ref, taps_ref, masks, ext):
    rows = x_ref.shape[0]
    ext[pl.ds(0, HALO), :] = halo_ref[...].astype(f32)
    ext[pl.ds(HALO, rows), :] = x_ref[...].astype(f32)
    total = taps_ref[pl.ds(KW - 1, 1), :] * ext[pl.ds(HALO, rows), :]
    for i in range(KW - 1):
        total = total + taps_ref[pl.ds(i, 1), :] * ext[pl.ds(HALO - KW + 1 + i, rows), :] * masks[i]
    return total


def low(x):
    return x.astype(bf16).astype(f32)


def unit_scale(x):
    return lax.rsqrt(jnp.sum(x * x, axis=-1, keepdims=True) + EPS_UNIT)


def head_column(table, head):
    lane = lax.broadcasted_iota(jnp.int32, table.shape, 1)
    return jnp.sum(jnp.where(lane == head, table, 0.0), axis=1, keepdims=True)


def chunk_marks(dcol_ref, c):
    at = HALO + c * CHUNK
    docs = dcol_ref[pl.ds(at, CHUNK), :]
    prior = dcol_ref[pl.ds(at - 1, 1), :]
    last = dcol_ref[pl.ds(at + CHUNK - 1, 1), :]
    carry = (docs == prior).astype(f32)
    tail = (docs == last).astype(f32)
    carry_last = (last == prior).astype(f32)
    return docs, carry, tail, carry_last


def tri_index():
    row = lax.broadcasted_iota(jnp.int32, (CHUNK, CHUNK), 0)
    col = lax.broadcasted_iota(jnp.int32, (CHUNK, CHUNK), 1)
    return row, col


def inverses(systems, differ):
    row, col = tri_index()
    eye = (row == col).astype(f32)
    found = [eye - jnp.where(differ == 1, low_part, 0.0) for low_part in systems]
    step = 2
    while step < CHUNK:
        side = (differ >= step) & (differ < 2 * step)
        lows = [x.astype(bf16) for x in found]
        inner = [dot_nn(jnp.where(side, s, 0.0), x) for s, x in zip(systems, lows)]
        outer = [dot_nn(x, y) for x, y in zip(lows, inner)]
        found = [x - y for x, y in zip(found, outer)]
        step *= 2
    return found


def fwd_local_kernel(
    q_ref, k_ref, v_ref, hq_ref, hk_ref, hv_ref, tq_ref, tk_ref, tv_ref, lg_ref, dcol_ref, drow_ref,
    qn_ref, kn_ref, tinv_ref, wu_ref, gain_ref, pre_ref, total_ref, ext,
):
    head = pl.program_id(0)
    rows = q_ref.shape[0]
    chunks = rows // CHUNK
    masks = conv_masks(dcol_ref, rows)

    def filtered(x, halo, taps):
        s = conv_sum(x, halo, taps, masks, ext)
        return low(s * sigmoid(s))

    query = filtered(q_ref, hq_ref, tq_ref)
    qn_ref[...] = (query * (unit_scale(query) * HD**-0.5)).astype(bf16)
    keys = filtered(k_ref, hk_ref, tk_ref)
    kn = keys * unit_scale(keys)
    kn_ref[...] = kn.astype(bf16)
    values = filtered(v_ref, hv_ref, tv_ref)
    beta = sigmoid(head_column(lg_ref[...].astype(f32), head))
    kb = beta * kn
    vb = beta * values
    row, col = tri_index()
    differ = row ^ col
    marks = [chunk_marks(dcol_ref, c) for c in range(chunks)]
    cut = lambda x, c: x[c * CHUNK : (c + 1) * CHUNK]
    systems = []
    for c in range(chunks):
        docs = marks[c][0]
        keep = (docs == drow_ref[pl.ds(c, 1), :]) & (col < row)
        systems.append(jnp.where(keep, dot_nt(cut(kb, c), cut(kn, c)), 0.0))
    found = inverses(systems, differ)
    both = [
        dot_nn(found[c], jnp.concatenate([cut(kb, c), cut(vb, c)], axis=1)) for c in range(chunks)
    ]
    state = None
    eye = (row == col).astype(f32)
    for c in range(chunks):
        tinv_ref[0, pl.ds(c * CHUNK, CHUNK), :] = found[c].astype(bf16)
        _, carry, tail, carry_last = marks[c]
        w, u = both[c][:, :HD], both[c][:, HD:]
        wu_ref[0, pl.ds(c * CHUNK, CHUNK), :] = both[c].astype(bf16)
        step = dot_tn(cut(kn, c) * tail, jnp.concatenate([w * carry, u], axis=1))
        gain_ref[0, pl.ds(c * CHUNK, CHUNK), :] = step[:, :HD].astype(bf16)
        if c == 0:
            state = jnp.concatenate([eye, jnp.zeros_like(eye)], axis=1)
        pre_ref[0, pl.ds(c * CHUNK, CHUNK), :] = state.astype(bf16)
        moved = carry_last * state - dot_nn(step[:, :HD], state)
        state = jnp.concatenate([moved[:, :HD], moved[:, HD:] + step[:, HD:]], axis=1)
    total_ref[0] = state.astype(bf16)


def col_spec(rows, base):
    return pl.BlockSpec((rows, HD), lambda h: (0, base + h))


def full_spec(shape):
    return pl.BlockSpec(shape, lambda h: (0,) * len(shape))


def head_spec(shape):
    return pl.BlockSpec((1,) + shape, lambda h: (h,) + (0,) * len(shape))


def params():
    return pltpu.CompilerParams(vmem_limit_bytes=VMEM_LIMIT, dimension_semantics=("arbitrary",))


def cost(units, rows, traffic):
    return pl.CostEstimate(flops=2 * units * HD * HD * HD * H * (rows // CHUNK), bytes_accessed=traffic, transcendentals=0)


def fwd_local(projected, halo, taps, logits, dcol, drow):
    rows = projected.shape[0]
    chunks = rows // CHUNK
    sds = jax.ShapeDtypeStruct
    return pl.pallas_call(
        fwd_local_kernel,
        grid=(H,),
        in_specs=[col_spec(rows, 0), col_spec(rows, H), col_spec(rows, 2 * H)]
        + [col_spec(HALO, 0), col_spec(HALO, H), col_spec(HALO, 2 * H)]
        + [col_spec(KW, 0), col_spec(KW, H), col_spec(KW, 2 * H)]
        + [full_spec((rows, H)), full_spec((rows + HALO, 1)), full_spec((chunks, CHUNK))],
        out_specs=[
            col_spec(rows, 0),
            col_spec(rows, 0),
            head_spec((rows, CHUNK)),
            head_spec((rows, 2 * HD)),
            head_spec((rows, HD)),
            head_spec((rows, 2 * HD)),
            head_spec((HD, 2 * HD)),
        ],
        out_shape=[
            sds((rows, D), bf16),
            sds((rows, D), bf16),
            sds((H, rows, CHUNK), bf16),
            sds((H, rows, 2 * HD), bf16),
            sds((H, rows, HD), bf16),
            sds((H, rows, 2 * HD), bf16),
            sds((H, HD, 2 * HD), bf16),
        ],
        scratch_shapes=[pltpu.VMEM((rows + HALO, HD), f32)],
        compiler_params=params(),
        cost_estimate=cost(60, rows, rows * D * 24),
        name="delta_local",
    )(*([projected] * 3 + [halo] * 3 + [taps] * 3 + [logits, dcol, drow]))


def fwd_read_kernel(qn_ref, kn_ref, wu_ref, dcol_ref, drow_ref, r_ref, o_ref):
    rows = qn_ref.shape[0]
    row, col = tri_index()
    for c in range(rows // CHUNK):
        at = pl.ds(c * CHUNK, CHUNK)
        docs, carry, _, _ = chunk_marks(dcol_ref, c)
        keep = (docs == drow_ref[pl.ds(c, 1), :]) & (col <= row)
        part = jnp.where(keep, dot_nt(qn_ref[at, :], kn_ref[at, :]), 0.0)
        w = wu_ref[0, at, :HD].astype(f32) * carry
        both = dot_nn(part, jnp.concatenate([w.astype(bf16), wu_ref[0, at, HD:]], axis=1))
        r_ref[at, :] = (qn_ref[at, :].astype(f32) * carry - both[:, :HD]).astype(bf16)
        o_ref[at, :] = both[:, HD:]


def fwd_read(qn, kn, wu, dcol, drow):
    rows = qn.shape[0]
    chunks = rows // CHUNK
    sds = jax.ShapeDtypeStruct
    return pl.pallas_call(
        fwd_read_kernel,
        grid=(H,),
        in_specs=[col_spec(rows, 0), col_spec(rows, 0), head_spec((rows, 2 * HD)), full_spec((rows + HALO, 1)), full_spec((chunks, CHUNK))],
        out_specs=[col_spec(rows, 0), col_spec(rows, 0)],
        out_shape=[sds((rows, D), bf16), sds((rows, D), f32)],
        compiler_params=params(),
        cost_estimate=cost(20, rows, rows * D * 14),
        name="delta_read",
    )(qn, kn, wu, dcol, drow)


def fwd_state_kernel(*refs):
    *near_refs, far_ref, pre_ref, r_ref, o_ref, gain_ref, state_ref, out_ref, head_ref = refs
    rows = r_ref.shape[0]
    state = far_ref[0].astype(f32)
    for near_ref in reversed(near_refs):
        state = dot_nn(near_ref[0, :, :HD], state) + near_ref[0, :, HD:].astype(f32)
    for c in range(rows // CHUNK):
        at = pl.ds(c * CHUNK, CHUNK)
        now = dot_nn(pre_ref[0, at, :HD], state) + pre_ref[0, at, HD:].astype(f32)
        state_ref[0, at, :] = now.astype(bf16)
        o = o_ref[at, :] + dot_nn(r_ref[at, :], now)
        out_ref[at, :] = o
        scale = lax.rsqrt(jnp.mean(o * o, axis=-1, keepdims=True) + EPS_NORM)
        head_ref[at, :] = (o * scale * gain_ref[...]).astype(bf16)


def fwd_state(nears, far, pre, r, o, gain):
    rows = r.shape[0]
    sds = jax.ShapeDtypeStruct
    return pl.pallas_call(
        fwd_state_kernel,
        grid=(H,),
        in_specs=[
            *[head_spec((HD, 2 * HD)) for _ in nears],
            head_spec((HD, HD)),
            head_spec((rows, 2 * HD)),
            col_spec(rows, 0),
            col_spec(rows, 0),
            full_spec((1, HD)),
        ],
        out_specs=[head_spec((rows, HD)), col_spec(rows, 0), col_spec(rows, 0)],
        out_shape=[sds((H, rows, HD), bf16), sds((rows, D), f32), sds((rows, D), bf16)],
        compiler_params=params(),
        cost_estimate=cost(10, rows, rows * D * 14),
        name="delta_state",
    )(*nears, far, pre, r, o, gain)


def bwd_local_kernel(dhead_ref, o_ref, r_ref, gain_ref, step_ref, dcol_ref, do_ref, dgain_ref, total_ref):
    rows = o_ref.shape[0]
    chunks = rows // CHUNK

    @pl.when(pl.program_id(0) == 0)
    def _():
        dgain_ref[...] = jnp.zeros_like(dgain_ref)

    o = o_ref[...]
    dy = dhead_ref[...].astype(f32)
    scale = lax.rsqrt(jnp.mean(o * o, axis=-1, keepdims=True) + EPS_NORM)
    x = o * scale
    dgain_ref[...] += jnp.sum(dy * x, axis=0, keepdims=True)
    dx = dy * gain_ref[...]
    do = scale * (dx - x * jnp.mean(dx * x, axis=-1, keepdims=True))
    do_ref[...] = do.astype(bf16)
    gives = [dot_tn(r_ref[pl.ds(c * CHUNK, CHUNK), :], do[c * CHUNK : (c + 1) * CHUNK]) for c in range(chunks)]
    state = jnp.zeros((HD, HD), f32)
    for c in reversed(range(chunks)):
        carry_last = chunk_marks(dcol_ref, c)[3]
        if c == chunks - 1:
            state = gives[c]
        else:
            state = carry_last * state - dot_tn(step_ref[0, pl.ds(c * CHUNK, CHUNK), :], state) + gives[c]
    total_ref[0] = state.astype(bf16)


def bwd_local(dhead, o, r, gain, step, dcol):
    rows = o.shape[0]
    sds = jax.ShapeDtypeStruct
    return pl.pallas_call(
        bwd_local_kernel,
        grid=(H,),
        in_specs=[col_spec(rows, 0), col_spec(rows, 0), col_spec(rows, 0), full_spec((1, HD)), head_spec((rows, HD)), full_spec((rows + HALO, 1))],
        out_specs=[col_spec(rows, 0), full_spec((1, HD)), head_spec((HD, HD))],
        out_shape=[sds((rows, D), bf16), sds((1, HD), f32), sds((H, HD, HD), bf16)],
        compiler_params=params(),
        cost_estimate=cost(12, rows, rows * D * 12),
        name="delta_back_local",
    )(dhead, o, r, gain, step, dcol)


def bwd_main_kernel(moves, *refs):
    later, refs = refs[: 2 * moves + 1], refs[2 * moves + 1 :]
    bwd_main_body(later, *refs)


def bwd_main_body(
    later, q_ref, k_ref, v_ref, hq_ref, hk_ref, hv_ref, tq_ref, tk_ref, tv_ref, lg_ref, dcol_ref, drow_ref,
    tinv_ref, wu_ref, step_ref, state_ref, r_ref, do_ref,
    dq_ref, dk_ref, dv_ref, rq_ref, rk_ref, rv_ref, cq_ref, ck_ref, cv_ref, dl_ref, ext, grad,
):
    head = pl.program_id(0)
    rows = q_ref.shape[0]
    chunks = rows // CHUNK
    masks = conv_masks(dcol_ref, rows)
    row, col = tri_index()
    cut = lambda x, c: x[c * CHUNK : (c + 1) * CHUNK]

    def filtered(x, halo, taps):
        s = conv_sum(x, halo, taps, masks, ext)
        gate = sigmoid(s)
        return low(s * gate), gate * (1.0 + s * (1.0 - gate))

    query, slope_q = filtered(q_ref, hq_ref, tq_ref)
    scale_q = unit_scale(query)
    qn = query * scale_q * HD**-0.5
    keys, slope_k = filtered(k_ref, hk_ref, tk_ref)
    scale_k = unit_scale(keys)
    kn = keys * scale_k
    values, slope_v = filtered(v_ref, hv_ref, tv_ref)
    beta = sigmoid(head_column(lg_ref[...].astype(f32), head))
    kb = beta * kn

    moves = len(later) // 2
    ds = later[-1][0].astype(f32)
    for i in reversed(range(moves)):
        ds = dot_tn(later[i][0], ds) + later[moves + i][0].astype(f32)
    marks = [chunk_marks(dcol_ref, c) for c in range(chunks)]
    leaving = [None] * chunks
    gives = [dot_tn(r_ref[pl.ds(c * CHUNK, CHUNK), :], do_ref[pl.ds(c * CHUNK, CHUNK), :]) for c in range(chunks)]
    for c in reversed(range(chunks)):
        leaving[c] = ds.astype(bf16)
        if c:
            ds = marks[c][3] * ds - dot_tn(step_ref[0, pl.ds(c * CHUNK, CHUNK), :], ds) + gives[c]

    dqs, dks, dvs, dbs = [], [], [], []
    for c in range(chunks):
        at = pl.ds(c * CHUNK, CHUNK)
        docs, carry, tail, _ = marks[c]
        same = docs == drow_ref[pl.ds(c, 1), :]
        q_c, k_c, kb_c = cut(qn, c).astype(bf16), cut(kn, c).astype(bf16), cut(kb, c).astype(bf16)
        do = do_ref[at, :]
        wu = wu_ref[0, at, :]
        state = state_ref[0, at, :]
        deltas = (wu[:, HD:].astype(f32) - carry * dot_nn(wu[:, :HD], state)).astype(bf16)
        part = jnp.where(same & (col <= row), dot_nt(q_c, k_c), 0.0)
        dd = dot_tn(part, do) + tail * dot_nn(k_c, leaving[c])
        dpart = jnp.where(same & (col <= row), dot_nt(do, deltas), 0.0)
        through = dot_nt(jnp.concatenate([do, dd.astype(bf16)], axis=0), state)
        dkf = dot_nt(deltas, leaving[c])
        dwu = dot_tn(tinv_ref[0, at, :], jnp.concatenate([-(carry * through[CHUNK:]), dd], axis=1))
        dlow = jnp.where(same & (col < row), -dot_nt(dwu, wu), 0.0)
        pair = jnp.concatenate([dpart.astype(bf16), dlow.astype(bf16)], axis=0)
        onto = dot_nn(pair, k_c)
        dqs.append(carry * through[:CHUNK] + onto[:CHUNK])
        dkb = dwu[:, :HD] + onto[CHUNK:]
        dvb = dwu[:, HD:]
        b_c = cut(beta, c)
        dks.append(dot_tn(pair, jnp.concatenate([q_c, kb_c], axis=0)) + tail * dkf + b_c * dkb)
        dvs.append(b_c * dvb)
        dbs.append(jnp.sum(dkb * cut(kn, c) + dvb * cut(values, c), axis=1, keepdims=True))

    join = lambda parts: jnp.concatenate(parts, axis=0)
    dqn = join(dqs) * HD**-0.5
    unit = query * scale_q
    dquery = scale_q * (dqn - unit * jnp.sum(dqn * unit, axis=-1, keepdims=True))
    dkn = join(dks)
    dkeys = scale_k * (dkn - kn * jnp.sum(dkn * kn, axis=-1, keepdims=True))
    dlogit = join(dbs) * beta * (1.0 - beta)
    lane = lax.broadcasted_iota(jnp.int32, (rows, H), 1)

    @pl.when(head == 0)
    def _():
        dl_ref[...] = jnp.zeros_like(dl_ref)

    dl_ref[...] = jnp.where(lane == head, dlogit, dl_ref[...].astype(f32)).astype(bf16)

    def conv_back(dfilt, slope, x_ref, halo_ref, taps_ref, out_ref, rim_ref, dtap_ref):
        ds_ = low(dfilt) * slope
        ext[pl.ds(0, HALO), :] = halo_ref[...].astype(f32)
        ext[pl.ds(HALO, rows), :] = x_ref[...].astype(f32)
        grad[...] = jnp.zeros_like(grad)
        dtap_ref[pl.ds(KW - 1, 1), :] = jnp.sum(ds_ * ext[pl.ds(HALO, rows), :], axis=0, keepdims=True)
        grad[pl.ds(HALO, rows), :] = ds_ * taps_ref[pl.ds(KW - 1, 1), :]
        for i in range(KW - 1):
            masked = ds_ * masks[i]
            place_i = pl.ds(HALO - KW + 1 + i, rows)
            dtap_ref[pl.ds(i, 1), :] = jnp.sum(masked * ext[place_i, :], axis=0, keepdims=True)
            grad[place_i, :] = grad[place_i, :] + masked * taps_ref[pl.ds(i, 1), :]
        rim_ref[...] = grad[pl.ds(0, HALO), :].astype(bf16)
        out_ref[...] = grad[pl.ds(HALO, rows), :].astype(out_ref.dtype)

    conv_back(dquery, slope_q, q_ref, hq_ref, tq_ref, dq_ref, rq_ref, cq_ref)
    conv_back(dkeys, slope_k, k_ref, hk_ref, tk_ref, dk_ref, rk_ref, ck_ref)
    conv_back(join(dvs), slope_v, v_ref, hv_ref, tv_ref, dv_ref, rv_ref, cv_ref)


def bwd_main(moves, gives, projected, halo, taps, logits, dcol, drow, tinv, wu, step, state, r, do):
    rows = projected.shape[0]
    chunks = rows // CHUNK
    sds = jax.ShapeDtypeStruct
    return pl.pallas_call(
        partial(bwd_main_kernel, len(moves)),
        grid=(H,),
        in_specs=[head_spec((HD, HD)) for _ in (*moves, *gives)]
        + [col_spec(rows, 0), col_spec(rows, H), col_spec(rows, 2 * H)]
        + [col_spec(HALO, 0), col_spec(HALO, H), col_spec(HALO, 2 * H)]
        + [col_spec(KW, 0), col_spec(KW, H), col_spec(KW, 2 * H)]
        + [full_spec((rows, H)), full_spec((rows + HALO, 1)), full_spec((chunks, CHUNK))]
        + [head_spec((rows, CHUNK)), head_spec((rows, 2 * HD)), head_spec((rows, HD)), head_spec((rows, HD))]
        + [col_spec(rows, 0), col_spec(rows, 0)],
        out_specs=[col_spec(rows, 0)] * 3 + [col_spec(HALO, 0)] * 3 + [col_spec(KW, 0)] * 3 + [full_spec((rows, H))],
        out_shape=[sds((rows, D), f32)] * 3 + [sds((HALO, D), bf16)] * 3 + [sds((KW, D), f32)] * 3 + [sds((rows, H), bf16)],
        scratch_shapes=[pltpu.VMEM((rows + HALO, HD), f32), pltpu.VMEM((rows + HALO, HD), f32)],
        compiler_params=params(),
        cost_estimate=cost(90, rows, rows * D * 40),
        name="delta_back",
    )(*moves, *gives, *([projected] * 3 + [halo] * 3 + [taps] * 3), logits, dcol, drow, tinv, wu, step, state, r, do)


epsilon_norm = EPS_NORM
LAYERS = 2


def shifted(block, axis, distance):
    devices = range(lax.axis_size(axis))
    route = [(i - distance, i) for i in devices if i - distance in devices]
    return lax.ppermute(block, axis, route)


def root_norm(values, gain):
    return (
        values * lax.rsqrt(jnp.mean(values * values, axis=-1, keepdims=True) + epsilon_norm) * gain
    )


def swiglu_act(gate_up):
    half_width = gate_up.shape[1] // 2
    return jax.nn.silu(gate_up[:, :half_width]) * gate_up[:, half_width:]


def contract_last(left, right):
    return lax.dot_general(
        left, right, (((1,), (1,)), ((), ())), preferred_element_type=jnp.float32
    )


def contract_first(left, right):
    return lax.dot_general(
        left, right, (((0,), (0,)), ((), ())), preferred_element_type=jnp.float32
    )


def fetch_rows(weights):
    return lax.all_gather(weights, "fsdp", axis=0, tiled=True)


def reduce_rows(left, right):
    return lax.psum_scatter(
        contract_first(left, right).astype(jnp.bfloat16), "fsdp", scatter_dimension=0, tiled=True
    )


def on_device(
    tokens,
    segments,
    valid_mask,
    norm_gains,
    head_gain,
    conv_weight,
    beta_weight,
    qkv_weight,
    out_weight,
    gate_up_weight,
    down_weight,
    cotangent,
):
    rows = tokens.shape[1]
    pieces = lax.axis_size("seq")
    doc_ids = segments[0]
    doc_pad = jnp.concatenate([jnp.full((HALO,), -1, jnp.int32), doc_ids])
    piece_start = lax.axis_index("seq") * rows
    dcol = lax.dynamic_slice_in_dim(doc_pad, piece_start, rows + HALO)
    drow = dcol[HALO:].reshape(rows // CHUNK, CHUNK)
    dcol = dcol[:, None]
    valid_rows = valid_mask[0].astype(jnp.float32)
    stream = tokens[0].astype(jnp.float32)
    square_sums = []
    stored = []
    for at in range(LAYERS):
        qkv_full = fetch_rows(qkv_weight[at])
        out_full = fetch_rows(out_weight[at])
        gate_up_full = fetch_rows(gate_up_weight[at])
        down_full = fetch_rows(down_weight[at])
        square_sums.append(jnp.sum(jnp.sum(stream * stream, axis=1) * valid_rows))
        normed_one, pull_one = jax.vjp(root_norm, stream, norm_gains[at, 0])
        normed_one = normed_one.astype(jnp.bfloat16)
        projected = jnp.dot(normed_one, qkv_full, preferred_element_type=jnp.float32).astype(bf16)
        logits = jnp.dot(normed_one, beta_weight[at], preferred_element_type=jnp.float32).astype(bf16)
        halo = shifted(projected[rows - HALO :], "seq", 1)
        qn, kn, tinv, wu, step, pre, total = fwd_local(
            projected, halo, conv_weight[at], logits, dcol, drow
        )
        nears = [shifted(total, "seq", d) for d in range(1, pieces - 1)]
        far = shifted(total[:, :, HD:], "seq", pieces - 1)
        moves = [shifted(total[:, :, :HD], "seq", -d) for d in range(1, pieces - 1)]
        reads, local_out = fwd_read(qn, kn, wu, dcol, drow)
        state, mixed, attended = fwd_state(nears, far, pre, reads, local_out, head_gain[at][None])
        branch = jnp.dot(attended, out_full, preferred_element_type=jnp.float32)
        square_sums.append(jnp.sum(jnp.sum(branch * branch, axis=1) * valid_rows))
        stream = stream + branch
        normed_two, pull_two = jax.vjp(root_norm, stream, norm_gains[at, 1])
        normed_two = normed_two.astype(jnp.bfloat16)
        gate_up = jnp.dot(normed_two, gate_up_full, preferred_element_type=jnp.float32)
        activated, pull_act = jax.vjp(swiglu_act, gate_up)
        activated = activated.astype(jnp.bfloat16)
        branch = jnp.dot(activated, down_full, preferred_element_type=jnp.float32)
        square_sums.append(jnp.sum(jnp.sum(branch * branch, axis=1) * valid_rows))
        stream = stream + branch
        stored.append(
            (
                qkv_full, out_full, gate_up_full, down_full, pull_one, normed_one, attended, pull_two, normed_two,
                pull_act, activated, moves, mixed,
                (projected, halo, conv_weight[at], logits, dcol, drow, tinv, wu, step, state, reads),
            )
        )
    stream_grad = cotangent[0].astype(jnp.float32) * valid_rows[:, None]
    gain_list = []
    head_list = []
    filter_list = []
    beta_list = []
    weight_list = []
    for at in reversed(range(LAYERS)):
        (
            qkv_full, out_full, gate_up_full, down_full, pull_one, normed_one, attended, pull_two, normed_two,
            pull_act, activated, moves, mixed, kept,
        ) = stored[at]
        step, reads = kept[8], kept[10]
        branch_low = stream_grad.astype(jnp.bfloat16)
        grad_down = reduce_rows(activated, branch_low)
        (grad_gate_up,) = pull_act(contract_last(branch_low, down_full))
        grad_gate_up = grad_gate_up.astype(jnp.bfloat16)
        grad_gate = reduce_rows(normed_two, grad_gate_up)
        grad_state, gain_two = pull_two(contract_last(grad_gate_up, gate_up_full))
        stream_grad = stream_grad + grad_state
        branch_low = stream_grad.astype(jnp.bfloat16)
        grad_out = reduce_rows(attended, branch_low)
        grad_heads = contract_last(branch_low, out_full).astype(jnp.bfloat16)
        grad_mixed, gain_head, total = bwd_local(
            grad_heads, mixed, reads, head_gain[at][None], step, dcol
        )
        gives = [shifted(total, "seq", -d) for d in range(1, pieces)]
        *parts, grad_logits = bwd_main(moves, gives, *kept, grad_mixed)
        rim = shifted(jnp.concatenate(parts[3:6], axis=1), "seq", -1).astype(f32)
        grad_filter = jnp.concatenate(parts[6:9], axis=1)
        grad_proj = jnp.concatenate(parts[:3], axis=1)
        grad_proj = jnp.concatenate(
            [grad_proj[: rows - HALO], grad_proj[rows - HALO :] + rim], axis=0
        ).astype(bf16)
        grad_qkv = reduce_rows(normed_one, grad_proj)
        grad_beta = contract_first(normed_one, grad_logits)
        grad_normed = contract_last(grad_proj, qkv_full) + contract_last(grad_logits, beta_weight[at])
        grad_state, gain_one = pull_one(grad_normed)
        stream_grad = stream_grad + grad_state
        weight_list.append(
            [lax.psum(grad, "seq").astype(f32) for grad in (grad_qkv, grad_out, grad_gate, grad_down)]
        )
        gain_list.append(jnp.stack([gain_one, gain_two]))
        head_list.append(gain_head[0])
        filter_list.append(grad_filter)
        beta_list.append(grad_beta)
    stats_sum, valid_count, gains_sum, head_sum, filter_sum, beta_sum = lax.psum(
        (
            jnp.stack(square_sums),
            jnp.sum(valid_rows),
            jnp.stack(gain_list[::-1]),
            jnp.stack(head_list[::-1]),
            jnp.stack(filter_list[::-1]),
            jnp.stack(beta_list[::-1]),
        ),
        ("seq", "fsdp"),
    )
    rms_stats = jnp.sqrt(stats_sum / (jnp.maximum(valid_count, 1.0) * D)).reshape(LAYERS, 3)
    return (
        stream.astype(jnp.bfloat16)[None],
        stream_grad[None],
        gains_sum,
        head_sum,
        filter_sum,
        beta_sum,
        *[jnp.stack(pair[::-1]) for pair in zip(*weight_list)],
        rms_stats,
    )


def solution(mesh):
    return jax.shard_map(
        on_device,
        mesh=mesh,
        in_specs=(
            P("fsdp", "seq", None),
            P("fsdp", None),
            P("fsdp", "seq"),
            P(),
            P(),
            P(),
            P(),
            P(None, "fsdp", None),
            P(None, "fsdp", None),
            P(None, "fsdp", None),
            P(None, "fsdp", None),
            P("fsdp", "seq", None),
        ),
        out_specs=(
            P("fsdp", "seq", None),
            P("fsdp", "seq", None),
            P(),
            P(),
            P(),
            P(),
            P(None, "fsdp", None),
            P(None, "fsdp", None),
            P(None, "fsdp", None),
            P(None, "fsdp", None),
            P(),
        ),
        check_vma=False,
    )
```

time: 4600 us -> 1560 us (0.34)
  other arithmetic: 1850 us -> 28.8 us
  matrix products: 1060 us -> 211 us
  local copies, waits for them, and re-layouts: 824 us -> 50.3 us
  waiting for transfers between devices: 645 us -> 955 us
  Pallas kernels: 0 us -> 207 us
  blocking collectives: 92.9 us -> 38.1 us
    another operation x264 -> x6, other arithmetic: 1310 us -> 9.09 us  [the longest x4 9.06 us: on_device(): jnp.stack(pair[::-1])]
    dot_general x1410 -> x2, matrix products: 754 us -> 0.9 us  [on_device(): jnp.dot(normed_one, beta_weight[at], preferred_element_type=jnp.float32)]
    squeeze x384 -> x1, local copies, waits for them, and re-layouts: 290 us -> 0.01 us  [on_device(): conv_weight[at]]
    all_gather x8, waiting for transfers between devices: 52.1 us -> 308 us  [fetch_rows(): return lax.all_gather(weights, 'fsdp', axis=0, tiled=True)]
    convert_element_type x399 -> x0, other arithmetic: 247 us -> none  [the longest x128 121 us: advance(): tail_doc = (doc_b == doc_b[block_size - 1]).astype(jnp.float32)]
    pallas_call x0 -> x10, Pallas kernels: none -> 207 us  [the longest x2 92.5 us: bwd_main(): pl.pallas_call(partial(bwd_main_kernel, len(moves)), grid=(H,), in_specs=...]
    dynamic_slice x129 -> x1, local copies, waits for them, and re-layouts: 160 us -> 0.08 us  [on_device(): dcol = lax.dynamic_slice_in_dim(doc_pad, piece_start, rows + HALO)]
    slice x271 -> x12, local copies, waits for them, and re-layouts: 160 us -> 9.16 us  [the longest x1 2.76 us: on_device(): qkv_full = fetch_rows(qkv_weight[at])]
where the time goes in v1:
time: 1560 us; the launch traced here: 1550 us
  waiting for transfers between devices  955 us (61%)
  matrix products  211 us (14%)
  Pallas kernels  207 us (13%)
  local copies, waits for them, and re-layouts  50.3 us (3%)
  starting transfers between devices  42.4 us (3%)
  blocking collectives  38.1 us (2%)
  other arithmetic  28.8 us (2%)
  between operations  16.5 us (1%)
    reduce_scatter x8, waiting for transfers between devices, reduce_rows(): lax.psum_scatter(contract_first(left, right).astype(jnp.bfloat16), 'fsdp'...  396 us
    all_gather x8, waiting for transfers between devices, fetch_rows(): return lax.all_gather(weights, 'fsdp', axis=0, tiled=True)  308 us
    psum x1, waiting for transfers between devices, on_device(): lax.psum((jnp.stack(square_sums), jnp.sum(valid_rows), jnp.stack(gain_lis...  119 us
    pallas_call x2, Pallas kernels, bwd_main(): pl.pallas_call(partial(bwd_main_kernel, len(moves)), grid=(H,), in_specs=...  92.5 us
    psum x1, waiting for transfers between devices, on_device(): lax.psum(grad, 'seq').astype(f32)  85.1 us
    dot_general x10, matrix products, contract_last(): lax.dot_general(left, right, (((1,), (1,)), ((), ())), preferred_element_...  81.9 us
    pallas_call x2, Pallas kernels, fwd_local(): pl.pallas_call(fwd_local_kernel, grid=(H,), in_specs=[col_spec(rows, 0),...  63.5 us
    dot_general x10, matrix products, contract_first(): lax.dot_general(left, right, (((0,), (0,)), ((), ())), preferred_element_...  62.9 us
  transfers between devices with their start and end apart: 38, of which 23 were waited for; matrix products, arithmetic and copies ran while one was open for 16% of the time, Pallas kernels for 13%

profile of v1, /device:TPU:0, one launch (start us, length us, event | category | flops | bytes accessed | tf_op | source)
XLA Modules:
  0.0 1548.8 jit_solution(8247296047002450061)
XLA Ops:
  19.6 58.1 %all-gather.17.cloned.1.call-done = bf16[1,1024,3072]{2,1,0:T(8,128)(2,1)} async-done(((bf16[1,128,3072]{2,1,0:T(8,128)(2,1)}), bf16[1,1024,3072]{2,1,0:T(8,128)(2,1)}) %all-gather.17.cloned.1.call-update) | async-done | bytes 6291472 | tf_op jit(solution)/shard_map/all_gather | solution.py:482
  89.5 31.7 %delta_local.2 = (bf16[512,1024]{1,0:T(8,128)(2,1)S(1)}, bf16[512,1024]{1,0:T(8,128)(2,1)S(1)}, bf16[8,512,128]{2,1,0:T(8,128)(2,1)S(1)}, bf16[8,512,256]{2,1,0:...) custom-call(bf16[512,3072]{1,0:T(8,128)(2,1)} %copy-done.84, ...), custom_call_target="tpu_custom_call" | custom-call | flops 8053063680 | bytes 12582912 | tf_op jit(solution)/shard_map/delta_local/pallas_call | solution.py:177
  164.2 52.2 %all-gather.21.cloned.1.call-done = bf16[1,1024,5632]{2,1,0:T(8,128)(2,1)} async-done(((bf16[1,128,5632]{2,1,0:T(8,128)(2,1)}), bf16[1,1024,5632]{2,1,0:T(8,128)(2,1)}) %all-gather.21.cloned.1.call-update) | async-done | bytes 11534352 | tf_op jit(solution)/shard_map/all_gather | solution.py:482
  233.2 43.4 %all-gather.23.cloned.1.call-done = bf16[1,2816,1024]{2,1,0:T(8,128)(2,1)} async-done(((bf16[1,352,1024]{2,1,0:T(8,128)(2,1)}), bf16[1,2816,1024]{2,1,0:T(8,128)(2,1)}) %all-gather.23.cloned.1.call-update) | async-done | bytes 5767184 | tf_op jit(solution)/shard_map/all_gather | solution.py:482
  288.0 54.1 %all-gather.25.cloned.1.call-done = bf16[1,1024,3072]{2,1,0:T(8,128)(2,1)} async-done(((bf16[1,128,3072]{2,1,0:T(8,128)(2,1)}), bf16[1,1024,3072]{2,1,0:T(8,128)(2,1)}) %all-gather.25.cloned.1.call-update) | async-done | bytes 6291472 | tf_op jit(solution)/shard_map/all_gather | solution.py:482
  353.7 31.7 %delta_local.3 = (bf16[512,1024]{1,0:T(8,128)(2,1)S(1)}, bf16[512,1024]{1,0:T(8,128)(2,1)S(1)}, bf16[8,512,128]{2,1,0:T(8,128)(2,1)S(1)}, bf16[8,512,256]{2,1,0:...) custom-call(bf16[512,3072]{1,0:T(8,128)(2,1)} %copy-done.85, ...), custom_call_target="tpu_custom_call" | custom-call | flops 8053063680 | bytes 12582912 | tf_op jit(solution)/shard_map/delta_local/pallas_call | solution.py:177
  428.8 51.8 %all-gather.29.cloned.1.call-done = bf16[1,1024,5632]{2,1,0:T(8,128)(2,1)} async-done(((bf16[1,128,5632]{2,1,0:T(8,128)(2,1)}), bf16[1,1024,5632]{2,1,0:T(8,128)(2,1)}) %all-gather.29.cloned.1.call-update) | async-done | bytes 11534352 | tf_op jit(solution)/shard_map/all_gather | solution.py:482
  480.7 12.3 fusion.2
  493.0 48.1 %all-gather.31.cloned.1.call-done = bf16[1,2816,1024]{2,1,0:T(8,128)(2,1)} async-done(((bf16[1,352,1024]{2,1,0:T(8,128)(2,1)}), bf16[1,2816,1024]{2,1,0:T(8,128)(2,1)}) %all-gather.31.cloned.1.call-update) | async-done | bytes 5767184 | tf_op jit(solution)/shard_map/all_gather | solution.py:482
  541.0 13.0 fusion.81
  554.0 14.6 multiply_reduce_fusion.4
  613.9 46.3 %delta_back.2 = (f32[512,1024]{1,0:T(8,128)}, f32[512,1024]{1,0:T(8,128)}, f32[512,1024]{1,0:T(8,128)}, bf16[8,1024]{1,0:T(8,128)(2,1)S(1)}, bf16[8,1024]{1,0:T(...) custom-call(bf16[8,128,128]{2,1,0:T(8,128)(2,1)} %collective-permute, ...), custom_call_target="tpu_custom_call" | custom-call | flops 12079595520 | bytes 20971520 | tf_op jit(solution)/shard_map/delta_back/pallas_call | solution.py:429
  693.3 14.5 multiply_reduce_fusion.6
  777.6 46.3 %delta_back.3 = (f32[512,1024]{1,0:T(8,128)}, f32[512,1024]{1,0:T(8,128)}, f32[512,1024]{1,0:T(8,128)}, bf16[8,1024]{1,0:T(8,128)(2,1)S(1)}, bf16[8,1024]{1,0:T(...) custom-call(bf16[8,128,128]{2,1,0:T(8,128)(2,1)S(1)} %collective-per, ...), custom_call_target="tpu_custom_call" | custom-call | flops 12079595520 | bytes 20971520 | tf_op jit(solution)/shard_map/delta_back/pallas_call | solution.py:429
  838.9 13.5 convolution_convert_fusion
  854.0 13.5 convolution_convert_fusion.1
  867.7 14.9 reduce-scatter.21.cloned.1.call-done
  882.6 70.5 %reduce-scatter.11.cloned.1.call-done = bf16[128,3072]{1,0:T(8,128)(2,1)} async-done(((bf16[1024,3072]{1,0:T(8,128)(2,1)}), bf16[128,3072]{1,0:T(8,128)(2,1)}) %reduce-scatter.11.cloned.1.call-update) | async-done | bytes 786448 | tf_op jit(solution)/shard_map/reduce_scatter | solution.py:486
  953.1 70.4 %reduce-scatter.9.cloned.1.call-done = bf16[128,3072]{1,0:T(8,128)(2,1)} async-done(((bf16[1024,3072]{1,0:T(8,128)(2,1)}), bf16[128,3072]{1,0:T(8,128)(2,1)}) %reduce-scatter.9.cloned.1.call-update) | async-done | bytes 786448 | tf_op jit(solution)/shard_map/reduce_scatter | solution.py:486
  1023.5 119.9 %reduce-scatter.19.cloned.1.call-done = bf16[128,5632]{1,0:T(8,128)(2,1)} async-done(((bf16[1024,5632]{1,0:T(8,128)(2,1)}), bf16[128,5632]{1,0:T(8,128)(2,1)}) %reduce-scatter.19.cloned.1.call-update) | async-done | bytes 1441808 | tf_op jit(solution)/shard_map/reduce_scatter | solution.py:486
  1143.4 119.9 %reduce-scatter.17.cloned.1.call-done = bf16[128,5632]{1,0:T(8,128)(2,1)} async-done(((bf16[1024,5632]{1,0:T(8,128)(2,1)}), bf16[128,5632]{1,0:T(8,128)(2,1)}) %reduce-scatter.17.cloned.1.call-update) | async-done | bytes 1441808 | tf_op jit(solution)/shard_map/reduce_scatter | solution.py:486
  1282.3 38.1 %all-reduce.5 = (f32[2,2,1024]{2,1,0:T(2,128)}, f32[2,128]{1,0:T(2,128)}, f32[6]{0:T(128)S(1)}, f32[]{:T(128)}) all-reduce(f32[2,2,1024]{2,1,0:T(2,128)S(1)} %pad_maximum_fusion.14, f32[2,128]{1,0:T(2,128)S(1)} %pad_maximum_fusion.15, f32[6]{0:T(128)S(1)} %stack.151, ...), channel_id=1, replica_groups=mesh['seq'=4,'fsdp'=8] {'seq','fsdp'}, use_global_device_ids=true, to_apply=%region_12.13 | all-reduce | flops 4359 | bytes 34872 | tf_op jit(solution)/shard_map/psum | solution.py:599
  1325.2 85.1 %all-reduce.13.cloned.1.call-done = (bf16[1,128,3072]{2,1,0:T(8,128)(2,1)}, bf16[1,128,3072]{2,1,0:T(8,128)(2,1)}, bf16[1,128,1024]{2,1,0:T(8,128)(2,1)}, bf16[1...) async-done(((bf16[1,128,3072]{2,1,0:T(8,128)(2,1)}, ...) | async-done | bytes 6422544 | tf_op jit(solution)/shard_map/psum | solution.py:593
  1419.3 119.3 %all-reduce.11.cloned.1.call-done = (f32[2,4,3072]{2,1,0:T(4,128)}, f32[2,1024,8]{1,2,0:T(8,128)}) async-done(((f32[2,4,3072]{2,1,0:T(4,128)}, f32[2,1024,8]{1,2,0:T(8,128)}), (f32[2,4,3072]{2,1,0:T(4,128)}, f32[2,1024,8]{1,2,0:T(8,128)})) %all-reduce.11.cloned.1.call-update) | async-done | bytes 163856 | tf_op jit(solution)/shard_map/psum | solution.py:599
  (352 shorter events, 349.2 us)
Async XLA Ops:
  7.2 70.5 %all-gather.17.cloned.1.call-start = ((), (), s32[]{:S(2)}) async-start(), calls=%async_computation.16 | async-start | bytes 7077888 | tf_op jit(solution)/shard_map/all_gather | solution.py:482
  10.0 148.9 %all-gather.19.cloned.1.call-start = ((), (), s32[]{:S(2)}) async-start(), calls=%async_computation.17 | async-start | bytes 2359296 | tf_op jit(solution)/shard_map/all_gather | solution.py:482
  11.0 205.4 %all-gather.21.cloned.1.call-start = ((), (), s32[]{:S(2)}) async-start(), calls=%async_computation.18 | async-start | bytes 12976128 | tf_op jit(solution)/shard_map/all_gather | solution.py:482
  12.8 263.9 %all-gather.23.cloned.1.call-start = ((), (), s32[]{:S(2)}) async-start(), calls=%async_computation.19 | async-start | bytes 6488064 | tf_op jit(solution)/shard_map/all_gather | solution.py:482
  15.4 326.7 %all-gather.25.cloned.1.call-start = ((), (), s32[]{:S(2)}) async-start(), calls=%async_computation.20 | async-start | bytes 7077888 | tf_op jit(solution)/shard_map/all_gather | solution.py:482
  16.0 407.1 %all-gather.27.cloned.1.call-start = ((), (), s32[]{:S(2)}) async-start(), calls=%async_computation.21 | async-start | bytes 2359296 | tf_op jit(solution)/shard_map/all_gather | solution.py:482
  16.6 464.1 %all-gather.29.cloned.1.call-start = ((), (), s32[]{:S(2)}) async-start(), calls=%async_computation.22 | async-start | bytes 12976128 | tf_op jit(solution)/shard_map/all_gather | solution.py:482
  17.3 523.7 %all-gather.31.cloned.1.call-start = ((), (), s32[]{:S(2)}) async-start(), calls=%async_computation.23 | async-start | bytes 6488064 | tf_op jit(solution)/shard_map/all_gather | solution.py:482
  18.1 849.5 %reduce-scatter.15.cloned.1.call-start = ((), (), s32[]{:S(2)}) async-start(), calls=%async_computation.11 | async-start | bytes 2359296 | tf_op jit(solution)/shard_map/reduce_scatter | solution.py:486
  121.2 20.7 %collective-permute-start.1 = (bf16[8,128,256]{2,1,0:T(8,128)(2,1)S(1)}, bf16[8,128,256]{2,1,0:T(8,128)(2,1)S(1)}, u32[]{:S(2)}, u32[]{:S(2)}) collective-permute-start(bf16[8,128,256]{2,1,0:T(8,128)(2,1)S(1)} %get-tuple-element.61), channel_id=1, source_target_pairs={{0,8},{8,16},{16,24},{1,9},{9,17},{17,25},{2,10},{10,18},{18,26},{... | collective-permute-start | bytes 1572872 | tf_op jit(solution)/shard_map/ppermute | solution.py:455
  125.5 23.8 %collective-permute-start.2 = (bf16[8,128,256]{2,1,0:T(8,128)(2,1)S(1)}, bf16[8,128,256]{2,1,0:T(8,128)(2,1)S(1)}, u32[]{:S(2)}, u32[]{:S(2)}) collective-permute-start(bf16[8,128,256]{2,1,0:T(8,128)(2,1)S(1)} %get-tuple-element.61), channel_id=1, source_target_pairs={{0,16},{8,24},{1,17},{9,25},{2,18},{10,26},{3,19},{11,27},{4,20},{... | collective-permute-start | bytes 1572872 | tf_op jit(solution)/shard_map/ppermute | solution.py:455
  385.4 22.1 %collective-permute-start.5 = (bf16[8,128,256]{2,1,0:T(8,128)(2,1)S(1)}, bf16[8,128,256]{2,1,0:T(8,128)(2,1)S(1)}, u32[]{:S(2)}, u32[]{:S(2)}) collective-permute-start(bf16[8,128,256]{2,1,0:T(8,128)(2,1)S(1)} %get-tuple-element.69), channel_id=1, source_target_pairs={{0,8},{8,16},{16,24},{1,9},{9,17},{17,25},{2,10},{10,18},{18,26},{... | collective-permute-start | bytes 1572872 | tf_op jit(solution)/shard_map/ppermute | solution.py:455
  389.7 23.8 %collective-permute-start.6 = (bf16[8,128,256]{2,1,0:T(8,128)(2,1)S(1)}, bf16[8,128,256]{2,1,0:T(8,128)(2,1)S(1)}, u32[]{:S(2)}, u32[]{:S(2)}) collective-permute-start(bf16[8,128,256]{2,1,0:T(8,128)(2,1)S(1)} %get-tuple-element.69), channel_id=1, source_target_pairs={{0,16},{8,24},{1,17},{9,25},{2,18},{10,26},{3,19},{11,27},{4,20},{... | collective-permute-start | bytes 1572872 | tf_op jit(solution)/shard_map/ppermute | solution.py:455
  395.2 202.9 %collective-permute-start.8 = (bf16[8,128,128]{2,1,0:T(8,128)(2,1)}, bf16[8,128,128]{2,1,0:T(8,128)(2,1)}, u32[]{:S(2)}, u32[]{:S(2)}) collective-permute-start(bf16[8,128,128]{2,1,0:T(8,128)(2,1)} %get-tuple-element.164), channel_id=1, source_target_pairs={{8,0},{16,8},{24,16},{9,1},{17,9},{25,17},{10,2},{18,10},{26,18},{... | collective-permute-start | bytes 786440 | tf_op jit(solution)/shard_map/ppermute | solution.py:455
  396.5 201.6 %collective-permute-start.9 = (bf16[8,128,128]{2,1,0:T(8,128)(2,1)}, bf16[8,128,128]{2,1,0:T(8,128)(2,1)}, u32[]{:S(2)}, u32[]{:S(2)}) collective-permute-start(bf16[8,128,128]{2,1,0:T(8,128)(2,1)} %get-tuple-element.164), channel_id=1, source_target_pairs={{16,0},{24,8},{17,1},{25,9},{18,2},{26,10},{19,3},{27,11},{20,4},{... | collective-permute-start | bytes 786440 | tf_op jit(solution)/shard_map/ppermute | solution.py:455
  598.0 269.6 %reduce-scatter.13.cloned.1.call-start = ((), (), s32[]{:S(2)}) async-start(), calls=%async_computation.10 | async-start | bytes 2359296 | tf_op jit(solution)/shard_map/reduce_scatter | solution.py:486
  716.9 150.8 %reduce-scatter.23.cloned.1.call-start = ((), (), s32[]{:S(2)}) async-start(), calls=%async_computation.15 | async-start | bytes 6488064 | tf_op jit(solution)/shard_map/reduce_scatter | solution.py:486
  725.1 157.5 %reduce-scatter.21.cloned.1.call-start = ((), (), s32[]{:S(2)}) async-start(), calls=%async_computation.14 | async-start | bytes 6488064 | tf_op jit(solution)/shard_map/reduce_scatter | solution.py:486
  733.5 219.7 %reduce-scatter.11.cloned.1.call-start = ((), (), s32[]{:S(2)}) async-start(), calls=%async_computation.9 | async-start | bytes 7077888 | tf_op jit(solution)/shard_map/reduce_scatter | solution.py:486
  742.1 281.4 %reduce-scatter.9.cloned.1.call-start = ((), (), s32[]{:S(2)}) async-start(), calls=%async_computation.8 | async-start | bytes 7077888 | tf_op jit(solution)/shard_map/reduce_scatter | solution.py:486
  837.3 306.1 %reduce-scatter.19.cloned.1.call-start = ((), (), s32[]{:S(2)}) async-start(), calls=%async_computation.13 | async-start | bytes 12976128 | tf_op jit(solution)/shard_map/reduce_scatter | solution.py:486
  852.4 410.8 %reduce-scatter.17.cloned.1.call-start = ((), (), s32[]{:S(2)}) async-start(), calls=%async_computation.12 | async-start | bytes 12976128 | tf_op jit(solution)/shard_map/reduce_scatter | solution.py:486
  867.6 542.7 %all-reduce.13.cloned.1.call-start = ((), (), s32[]{:S(2)}) async-start(), calls=%async_computation.25 | async-start | bytes 12845056 | tf_op jit(solution)/shard_map/psum | solution.py:593
  1263.3 275.4 %all-reduce.11.cloned.1.call-start = ((), (), s32[]{:S(2)}) async-start(), calls=%async_computation.24 | async-start | bytes 327680 | tf_op jit(solution)/shard_map/psum | solution.py:599
  (105 other events, 1497.6 us)
Sparse Core Ops, SparseCore 0:
  10.2 67.4 all-gather.16
  79.3 27.7 all-gather.18
  108.8 107.5 all-gather.20
  217.9 58.7 all-gather.22
  278.7 63.4 all-gather.24
  343.6 27.7 all-gather.26
  373.0 107.5 all-gather.28
  482.3 58.6 all-gather.30
  598.2 36.8 reduce-scatter.14
  717.0 34.4 reduce-scatter.12
  753.7 63.3 reduce-scatter.22
  819.3 63.2 reduce-scatter.20
  884.9 68.1 reduce-scatter.10
  955.3 68.1 reduce-scatter.8
  1025.7 117.6 reduce-scatter.18
  1145.5 117.6 reduce-scatter.16
  1267.7 142.4 all-reduce.12
  1416.2 122.3 all-reduce.10

commit v2 on v1

v2 whole, which is shorter than its diff:
```python
from functools import partial
import jax
import jax.numpy as jnp
from jax import lax
from jax.experimental import pallas as pl
from jax.experimental.pallas import tpu as pltpu
from jax.sharding import PartitionSpec as P

D = 1024
H = 8
HD = 128
KW = 4
LAYERS = 2
CHUNK = 128
TOGETHER = 4
TOGETHER_BACK = 2
HALO = 16
f32 = jnp.float32
bf16 = jnp.bfloat16
EPS_NORM = 1e-05
EPS_UNIT = 1e-06
VMEM_LIMIT = 60 * 1024 * 1024


def dot_nn(a, b):
    return lax.dot_general(a.astype(bf16), b.astype(bf16), (((1,), (0,)), ((), ())), preferred_element_type=f32)


def dot_nt(a, b):
    return lax.dot_general(a.astype(bf16), b.astype(bf16), (((1,), (1,)), ((), ())), preferred_element_type=f32)


def dot_tn(a, b):
    return lax.dot_general(a.astype(bf16), b.astype(bf16), (((0,), (0,)), ((), ())), preferred_element_type=f32)


def sigmoid(x):
    return 1.0 / (1.0 + jnp.exp(-x))


def conv_masks(dcol_ref, rows):
    here = dcol_ref[pl.ds(HALO, rows), :]
    return [
        jnp.broadcast_to((dcol_ref[pl.ds(HALO - KW + 1 + i, rows), :] == here).astype(f32), (rows, HD))
        for i in range(KW - 1)
    ]


def conv_sum(x_ref, taps_ref, masks, ext, h):
    rows = x_ref.shape[0] - HALO
    lanes = pl.ds(h * HD, HD)
    ext[...] = x_ref[:, lanes].astype(f32)
    total = taps_ref[pl.ds(KW - 1, 1), lanes] * ext[pl.ds(HALO, rows), :]
    for i in range(KW - 1):
        total = total + taps_ref[pl.ds(i, 1), lanes] * ext[pl.ds(HALO - KW + 1 + i, rows), :] * masks[i]
    return total


def low(x):
    return x.astype(bf16).astype(f32)


def unit_scale(x):
    return lax.rsqrt(jnp.sum(x * x, axis=-1, keepdims=True) + EPS_UNIT)


def head_column(table, head):
    lane = lax.broadcasted_iota(jnp.int32, table.shape, 1)
    return jnp.sum(jnp.where(lane == head, table, 0.0), axis=1, keepdims=True)


def chunk_marks(dcol_ref, c):
    at = HALO + c * CHUNK
    docs = dcol_ref[pl.ds(at, CHUNK), :]
    prior = dcol_ref[pl.ds(at - 1, 1), :]
    last = dcol_ref[pl.ds(at + CHUNK - 1, 1), :]
    carry = (docs == prior).astype(f32)
    tail = (docs == last).astype(f32)
    carry_last = (last == prior).astype(f32)
    return docs, carry, tail, carry_last


def tri_index():
    row = lax.broadcasted_iota(jnp.int32, (CHUNK, CHUNK), 0)
    col = lax.broadcasted_iota(jnp.int32, (CHUNK, CHUNK), 1)
    return row, col


def inverses(systems, differ):
    row, col = tri_index()
    eye = (row == col).astype(f32)
    found = [eye - jnp.where(differ == 1, low_part, 0.0) for low_part in systems]
    step = 2
    while step < CHUNK:
        side = (differ >= step) & (differ < 2 * step)
        lows = [x.astype(bf16) for x in found]
        inner = [dot_nn(jnp.where(side, s, 0.0), x) for s, x in zip(systems, lows)]
        outer = [dot_nn(x, y) for x, y in zip(lows, inner)]
        found = [x - y for x, y in zip(found, outer)]
        step *= 2
    return found


def fwd_local_kernel(
    q_ref, k_ref, v_ref, tq_ref, tk_ref, tv_ref, lg_ref, dcol_ref, drow_ref, *refs,
):
    qn_ref, kn_ref, tinv_ref, wu_ref, gain_ref, pre_ref, total_ref, ext = refs[-8:]
    group = pl.program_id(0)
    rows = q_ref.shape[0] - HALO
    chunks = rows // CHUNK
    masks = conv_masks(dcol_ref, rows)
    heads = range(q_ref.shape[1] // HD)

    def filtered(x, taps, h):
        s = conv_sum(x, taps, masks, ext.at[h], h)
        return low(s * sigmoid(s))

    queries = [filtered(q_ref, tq_ref, h) for h in heads]
    keys = [filtered(k_ref, tk_ref, h) for h in heads]
    values = [filtered(v_ref, tv_ref, h) for h in heads]
    kns, kbs, vbs = [], [], []
    for h in heads:
        lanes = pl.ds(h * HD, HD)
        qn_ref[:, lanes] = (queries[h] * (unit_scale(queries[h]) * HD**-0.5)).astype(bf16)
        kn = keys[h] * unit_scale(keys[h])
        kn_ref[:, lanes] = kn.astype(bf16)
        beta = sigmoid(head_column(lg_ref[...].astype(f32), group * len(heads) + h))
        kns.append(kn.astype(bf16))
        kbs.append((beta * kn).astype(bf16))
        vbs.append((beta * values[h]).astype(bf16))
    row, col = tri_index()
    differ = row ^ col
    marks = [chunk_marks(dcol_ref, c) for c in range(chunks)]
    cut = lambda x, c: x[c * CHUNK : (c + 1) * CHUNK]
    items = [(h, c) for h in heads for c in range(chunks)]
    keeps = [(marks[c][0] == drow_ref[pl.ds(c, 1), :]) & (col < row) for c in range(chunks)]
    systems = [dot_nt(cut(kbs[h], c), cut(kns[h], c)) for h, c in items]
    systems = [jnp.where(keeps[c], s, 0.0) for s, (h, c) in zip(systems, items)]
    found = [x.astype(bf16) for x in inverses(systems, differ)]
    both = [
        dot_nn(x, jnp.concatenate([cut(kbs[h], c), cut(vbs[h], c)], axis=1)) for x, (h, c) in zip(found, items)
    ]
    tails = [(cut(kns[h], c).astype(f32) * marks[c][2]).astype(bf16) for h, c in items]
    moved = [
        jnp.concatenate([(b[:, :HD] * marks[c][1]).astype(bf16), b[:, HD:].astype(bf16)], axis=1)
        for b, (h, c) in zip(both, items)
    ]
    steps = [dot_tn(t, m) for t, m in zip(tails, moved)]
    for i, (h, c) in enumerate(items):
        at = pl.ds(c * CHUNK, CHUNK)
        tinv_ref[h, at, :] = found[i]
        wu_ref[h, at, :] = both[i].astype(bf16)
        gain_ref[h, at, :] = steps[i][:, :HD].astype(bf16)
    eye = (row == col).astype(f32)
    states = [jnp.concatenate([eye, jnp.zeros_like(eye)], axis=1) for _ in heads]
    for c in range(chunks):
        lows = [state.astype(bf16) for state in states]
        for h in heads:
            pre_ref[h, pl.ds(c * CHUNK, CHUNK), :] = lows[h]
        gone = [dot_nn(steps[h * chunks + c][:, :HD], lows[h]) for h in heads]
        states = [
            marks[c][3] * states[h]
            - gone[h]
            + jnp.concatenate([jnp.zeros_like(eye), steps[h * chunks + c][:, HD:]], axis=1)
            for h in heads
        ]
    for h in heads:
        total_ref[h] = states[h].astype(bf16)


def col_spec(rows, base, count=1):
    return pl.BlockSpec((rows, count * HD), lambda h: (0, base // count + h))


def full_spec(shape):
    return pl.BlockSpec(shape, lambda h: (0,) * len(shape))


def head_spec(shape, count=1):
    return pl.BlockSpec((count,) + shape, lambda h: (h,) + (0,) * len(shape))


def params():
    return pltpu.CompilerParams(vmem_limit_bytes=VMEM_LIMIT, dimension_semantics=("arbitrary",))


def cost(micros, rows):
    return pl.CostEstimate(flops=0, bytes_accessed=int(micros * 3.69e6 * rows / 512), transcendentals=0)


def fwd_local(projected, taps, logits, dcol, drow, after):
    rows = projected.shape[0] - HALO
    chunks = rows // CHUNK
    sds = jax.ShapeDtypeStruct
    return pl.pallas_call(
        fwd_local_kernel,
        grid=(H // TOGETHER,),
        in_specs=[col_spec(rows + HALO, i * H, TOGETHER) for i in range(3)]
        + [col_spec(KW, 0, TOGETHER), col_spec(KW, H, TOGETHER), col_spec(KW, 2 * H, TOGETHER)]
        + [full_spec((rows, HD)), full_spec((rows + HALO, 1)), full_spec((chunks, CHUNK))]
        + [pl.BlockSpec(memory_space=pl.ANY) for _ in after],
        out_specs=[
            col_spec(rows, 0, TOGETHER),
            col_spec(rows, 0, TOGETHER),
            head_spec((rows, CHUNK), TOGETHER),
            head_spec((rows, 2 * HD), TOGETHER),
            head_spec((rows, HD), TOGETHER),
            head_spec((rows, 2 * HD), TOGETHER),
            head_spec((HD, 2 * HD), TOGETHER),
        ],
        out_shape=[
            sds((rows, D), bf16),
            sds((rows, D), bf16),
            sds((H, rows, CHUNK), bf16),
            sds((H, rows, 2 * HD), bf16),
            sds((H, rows, HD), bf16),
            sds((H, rows, 2 * HD), bf16),
            sds((H, HD, 2 * HD), bf16),
        ],
        scratch_shapes=[pltpu.VMEM((TOGETHER, rows + HALO, HD), f32)],
        compiler_params=params(),
        cost_estimate=cost(14.5, rows),
        name="delta_local",
    )(*([projected] * 3 + [taps] * 3 + [logits, dcol, drow]), *after)


def fwd_read_kernel(qn_ref, kn_ref, wu_ref, dcol_ref, drow_ref, r_ref, o_ref):
    rows = qn_ref.shape[0]
    row, col = tri_index()
    chunks = range(rows // CHUNK)
    ats = [pl.ds(c * CHUNK, CHUNK) for c in chunks]
    marks = [chunk_marks(dcol_ref, c) for c in chunks]
    keeps = [(marks[c][0] == drow_ref[pl.ds(c, 1), :]) & (col <= row) for c in chunks]
    items = [(h, c) for h in range(qn_ref.shape[1] // HD) for c in chunks]
    lanes = [pl.ds(h * HD, HD) for h, _ in items]
    parts = [dot_nt(qn_ref[ats[c], lane], kn_ref[ats[c], lane]) for lane, (h, c) in zip(lanes, items)]
    parts = [jnp.where(keeps[c], part, 0.0).astype(bf16) for part, (h, c) in zip(parts, items)]
    ws = [(wu_ref[h, ats[c], :HD].astype(f32) * marks[c][1]).astype(bf16) for h, c in items]
    both = [
        dot_nn(part, jnp.concatenate([w, wu_ref[h, ats[c], HD:]], axis=1)) for part, w, (h, c) in zip(parts, ws, items)
    ]
    for lane, b, (h, c) in zip(lanes, both, items):
        r_ref[ats[c], lane] = (qn_ref[ats[c], lane].astype(f32) * marks[c][1] - b[:, :HD]).astype(bf16)
        o_ref[ats[c], lane] = b[:, HD:]


def fwd_read(qn, kn, wu, dcol, drow):
    rows = qn.shape[0]
    chunks = rows // CHUNK
    sds = jax.ShapeDtypeStruct
    return pl.pallas_call(
        fwd_read_kernel,
        grid=(H // TOGETHER,),
        in_specs=[col_spec(rows, 0, TOGETHER), col_spec(rows, 0, TOGETHER), head_spec((rows, 2 * HD), TOGETHER), full_spec((rows + HALO, 1)), full_spec((chunks, CHUNK))],
        out_specs=[col_spec(rows, 0, TOGETHER), col_spec(rows, 0, TOGETHER)],
        out_shape=[sds((rows, D), bf16), sds((rows, D), f32)],
        compiler_params=params(),
        cost_estimate=cost(3.2, rows),
        name="delta_read",
    )(qn, kn, wu, dcol, drow)


def fwd_state_kernel(moves, paired, place_ref, *refs):
    ins, (state_ref, out_ref, head_ref) = refs[: moves + 5], refs[-3:]
    *near_refs, far_ref, pre_ref, r_ref, o_ref, gain_ref = ins
    rows = r_ref.shape[0]
    heads = range(r_ref.shape[1] // HD)
    states = [far_ref[h].astype(f32) for h in heads]
    if paired:
        states = [jnp.where(place_ref[0] >= 2, state, 0.0) for state in states]
    for near_ref in reversed(near_refs):
        moved = [dot_nn(near_ref[h, :, :HD], states[h]) + near_ref[h, :, HD:].astype(f32) for h in heads]
        states = [jnp.where(place_ref[0] % 2 == 1, m, s) if paired else m for m, s in zip(moved, states)]
    lows = [state.astype(bf16) for state in states]
    items = [(h, c) for h in heads for c in range(rows // CHUNK)]
    ats = [pl.ds(c * CHUNK, CHUNK) for _, c in items]
    lanes = [pl.ds(h * HD, HD) for h, _ in items]
    nows = [dot_nn(pre_ref[h, at, :HD], lows[h]) for at, (h, c) in zip(ats, items)]
    nows = [(now + pre_ref[h, at, HD:].astype(f32)).astype(bf16) for now, at, (h, c) in zip(nows, ats, items)]
    outs = [dot_nn(r_ref[at, lane], now) for at, lane, now in zip(ats, lanes, nows)]
    for out, now, at, lane, (h, c) in zip(outs, nows, ats, lanes, items):
        state_ref[h, at, :] = now
        o = o_ref[at, lane] + out
        out_ref[at, lane] = o
        scale = lax.rsqrt(jnp.mean(o * o, axis=-1, keepdims=True) + EPS_NORM)
        head_ref[at, lane] = (o * scale * gain_ref[...]).astype(bf16)


def fwd_state(place, paired, nears, far, pre, r, o, gain, after):
    rows = r.shape[0]
    sds = jax.ShapeDtypeStruct
    return pl.pallas_call(
        partial(fwd_state_kernel, len(nears), paired),
        grid=(H // TOGETHER,),
        in_specs=[
            pl.BlockSpec(memory_space=pltpu.SMEM),
            *[head_spec((HD, 2 * HD), TOGETHER) for _ in nears],
            head_spec((HD, HD), TOGETHER),
            head_spec((rows, 2 * HD), TOGETHER),
            col_spec(rows, 0, TOGETHER),
            col_spec(rows, 0, TOGETHER),
            full_spec((1, HD)),
            *[pl.BlockSpec(memory_space=pl.ANY) for _ in after],
        ],
        out_specs=[head_spec((rows, HD), TOGETHER), col_spec(rows, 0, TOGETHER), col_spec(rows, 0, TOGETHER)],
        out_shape=[sds((H, rows, HD), bf16), sds((rows, D), f32), sds((rows, D), bf16)],
        compiler_params=params(),
        cost_estimate=cost(4.3, rows),
        name="delta_state",
    )(place, *nears, far, pre, r, o, gain, *after)


def bwd_local_kernel(dhead_ref, o_ref, r_ref, gain_ref, step_ref, dcol_ref, *refs):
    do_ref, dgain_ref, total_ref = refs[-3:]
    rows = o_ref.shape[0]
    chunks = rows // CHUNK

    @pl.when(pl.program_id(0) == 0)
    def _():
        dgain_ref[...] = jnp.zeros_like(dgain_ref)

    heads = range(o_ref.shape[1] // HD)
    ats = [pl.ds(c * CHUNK, CHUNK) for c in range(chunks)]
    marks = [chunk_marks(dcol_ref, c)[3] for c in range(chunks)]
    dos = []
    for h in heads:
        lanes = pl.ds(h * HD, HD)
        o = o_ref[:, lanes]
        dy = dhead_ref[:, lanes].astype(f32)
        scale = lax.rsqrt(jnp.mean(o * o, axis=-1, keepdims=True) + EPS_NORM)
        x = o * scale
        dgain_ref[...] += jnp.sum(dy * x, axis=0, keepdims=True)
        dx = dy * gain_ref[...]
        do = (scale * (dx - x * jnp.mean(dx * x, axis=-1, keepdims=True))).astype(bf16)
        do_ref[:, lanes] = do
        dos.append(do)
    gives = [
        [dot_tn(r_ref[ats[c], pl.ds(h * HD, HD)], dos[h][c * CHUNK : (c + 1) * CHUNK]) for c in range(chunks)] for h in heads
    ]
    states = [gives[h][chunks - 1] for h in heads]
    for c in reversed(range(chunks - 1)):
        gone = [dot_tn(step_ref[h, ats[c], :], states[h]) for h in heads]
        states = [marks[c] * states[h] - gone[h] + gives[h][c] for h in heads]
    for h in heads:
        total_ref[h] = states[h].astype(bf16)


def bwd_local(dhead, o, r, gain, step, dcol, after):
    rows = o.shape[0]
    sds = jax.ShapeDtypeStruct
    return pl.pallas_call(
        bwd_local_kernel,
        grid=(H // TOGETHER,),
        in_specs=[col_spec(rows, 0, TOGETHER), col_spec(rows, 0, TOGETHER), col_spec(rows, 0, TOGETHER), full_spec((1, HD)), head_spec((rows, HD), TOGETHER), full_spec((rows + HALO, 1))]
        + [pl.BlockSpec(memory_space=pl.ANY) for _ in after],
        out_specs=[col_spec(rows, 0, TOGETHER), full_spec((1, HD)), head_spec((HD, HD), TOGETHER)],
        out_shape=[sds((rows, D), bf16), sds((1, HD), f32), sds((H, HD, HD), bf16)],
        compiler_params=params(),
        cost_estimate=cost(3.8, rows),
        name="delta_back_local",
    )(dhead, o, r, gain, step, dcol, *after)


def bwd_main_kernel(moves, paired, place_ref, *refs):
    later, refs = refs[: 2 * moves + 1], refs[2 * moves + 1 :]
    ins, outs = refs[:15], refs[-12:]
    bwd_main_body(place_ref if paired else None, later, *ins, *outs)


def bwd_main_body(
    place_ref, later, q_ref, k_ref, v_ref, tq_ref, tk_ref, tv_ref, lg_ref, dcol_ref, drow_ref,
    tinv_ref, wu_ref, step_ref, state_ref, r_ref, do_ref,
    dproj_ref, rq_ref, rk_ref, rv_ref, cq_ref, ck_ref, cv_ref, dl_ref, ext, grad, held, sems,
):
    group = pl.program_id(0)
    rows = q_ref.shape[0] - HALO
    chunks = range(rows // CHUNK)
    heads = range(q_ref.shape[1] // HD)
    masks = conv_masks(dcol_ref, rows)
    row, col = tri_index()
    cut = lambda x, c: x[c * CHUNK : (c + 1) * CHUNK]

    def filtered(x, taps, h, which):
        s = conv_sum(x, taps, masks, ext.at[which + 3 * h], h)
        gate = sigmoid(s)
        return low(s * gate), gate * (1.0 + s * (1.0 - gate))

    queries, slope_q, scale_q, qns = [], [], [], []
    keys, slope_k, scale_k, kns = [], [], [], []
    values, slope_v, betas, kbs = [], [], [], []
    for h in heads:
        query, slope = filtered(q_ref, tq_ref, h, 0)
        queries.append(query)
        slope_q.append(slope)
        scale_q.append(unit_scale(query))
        qns.append((query * scale_q[h] * HD**-0.5).astype(bf16))
        key, slope = filtered(k_ref, tk_ref, h, 1)
        slope_k.append(slope)
        scale_k.append(unit_scale(key))
        kns.append(key * scale_k[h])
        value, slope = filtered(v_ref, tv_ref, h, 2)
        values.append(value)
        slope_v.append(slope)
        betas.append(sigmoid(head_column(lg_ref[...].astype(f32), group * len(heads) + h)))
        kbs.append((betas[h] * kns[h]).astype(bf16))

    moves = len(later) // 2
    marks = [chunk_marks(dcol_ref, c) for c in chunks]
    ats = [pl.ds(c * CHUNK, CHUNK) for c in chunks]
    items = [(h, c) for h in heads for c in chunks]
    lanes = [pl.ds(h * HD, HD) for h in heads]
    dss = [later[-1][h].astype(f32) for h in heads]
    if place_ref is not None:
        dss = [jnp.where(place_ref[0] < 2, ds, 0.0) for ds in dss]
    for i in reversed(range(moves)):
        moved = [dot_tn(later[i][h], dss[h]) + later[moves + i][h].astype(f32) for h in heads]
        dss = [m if place_ref is None else jnp.where(place_ref[0] % 2 == 0, m, ds) for m, ds in zip(moved, dss)]
    gives = [dot_tn(r_ref[ats[c], lanes[h]], do_ref[ats[c], lanes[h]]) for h, c in items]
    leaving = {}
    for c in reversed(chunks):
        for h in heads:
            leaving[h, c] = dss[h].astype(bf16)
        if c:
            gone = [dot_tn(step_ref[h, ats[c], :], leaving[h, c]) for h in heads]
            dss = [marks[c][3] * dss[h] - gone[h] + gives[h * len(chunks) + c] for h in heads]

    each = range(len(items))
    carries = [marks[c][1] for _, c in items]
    tails = [marks[c][2] for _, c in items]
    sames = [marks[c][0] == drow_ref[pl.ds(c, 1), :] for c in chunks]
    uptos = [sames[c] & (col <= row) for _, c in items]
    belows = [sames[c] & (col < row) for _, c in items]
    q_cs = [cut(qns[h], c) for h, c in items]
    k_cs = [cut(kns[h], c).astype(bf16) for h, c in items]
    kb_cs = [cut(kbs[h], c) for h, c in items]
    dos = [do_ref[ats[c], lanes[h]] for h, c in items]
    wus = [wu_ref[h, ats[c], :] for h, c in items]
    states = [state_ref[h, ats[c], :] for h, c in items]
    leave = [leaving[item] for item in items]
    parts = [dot_nt(q_cs[i], k_cs[i]) for i in each]
    reads = [dot_nn(wus[i][:, :HD], states[i]) for i in each]
    kds = [dot_nn(k_cs[i], leave[i]) for i in each]
    parts = [jnp.where(uptos[i], parts[i], 0.0).astype(bf16) for i in each]
    deltas = [(wus[i][:, HD:].astype(f32) - carries[i] * reads[i]).astype(bf16) for i in each]
    pds = [dot_tn(parts[i], dos[i]) for i in each]
    dparts = [dot_nt(dos[i], deltas[i]) for i in each]
    dkfs = [dot_nt(deltas[i], leave[i]) for i in each]
    dds = [pds[i] + tails[i] * kds[i] for i in each]
    throughs = [dot_nt(jnp.concatenate([dos[i], dds[i].astype(bf16)], axis=0), states[i]) for i in each]
    inner = [
        jnp.concatenate([(-(carries[i] * throughs[i][CHUNK:])).astype(bf16), dds[i].astype(bf16)], axis=1) for i in each
    ]
    dwus = [dot_tn(tinv_ref[h, ats[c], :], x) for x, (h, c) in zip(inner, items)]
    dlows = [dot_nt(dwus[i], wus[i]) for i in each]
    pairs = [
        jnp.concatenate(
            [jnp.where(uptos[i], dparts[i], 0.0).astype(bf16), jnp.where(belows[i], -dlows[i], 0.0).astype(bf16)], axis=0
        )
        for i in each
    ]
    ontos = [dot_nn(pairs[i], k_cs[i]) for i in each]
    backs = [dot_tn(pairs[i], jnp.concatenate([q_cs[i], kb_cs[i]], axis=0)) for i in each]
    b_cs = [cut(betas[h], c) for h, c in items]
    dqs = [carries[i] * throughs[i][:CHUNK] + ontos[i][:CHUNK] for i in each]
    dkbs = [dwus[i][:, :HD] + ontos[i][CHUNK:] for i in each]
    dks = [backs[i] + tails[i] * dkfs[i] + b_cs[i] * dkbs[i] for i in each]
    dvs = [b_cs[i] * dwus[i][:, HD:] for i in each]
    dbs = [
        jnp.sum(dkbs[i] * cut(kns[h], c) + dwus[i][:, HD:] * cut(values[h], c), axis=1, keepdims=True)
        for i, (h, c) in zip(each, items)
    ]

    @pl.when(group == 0)
    def _():
        dl_ref[...] = jnp.zeros_like(dl_ref)

    slot = lax.rem(group, 2)
    width = len(heads) * HD

    def sent(step, which):
        start = pl.multiple_of(which * D + step * width, 128)
        return pltpu.make_async_copy(
            held.at[lax.rem(step, 2), which], dproj_ref.at[:, pl.ds(start, width)], sems.at[lax.rem(step, 2), which]
        )

    @pl.when(group >= 2)
    def _():
        for which in range(3):
            sent(group - 2, which).wait()

    for i in range(KW - 1):
        grad[i, pl.ds(0, HALO), :] = jnp.zeros((HALO, HD), f32)
        grad[i, pl.ds(HALO + rows, 8), :] = jnp.zeros((8, HD), f32)

    def conv_back(dfilt, slope, taps_ref, rim_ref, dtap_ref, h, which):
        ds_ = low(dfilt) * slope
        lane = lanes[h]
        x = ext.at[which + 3 * h]
        dtap_ref[pl.ds(KW - 1, 1), lane] = jnp.sum(ds_ * x[pl.ds(HALO, rows), :], axis=0, keepdims=True)
        total = ds_ * taps_ref[pl.ds(KW - 1, 1), lane]
        rim = jnp.zeros((HALO, HD), f32)
        for i in range(KW - 1):
            masked = ds_ * masks[i]
            grad[i, pl.ds(HALO, rows), :] = masked
            place_i = pl.ds(HALO - KW + 1 + i, rows)
            dtap_ref[pl.ds(i, 1), lane] = jnp.sum(masked * x[place_i, :], axis=0, keepdims=True)
            tap = taps_ref[pl.ds(i, 1), lane]
            total = total + tap * grad[i, pl.ds(HALO + KW - 1 - i, rows), :]
            rim = rim + tap * grad[i, pl.ds(KW - 1 - i, HALO), :]
        rim_ref[:, lane] = rim.astype(bf16)
        held[slot, which, :, lane] = total.astype(bf16)

    lane_index = lax.broadcasted_iota(jnp.int32, (rows, HD), 1)
    for h in heads:
        join = lambda parts: jnp.concatenate(parts[h * len(chunks) : (h + 1) * len(chunks)], axis=0)
        dqn = join(dqs) * HD**-0.5
        unit = queries[h] * scale_q[h]
        dquery = scale_q[h] * (dqn - unit * jnp.sum(dqn * unit, axis=-1, keepdims=True))
        dkn = join(dks)
        dkeys = scale_k[h] * (dkn - kns[h] * jnp.sum(dkn * kns[h], axis=-1, keepdims=True))
        dlogit = join(dbs) * betas[h] * (1.0 - betas[h])
        dl_ref[...] = jnp.where(
            lane_index == group * len(heads) + h, dlogit, dl_ref[...].astype(f32)
        ).astype(bf16)
        conv_back(dquery, slope_q[h], tq_ref, rq_ref, cq_ref, h, 0)
        conv_back(dkeys, slope_k[h], tk_ref, rk_ref, ck_ref, h, 1)
        conv_back(join(dvs), slope_v[h], tv_ref, rv_ref, cv_ref, h, 2)
    for which in range(3):
        sent(group, which).start()

    @pl.when(group == pl.num_programs(0) - 1)
    def _():
        for which in range(3):
            sent(group - 1, which).wait()
            sent(group, which).wait()


def bwd_main(place, paired, moves, gives, projected, taps, logits, dcol, drow, tinv, wu, step, state, r, do, after):
    rows = projected.shape[0] - HALO
    chunks = rows // CHUNK
    sds = jax.ShapeDtypeStruct
    return pl.pallas_call(
        partial(bwd_main_kernel, len(moves), paired),
        grid=(H // TOGETHER_BACK,),
        in_specs=[pl.BlockSpec(memory_space=pltpu.SMEM)]
        + [head_spec((HD, HD), TOGETHER_BACK) for _ in (*moves, *gives)]
        + [col_spec(rows + HALO, i * H, TOGETHER_BACK) for i in range(3)]
        + [col_spec(KW, 0, TOGETHER_BACK), col_spec(KW, H, TOGETHER_BACK), col_spec(KW, 2 * H, TOGETHER_BACK)]
        + [full_spec((rows, HD)), full_spec((rows + HALO, 1)), full_spec((chunks, CHUNK))]
        + [head_spec((rows, CHUNK), TOGETHER_BACK), head_spec((rows, 2 * HD), TOGETHER_BACK), head_spec((rows, HD), TOGETHER_BACK), head_spec((rows, HD), TOGETHER_BACK)]
        + [col_spec(rows, 0, TOGETHER_BACK), col_spec(rows, 0, TOGETHER_BACK)]
        + [pl.BlockSpec(memory_space=pl.ANY) for _ in after],
        out_specs=[pl.BlockSpec(memory_space=pl.ANY)] + [col_spec(HALO, 0, TOGETHER_BACK)] * 3 + [col_spec(KW, 0, TOGETHER_BACK)] * 3 + [full_spec((rows, HD))],
        out_shape=[sds((rows, 3 * D), bf16)] + [sds((HALO, D), bf16)] * 3 + [sds((KW, D), f32)] * 3 + [sds((rows, HD), bf16)],
        scratch_shapes=[
            pltpu.VMEM((3 * TOGETHER_BACK, rows + HALO, HD), f32),
            pltpu.VMEM((KW - 1, rows + HALO + 8, HD), f32),
            pltpu.VMEM((2, 3, rows, TOGETHER_BACK * HD), bf16),
            pltpu.SemaphoreType.DMA((2, 3)),
        ],
        compiler_params=params(),
        cost_estimate=cost(24, rows),
        name="delta_back",
    )(place, *moves, *gives, *([projected] * 3 + [taps] * 3), logits, dcol, drow, tinv, wu, step, state, r, do, *after)


def pair_forward_kernel(place_ref, own_ref, other_ref, out_ref):
    late = place_ref[0] % 2 == 1
    for h in range(H):
        own, partner = own_ref[h].astype(f32), other_ref[h].astype(f32)
        first, second = jnp.where(late, partner, own), jnp.where(late, own, partner)
        out_ref[h] = (dot_nn(second[:, :HD], first[:, HD:]) + second[:, HD:]).astype(bf16)


def pair_backward_kernel(place_ref, own_a_ref, other_a_ref, own_ref, other_ref, out_ref):
    late = place_ref[0] % 2 == 1
    for h in range(H):
        own, partner = own_ref[h].astype(f32), other_ref[h].astype(f32)
        first, second = jnp.where(late, partner, own), jnp.where(late, own, partner)
        passed = jnp.where(late, other_a_ref[h, :, :HD].astype(f32), own_a_ref[h, :, :HD].astype(f32))
        out_ref[h] = (first + dot_tn(passed, second)).astype(bf16)


def pair_state(kernel, place, *arrays, after=()):
    count = len(arrays) + 1
    return pl.pallas_call(
        lambda *refs: kernel(*refs[:count], refs[-1]),
        in_specs=[pl.BlockSpec(memory_space=pltpu.SMEM)]
        + [pl.BlockSpec(memory_space=pltpu.VMEM)] * len(arrays)
        + [pl.BlockSpec(memory_space=pl.ANY)] * len(after),
        out_specs=pl.BlockSpec(memory_space=pltpu.VMEM),
        out_shape=jax.ShapeDtypeStruct((H, HD, HD), bf16),
        cost_estimate=cost(3, 512),
        name="pair_state",
        compiler_params=pltpu.CompilerParams(vmem_limit_bytes=VMEM_LIMIT),
    )(place, *arrays, *after)


def project_kernel(tail_ref, gain_ref, normed_ref, weight_ref, beta_ref, out_ref, logits_ref, low_tail):
    @pl.when(pl.program_id(0) == 0)
    def _():
        tail = tail_ref[...]
        scale = lax.rsqrt(jnp.mean(tail * tail, axis=-1, keepdims=True) + EPS_NORM)
        low_tail[...] = (tail * scale * gain_ref[...]).astype(bf16)
        logits_ref[...] = dot_nn(normed_ref[...], beta_ref[...]).astype(bf16)

    out_ref[pl.ds(0, HALO), :] = dot_nn(low_tail[...], weight_ref[...]).astype(bf16)
    out_ref[pl.ds(HALO, normed_ref.shape[0]), :] = dot_nn(normed_ref[...], weight_ref[...]).astype(bf16)


def project(tail, gain, normed, weight, beta, after, steps=4):
    rows, width = normed.shape[0], weight.shape[1]
    sds = jax.ShapeDtypeStruct
    return pl.pallas_call(
        lambda *refs: project_kernel(*refs[:5], *refs[-3:]),
        grid=(steps,),
        in_specs=[
            full_spec(tail.shape),
            full_spec((1, D)),
            full_spec(normed.shape),
            pl.BlockSpec((D, width // steps), lambda j: (0, j)),
            full_spec(beta.shape),
        ]
        + [pl.BlockSpec(memory_space=pl.ANY) for _ in after],
        out_specs=[pl.BlockSpec((rows + HALO, width // steps), lambda j: (0, j)), full_spec((rows, beta.shape[1]))],
        out_shape=[sds((rows + HALO, width), bf16), sds((rows, beta.shape[1]), bf16)],
        scratch_shapes=[pltpu.VMEM((HALO, D), bf16)],
        compiler_params=params(),
        cost_estimate=cost(5, rows),
        name="project",
    )(tail, gain, normed, weight, beta, *after)


def branch_kernel(x_ref, weight_ref, stream_ref, valid_ref, gain_ref, out_ref, normed_ref, sums_ref, total, *, last):
    step = pl.program_id(0)

    @pl.when(step == 0)
    def _():
        total[...] = jnp.zeros_like(total)

    total[...] += dot_nn(x_ref[...], weight_ref[...])

    @pl.when(step == pl.num_programs(0) - 1)
    def _():
        branch = total[...]
        stream = stream_ref[...] + branch
        out_ref[...] = stream
        sums_ref[pl.ds(0, 1), :] = jnp.sum(branch * branch * valid_ref[...], axis=0, keepdims=True)
        square = stream * stream
        sums_ref[pl.ds(1, 1), :] = jnp.sum(square * valid_ref[...], axis=0, keepdims=True)
        if last:
            normed_ref[...] = stream.astype(bf16)
        else:
            scale = lax.rsqrt(jnp.mean(square, axis=-1, keepdims=True) + EPS_NORM)
            normed_ref[...] = (stream * scale * gain_ref[...]).astype(bf16)


def branch(x, weight, stream, valid, gain, last, after, steps):
    rows, depth = x.shape
    sds = jax.ShapeDtypeStruct
    return pl.pallas_call(
        lambda *refs: branch_kernel(*refs[:5], *refs[-4:], last=last),
        grid=(steps,),
        in_specs=[
            pl.BlockSpec((rows, depth // steps), lambda j: (0, j)),
            pl.BlockSpec((depth // steps, D), lambda j: (j, 0)),
            full_spec((rows, D)),
            full_spec((rows, 1)),
            full_spec((1, D)),
        ]
        + [pl.BlockSpec(memory_space=pl.ANY) for _ in after],
        out_specs=[full_spec((rows, D)), full_spec((rows, D)), full_spec((2, D))],
        out_shape=[sds((rows, D), f32), sds((rows, D), bf16), sds((2, D), f32)],
        scratch_shapes=[pltpu.VMEM((rows, D), f32)],
        compiler_params=params(),
        cost_estimate=cost(5, rows),
        name="branch",
    )(x, weight, stream, valid, gain, *after)


def act_kernel(x_ref, gate_ref, up_ref, act_ref, both_ref):
    gate = dot_nn(x_ref[...], gate_ref[...])
    up = dot_nn(x_ref[...], up_ref[...])
    act_ref[...] = (gate * sigmoid(gate) * up).astype(bf16)
    both_ref[0] = gate.astype(bf16)
    both_ref[1] = up.astype(bf16)


def gated(x, weight, after, steps=11):
    rows, half = x.shape[0], weight.shape[1] // 2
    size = half // steps
    sds = jax.ShapeDtypeStruct
    return pl.pallas_call(
        lambda *refs: act_kernel(*refs[:3], *refs[-2:]),
        grid=(steps,),
        in_specs=[
            full_spec(x.shape),
            pl.BlockSpec((D, size), lambda j: (0, j)),
            pl.BlockSpec((D, size), lambda j: (0, steps + j)),
        ]
        + [pl.BlockSpec(memory_space=pl.ANY) for _ in after],
        out_specs=[pl.BlockSpec((rows, size), lambda j: (0, j)), pl.BlockSpec((2, rows, size), lambda j: (0, 0, j))],
        out_shape=[sds((rows, half), bf16), sds((2, rows, half), bf16)],
        compiler_params=params(),
        cost_estimate=cost(9, rows),
        name="gated",
    )(x, weight, weight, *after)


def act_back_kernel(g_ref, down_ref, both_ref, out_ref):
    dact = dot_nt(g_ref[...], down_ref[...])
    gate, up = both_ref[0].astype(f32), both_ref[1].astype(f32)
    part = sigmoid(gate)
    silu = gate * part
    out_ref[0] = (dact * up * (part + silu * (1.0 - part))).astype(bf16)
    out_ref[1] = (dact * silu).astype(bf16)


def gated_back(g, down, both, after, steps=11):
    rows, half = g.shape[0], down.shape[0]
    size = half // steps
    block = pl.BlockSpec((2, rows, size), lambda j: (0, 0, j))
    return pl.pallas_call(
        lambda *refs: act_back_kernel(*refs[:3], refs[-1]),
        grid=(steps,),
        in_specs=[full_spec(g.shape), pl.BlockSpec((size, D), lambda j: (j, 0)), block]
        + [pl.BlockSpec(memory_space=pl.ANY) for _ in after],
        out_specs=block,
        out_shape=jax.ShapeDtypeStruct((2, rows, half), bf16),
        compiler_params=params(),
        cost_estimate=cost(8, rows),
        name="gated_back",
    )(g, down, both, *after)


def norm_back_kernel(d_ref, weight_ref, extra_ref, extra_weight_ref, stream_ref, g_ref, gain_ref, out_ref, low_ref, dgain_ref, total):
    step = pl.program_id(0)

    @pl.when(step == 0)
    def _():
        if extra_ref is None:
            total[...] = jnp.zeros_like(total)
        else:
            total[...] = dot_nt(extra_ref[...], extra_weight_ref[...])

    block = d_ref[0] if len(d_ref.shape) == 3 else d_ref[...]
    total[...] += dot_nt(block, weight_ref[...])

    @pl.when(step == pl.num_programs(0) - 1)
    def _():
        dn = total[...]
        stream = stream_ref[...]
        scale = lax.rsqrt(jnp.mean(stream * stream, axis=-1, keepdims=True) + EPS_NORM)
        x = stream * scale
        dgain_ref[...] = jnp.sum(dn * x, axis=0, keepdims=True)
        dx = dn * gain_ref[...]
        g = g_ref[...] + scale * (dx - x * jnp.mean(dx * x, axis=-1, keepdims=True))
        out_ref[...] = g
        low_ref[...] = g.astype(bf16)


def norm_back(d, weight, extra, stream, g, gain, after):
    rows = stream.shape[0]
    steps = 4
    size = weight.shape[1] // steps
    sds = jax.ShapeDtypeStruct
    if d.ndim == 3:
        d_spec = pl.BlockSpec((1, rows, size), lambda k: (k // 2, 0, k % 2))
    else:
        d_spec = pl.BlockSpec((rows, size), lambda k: (0, k))
    count = 5 + len(extra)

    def kernel(*refs):
        ins, outs = refs[:count], refs[-4:]
        more = ins[2 : 2 + len(extra)] if extra else (None, None)
        norm_back_kernel(*ins[:2], *more, *ins[2 + len(extra) :], *outs)

    return pl.pallas_call(
        kernel,
        grid=(steps,),
        in_specs=[d_spec, pl.BlockSpec((D, size), lambda k: (0, k))]
        + [full_spec(array.shape) for array in extra]
        + [full_spec((rows, D)), full_spec((rows, D)), full_spec((1, D))]
        + [pl.BlockSpec(memory_space=pl.ANY) for _ in after],
        out_specs=[full_spec((rows, D)), full_spec((rows, D)), full_spec((1, D))],
        out_shape=[sds((rows, D), f32), sds((rows, D), bf16), sds((1, D), f32)],
        scratch_shapes=[pltpu.VMEM((rows, D), f32)],
        compiler_params=params(),
        cost_estimate=cost(9, rows),
        name="norm_back",
    )(d, weight, *extra, stream, g, gain, *after)


def other(block, axis, mask):
    return lax.ppermute(block, axis, [(i, i ^ mask) for i in range(lax.axis_size(axis))])


def sum_over(block, axis):
    mask = 1
    while mask < lax.axis_size(axis):
        block = block + other(block, axis, mask)
        mask *= 2
    return block


ANY = pl.BlockSpec(memory_space=pl.ANY)
SMEM = pl.BlockSpec(memory_space=pltpu.SMEM)
VMEM = pl.BlockSpec(memory_space=pltpu.VMEM)


def run_copies(pairs, sems):
    copies = [pltpu.make_async_copy(src, dst, sems.at[i]) for i, (src, dst) in enumerate(pairs)]
    for copy in copies:
        copy.start()
    for copy in copies:
        copy.wait()


def aligned(index, size):
    return pl.ds(pl.multiple_of(index * size, 128), size)


def offsets(sizes):
    return [sum(sizes[:i]) for i in range(len(sizes))]


def pack_kernel(place_ref, *refs, plan):
    count = sum(len(sizes) for _, sizes in plan)
    ins, outs, sems = list(refs[:count]), refs[-len(plan) - 1 : -1], refs[-1]
    quarter = place_ref[0]
    pairs = []
    for (layer, sizes), out_ref in zip(plan, outs):
        for at, size in zip(offsets(sizes), sizes):
            pairs.append((ins.pop(0).at[layer, :, aligned(quarter, size)], out_ref.at[:, pl.ds(at, size)]))
    run_copies(pairs, sems)


def pack(place, groups, after):
    plan = [(layer, [weight.shape[2] // 4 for weight in weights]) for weights, layer in groups]
    weights = [weight for group, _ in groups for weight in group]
    return pl.pallas_call(
        partial(pack_kernel, plan=plan),
        in_specs=[SMEM] + [ANY] * (len(weights) + len(after)),
        out_specs=[VMEM] * len(groups),
        out_shape=[jax.ShapeDtypeStruct((128, sum(sizes)), bf16) for _, sizes in plan],
        scratch_shapes=[pltpu.SemaphoreType.DMA((len(weights),))],
        cost_estimate=cost(2 * len(groups), 512),
        name="pack_quarters",
        compiler_params=pltpu.CompilerParams(vmem_limit_bytes=VMEM_LIMIT),
    )(place, *weights, *after)


def spread_kernel(place_ref, *refs, sizes):
    pieces, outs, sems = refs[:10], refs[-len(sizes) - 1 : -1], refs[-1]
    seq, core = place_ref[0], place_ref[1]
    chips = outs[0].shape[0]
    pairs = []
    for own, (h, x, y, a, b) in ((core, pieces[:5]), (1 - core, pieces[5:])):
        for piece, mask, at in ((h, 0, 0), (x, 1, 0), (y, 2, 0), (a, 3, 0), (b, 3, chips // 2)):
            here = pl.ds(at, piece.shape[0])
            for out_ref, start, size in zip(outs, offsets(sizes), sizes):
                pairs.append((piece.at[:, :, pl.ds(start, size)], out_ref.at[here, own, :, aligned(seq ^ mask, size)]))
    run_copies(pairs, sems)


def spread(place, pieces, sizes, after):
    chips = pieces[0].shape[0] // 128
    pieces = [piece.reshape(-1, 128, piece.shape[1]) for piece in pieces]
    weights = pl.pallas_call(
        partial(spread_kernel, sizes=sizes),
        in_specs=[SMEM] + [ANY] * (len(pieces) + len(after)),
        out_specs=[VMEM] * len(sizes),
        out_shape=[jax.ShapeDtypeStruct((chips, 2, 128, size * 4), bf16) for size in sizes],
        scratch_shapes=[pltpu.SemaphoreType.DMA((len(pieces) * len(sizes),))],
        compiler_params=pltpu.CompilerParams(vmem_limit_bytes=VMEM_LIMIT),
        cost_estimate=cost(7, 512),
        name="spread_weights",
    )(place, *pieces, *after)
    return [weight.reshape(-1, weight.shape[3]) for weight in weights]


def gate(array, after):
    return pl.pallas_call(
        lambda *refs: None,
        in_specs=[ANY] * (1 + len(after)),
        out_specs=ANY,
        out_shape=jax.ShapeDtypeStruct(array.shape, array.dtype),
        input_output_aliases={0: 0},
        cost_estimate=cost(0.5, 512),
        name="gate",
        compiler_params=pltpu.CompilerParams(vmem_limit_bytes=VMEM_LIMIT),
    )(array, *after)


def relay_kernel(x_ref, y_ref, *refs):
    a_ref, b_ref, _, _, sems = refs[-5:]
    half = a_ref.shape[0]
    run_copies([(x_ref.at[pl.ds(0, half)], a_ref), (y_ref.at[pl.ds(half, half)], b_ref)], sems)


def relay(over_x, over_y, after):
    half = jax.ShapeDtypeStruct((over_x.shape[0] // 2, over_x.shape[1]), over_x.dtype)
    whole = jax.ShapeDtypeStruct(over_x.shape, over_x.dtype)
    a, b, over_x, over_y = pl.pallas_call(
        relay_kernel,
        in_specs=[ANY] * (2 + len(after)),
        out_specs=[VMEM] * 2 + [ANY] * 2,
        out_shape=[half] * 2 + [whole] * 2,
        input_output_aliases={0: 2, 1: 3},
        scratch_shapes=[pltpu.SemaphoreType.DMA((2,))],
        cost_estimate=cost(2.5, 512),
        name="relay",
        compiler_params=pltpu.CompilerParams(vmem_limit_bytes=VMEM_LIMIT),
    )(over_x, over_y, *after)
    return (a, b), (over_x, over_y)


def core_groups():
    return [list(range(core, lax.axis_size("fsdp"), 2)) for core in range(2)]


def gather_chips(packed):
    return lax.all_gather(packed, "fsdp", axis=0, axis_index_groups=core_groups(), tiled=True)


def scatter_chips(total):
    return lax.psum_scatter(total, "fsdp", scatter_dimension=0, axis_index_groups=core_groups(), tiled=True)


def first_round(block):
    return other(block, "seq", 1), other(block, "seq", 2)


def second_round(passed):
    return other(passed[0], "seq", 2), other(passed[1], "seq", 1)


def interleaved(ref, core):
    blocks = ref.shape[1] // 256
    return jnp.concatenate([ref[:, aligned(2 * z + core, 128)] for z in range(blocks)], axis=1)


def grad_pieces_kernel(place_ref, *refs, count):
    ins, (o0_ref, o1_ref, o2_ref, oa_ref, ob_ref), scratch = refs[: 4 * count], refs[-6 - count : -1 - count], refs[-1 - count :]
    lefts, rights, turned, total = ins[: 2 * count], ins[2 * count :], scratch[:count], scratch[count]
    step = pl.program_id(0)
    tokens = lefts[0].shape[0]

    @pl.when(step == 0)
    def _():
        for i in range(2 * count):
            turned[i // 2][:, pl.ds((i % 2) * tokens, tokens)] = interleaved(lefts[i], place_ref[1]).T

    start = 0
    for i in range(count):
        a_ref, b_ref = rights[2 * i : 2 * i + 2]
        size = a_ref.shape[-1]
        a, b = [ref[0] if len(ref.shape) == 3 else ref[...] for ref in (a_ref, b_ref)]
        total[:, pl.ds(start, size)] = (
            dot_nn(turned[i][:, pl.ds(0, tokens)], a) + dot_nn(turned[i][:, pl.ds(tokens, tokens)], b)
        ).astype(bf16)
        start += size
    half = total.shape[0] // 2
    for i, out in enumerate((o0_ref, o1_ref, o2_ref)):

        @pl.when(step == i)
        def _(out=out):
            out[...] = total[...]

    @pl.when(step == 3)
    def _():
        oa_ref[...] = total[pl.ds(0, half), :]
        ob_ref[...] = total[pl.ds(half, half), :]


def grad_pieces(place, pairs, after):
    lefts = [left for pair in pairs for left in pair[0]]
    rights = [right for pair in pairs for right in pair[1]]
    tokens, rows = lefts[0].shape[0], lefts[0].shape[1] // 2
    sizes = [right.size // tokens // 4 for right in rights]
    width = sum(sizes[::2])
    whole = lambda array: pl.BlockSpec(array.shape, lambda j, place_ref: (0, 0))

    def quarter(right, size):
        if right.ndim == 2:
            return pl.BlockSpec((tokens, size), lambda j, place_ref: (0, place_ref[0] ^ j))
        return pl.BlockSpec(
            (1, tokens, size), lambda j, place_ref: ((place_ref[0] ^ j) // 2, 0, lax.rem(place_ref[0] ^ j, 2))
        )

    shapes = [(rows, width)] * 3 + [(rows // 2, width)] * 2
    return pl.pallas_call(
        partial(grad_pieces_kernel, count=len(pairs)),
        grid_spec=pltpu.PrefetchScalarGridSpec(
            num_scalar_prefetch=1,
            grid=(4,),
            in_specs=[whole(left) for left in lefts] + [quarter(right, size) for right, size in zip(rights, sizes)] + [ANY] * len(after),
            out_specs=[pl.BlockSpec(shape, lambda j, place_ref: (0, 0)) for shape in shapes],
            scratch_shapes=[pltpu.VMEM((rows, 2 * tokens), bf16) for _ in pairs] + [pltpu.VMEM((rows, width), bf16)],
        ),
        out_shape=[jax.ShapeDtypeStruct(shape, bf16) for shape in shapes],
        compiler_params=pltpu.CompilerParams(vmem_limit_bytes=VMEM_LIMIT),
        cost_estimate=cost(12, 512),
        name="grad_pieces",
    )(place, *lefts, *rights, *after)


def settle_kernel(place_ref, *refs, sizes):
    pieces, outs = refs[:5], refs[-len(sizes) :]
    rows = pieces[0].shape[0]
    masks = ((0, 0, rows), (1, 0, rows), (2, 0, rows), (3, 0, rows // 2), (3, rows // 2, rows // 2))
    for piece, (mask, at, count) in zip(pieces, masks):
        for out_ref, start, size in zip(outs, offsets(sizes), sizes):
            out_ref[0, pl.ds(at, count), aligned(place_ref[0] ^ mask, size)] = piece[:, pl.ds(start, size)].astype(f32)


def settle(place, pieces, sizes, layer, so_far):
    rows = pieces[0].shape[0]
    whole = lambda array: pl.BlockSpec(array.shape, lambda i: (0, 0))
    return pl.pallas_call(
        partial(settle_kernel, sizes=sizes),
        grid=(1,),
        in_specs=[SMEM] + [whole(piece) for piece in pieces] + [ANY] * len(so_far),
        out_specs=[pl.BlockSpec((1, rows, 4 * size), lambda i: (layer, 0, 0)) for size in sizes],
        out_shape=[jax.ShapeDtypeStruct((LAYERS, rows, 4 * size), f32) for size in sizes],
        input_output_aliases={6 + i: i for i in range(len(so_far))},
        compiler_params=pltpu.CompilerParams(vmem_limit_bytes=VMEM_LIMIT),
        cost_estimate=cost(3, 512),
        name="settle_gradient",
    )(place, *pieces, *so_far)


def merge_kernel(x_ref, y_ref, a_ref, b_ref, *refs):
    ox_ref, oy_ref = refs[-2:]
    ox_ref[...] = (x_ref[...].astype(f32) + b_ref[...].astype(f32)).astype(bf16)
    oy_ref[...] = (y_ref[...].astype(f32) + a_ref[...].astype(f32)).astype(bf16)


def merge(over_x, over_y, diag_a, diag_b, after):
    half, width = diag_a.shape
    rows = half // 4
    lower = pl.BlockSpec((rows, width), lambda i: (i, 0))
    upper = pl.BlockSpec((rows, width), lambda i: (i + 4, 0))
    whole = jax.ShapeDtypeStruct(over_x.shape, bf16)
    return pl.pallas_call(
        merge_kernel,
        grid=(4,),
        in_specs=[upper, lower, lower, lower] + [ANY] * len(after),
        out_specs=[upper, lower],
        out_shape=[whole, whole],
        input_output_aliases={0: 0, 1: 1},
        compiler_params=pltpu.CompilerParams(vmem_limit_bytes=VMEM_LIMIT),
        cost_estimate=cost(3.5, 512),
        name="merge",
    )(over_x, over_y, diag_a, diag_b, *after)


def total_kernel(own_ref, x_ref, y_ref, *refs):
    refs[-1][...] = (own_ref[...].astype(f32) + x_ref[...].astype(f32) + y_ref[...].astype(f32)).astype(bf16)


def total_of(own, from_x, from_y, after):
    rows, width = own.shape
    block = pl.BlockSpec((rows // 4, width), lambda i: (i, 0))
    return pl.pallas_call(
        total_kernel,
        grid=(4,),
        in_specs=[block] * 3 + [ANY] * len(after),
        out_specs=block,
        out_shape=jax.ShapeDtypeStruct(own.shape, bf16),
        compiler_params=pltpu.CompilerParams(vmem_limit_bytes=VMEM_LIMIT),
        cost_estimate=cost(4, 512),
        name="total",
    )(own, from_x, from_y, *after)


def gather_start(scattered, after):
    block = gate(scattered, after) if after else scattered
    return block, first_round(block)


def gather_settle(place, block, over, sizes, layer, so_far, after):
    passed, over = relay(*over, after)
    pieces = [block, *over, *second_round(passed)]
    return settle(place, pieces, sizes, layer, so_far), passed


def small_kernel(*refs):
    ins, out_ref = refs[:-1], refs[-1]
    at = 0
    out_ref[...] = jnp.zeros_like(out_ref)
    for ref in ins:
        for start in range(0, ref.shape[1], D):
            size = min(D, ref.shape[1] - start)
            out_ref[pl.ds(at, ref.shape[0]), pl.ds(0, size)] = ref[:, pl.ds(start, size)]
            at += ref.shape[0]


def small_rows(arrays):
    counts = [array.shape[0] * -(-array.shape[1] // D) for array in arrays]
    packed = pl.pallas_call(
        small_kernel,
        in_specs=[VMEM] * len(arrays),
        out_specs=VMEM,
        out_shape=jax.ShapeDtypeStruct((-(-sum(counts) // 8) * 8, D), f32),
        cost_estimate=cost(2, 512),
        name="small_rows",
        compiler_params=pltpu.CompilerParams(vmem_limit_bytes=VMEM_LIMIT),
    )(*arrays)
    return packed, offsets(counts)


def small_part(packed, start, shape):
    parts = -(-shape[1] // D)
    rows = [packed[start + i * shape[0] : start + (i + 1) * shape[0], : min(D, shape[1])] for i in range(parts)]
    return jnp.concatenate(rows, axis=1)


epsilon_norm = EPS_NORM


def shifted(block, axis, distance):
    devices = range(lax.axis_size(axis))
    route = [(i - distance, i) for i in devices if i - distance in devices]
    return lax.ppermute(block, axis, route)


def root_norm(values, gain):
    return (
        values * lax.rsqrt(jnp.mean(values * values, axis=-1, keepdims=True) + epsilon_norm) * gain
    )


def swiglu_act(gate_up):
    half_width = gate_up.shape[1] // 2
    return jax.nn.silu(gate_up[:, :half_width]) * gate_up[:, half_width:]


def contract_last(left, right):
    return lax.dot_general(
        left, right, (((1,), (1,)), ((), ())), preferred_element_type=jnp.float32
    )


def contract_first(left, right):
    return lax.dot_general(
        left, right, (((0,), (0,)), ((), ())), preferred_element_type=jnp.float32
    )


def fetch_rows(weights):
    return lax.all_gather(weights, "fsdp", axis=0, tiled=True)


def reduce_rows(left, right):
    return lax.psum_scatter(
        contract_first(left, right).astype(jnp.bfloat16), "fsdp", scatter_dimension=0, tiled=True
    )


def documents(segments, rows):
    doc_pad = jnp.concatenate([jnp.full((HALO,), -1, jnp.int32), segments])
    dcol = lax.dynamic_slice_in_dim(doc_pad, lax.axis_index("seq") * rows, rows + HALO)
    return dcol[:, None], dcol[HALO:].reshape(rows // CHUNK, CHUNK)


def on_device(
    tokens,
    segments,
    valid_mask,
    norm_gains,
    head_gain,
    conv_weight,
    beta_weight,
    qkv_weight,
    out_weight,
    gate_up_weight,
    down_weight,
    cotangent,
):
    rows = tokens.shape[1]
    pieces = lax.axis_size("seq")
    dcol, drow = documents(segments[0], rows)
    place = jnp.stack([lax.axis_index("seq"), lax.axis_index("fsdp") % 2]).astype(jnp.int32)
    valid_rows = valid_mask[0].astype(jnp.float32)
    stream = tokens[0].astype(jnp.float32)
    square_sums = []
    stored = []
    for at in range(LAYERS):
        qkv_full = fetch_rows(qkv_weight[at])
        out_full = fetch_rows(out_weight[at])
        gate_up_full = fetch_rows(gate_up_weight[at])
        down_full = fetch_rows(down_weight[at])
        square_sums.append(jnp.sum(jnp.sum(stream * stream, axis=1) * valid_rows))
        normed_one, pull_one = jax.vjp(root_norm, stream, norm_gains[at, 0])
        normed_one = normed_one.astype(jnp.bfloat16)
        projected = jnp.dot(normed_one, qkv_full, preferred_element_type=jnp.float32).astype(bf16)
        logits = jnp.dot(normed_one, beta_weight[at], preferred_element_type=jnp.float32).astype(bf16)
        logits = jnp.pad(logits, ((0, 0), (0, HD - H)))
        projected = jnp.concatenate([shifted(projected[rows - HALO :], "seq", 1), projected], axis=0)
        qn, kn, tinv, wu, step, pre, total = fwd_local(
            projected, conv_weight[at], logits, dcol, drow, []
        )
        nears = [shifted(total, "seq", d) for d in range(1, pieces - 1)]
        far = shifted(total[:, :, HD:], "seq", pieces - 1)
        moves = [shifted(total[:, :, :HD], "seq", -d) for d in range(1, pieces - 1)]
        reads, local_out = fwd_read(qn, kn, wu, dcol, drow)
        state, mixed, attended = fwd_state(
            place, False, nears, far, pre, reads, local_out, head_gain[at][None], []
        )
        branch = jnp.dot(attended, out_full, preferred_element_type=jnp.float32)
        square_sums.append(jnp.sum(jnp.sum(branch * branch, axis=1) * valid_rows))
        stream = stream + branch
        normed_two, pull_two = jax.vjp(root_norm, stream, norm_gains[at, 1])
        normed_two = normed_two.astype(jnp.bfloat16)
        gate_up = jnp.dot(normed_two, gate_up_full, preferred_element_type=jnp.float32)
        activated, pull_act = jax.vjp(swiglu_act, gate_up)
        activated = activated.astype(jnp.bfloat16)
        branch = jnp.dot(activated, down_full, preferred_element_type=jnp.float32)
        square_sums.append(jnp.sum(jnp.sum(branch * branch, axis=1) * valid_rows))
        stream = stream + branch
        stored.append(
            (
                qkv_full, out_full, gate_up_full, down_full, pull_one, normed_one, attended, pull_two, normed_two,
                pull_act, activated, moves, mixed,
                (projected, conv_weight[at], logits, dcol, drow, tinv, wu, step, state, reads),
            )
        )
    stream_grad = cotangent[0].astype(jnp.float32) * valid_rows[:, None]
    gain_list = []
    head_list = []
    filter_list = []
    beta_list = []
    weight_list = []
    for at in reversed(range(LAYERS)):
        (
            qkv_full, out_full, gate_up_full, down_full, pull_one, normed_one, attended, pull_two, normed_two,
            pull_act, activated, moves, mixed, kept,
        ) = stored[at]
        step, reads = kept[7], kept[9]
        branch_low = stream_grad.astype(jnp.bfloat16)
        grad_down = reduce_rows(activated, branch_low)
        (grad_gate_up,) = pull_act(contract_last(branch_low, down_full))
        grad_gate_up = grad_gate_up.astype(jnp.bfloat16)
        grad_gate = reduce_rows(normed_two, grad_gate_up)
        grad_state, gain_two = pull_two(contract_last(grad_gate_up, gate_up_full))
        stream_grad = stream_grad + grad_state
        branch_low = stream_grad.astype(jnp.bfloat16)
        grad_out = reduce_rows(attended, branch_low)
        grad_heads = contract_last(branch_low, out_full).astype(jnp.bfloat16)
        grad_mixed, gain_head, total = bwd_local(
            grad_heads, mixed, reads, head_gain[at][None], step, dcol, []
        )
        gives = [shifted(total, "seq", -d) for d in range(1, pieces)]
        grad_proj, *parts, grad_logits = bwd_main(place, False, moves, gives, *kept, grad_mixed, [])
        grad_logits = grad_logits[:, :H]
        rim = shifted(jnp.concatenate(parts[:3], axis=1), "seq", -1)
        grad_filter = jnp.concatenate(parts[3:6], axis=1)
        grad_proj = grad_proj.at[rows - HALO :].add(rim)
        grad_qkv = reduce_rows(normed_one, grad_proj)
        grad_beta = contract_first(normed_one, grad_logits)
        grad_normed = contract_last(grad_proj, qkv_full) + contract_last(grad_logits, beta_weight[at])
        grad_state, gain_one = pull_one(grad_normed)
        stream_grad = stream_grad + grad_state
        weight_list.append(
            [lax.psum(grad, "seq").astype(f32) for grad in (grad_qkv, grad_out, grad_gate, grad_down)]
        )
        gain_list.append(jnp.stack([gain_one, gain_two]))
        head_list.append(gain_head[0])
        filter_list.append(grad_filter)
        beta_list.append(grad_beta)
    stats_sum, valid_count, gains_sum, head_sum, filter_sum, beta_sum = lax.psum(
        (
            jnp.stack(square_sums),
            jnp.sum(valid_rows),
            jnp.stack(gain_list[::-1]),
            jnp.stack(head_list[::-1]),
            jnp.stack(filter_list[::-1]),
            jnp.stack(beta_list[::-1]),
        ),
        ("seq", "fsdp"),
    )
    rms_stats = jnp.sqrt(stats_sum / (jnp.maximum(valid_count, 1.0) * D)).reshape(LAYERS, 3)
    return (
        stream.astype(jnp.bfloat16)[None],
        stream_grad[None],
        gains_sum,
        head_sum,
        filter_sum,
        beta_sum,
        *[jnp.stack(pair[::-1]) for pair in zip(*weight_list)],
        rms_stats,
    )


def on_device_axes(
    tokens,
    segments,
    valid_mask,
    norm_gains,
    head_gain,
    conv_weight,
    beta_weight,
    qkv_weight,
    out_weight,
    gate_up_weight,
    down_weight,
    cotangent,
):
    rows = tokens.shape[1]
    dcol, drow = documents(segments[0], rows)
    place = jnp.stack([lax.axis_index("seq"), lax.axis_index("fsdp") % 2]).astype(jnp.int32)
    valid_rows = valid_mask[0].astype(f32)
    near = lambda array: (array, other(array, "fsdp", 1))
    size_qkv, size_out, size_gate = [weight.shape[2] // 4 for weight in (qkv_weight, out_weight, gate_up_weight)]
    sizes_one, sizes_two = (size_qkv, size_out), (size_gate,)
    groups = []
    for at in range(LAYERS):
        groups += [((qkv_weight, out_weight), at), ((gate_up_weight,), at)]
    packs = pack(place, groups[:1], [])
    packs += pack(place, groups[1:], packs)
    blocks, downs = [], []
    for at in range(LAYERS):
        blocks += [gather_chips(packed) for packed in packs[2 * at : 2 * at + 2]]
        downs.append(lax.all_gather(down_weight[at], "fsdp", axis=0, tiled=True))

    def launch(block, after):
        block = gate(block, after) if after else block
        return block, first_round(block)

    def finish(block, over, after):
        near_block = other(block, "fsdp", 1)
        passed, over = relay(*over, [near_block, *after])
        near_over = [other(piece, "fsdp", 1) for piece in over]
        return [block, *over], [near_block, *near_over], second_round(passed), passed

    def complete(came, after):
        own, near_own, passed, _ = came
        passed = [gate(piece, after) if after else piece for piece in passed]
        return [*own, *passed, *near_own, *[other(piece, "fsdp", 1) for piece in passed]]

    stream = tokens[0].astype(f32)
    tail = shifted(tokens[0, rows - HALO :], "seq", 1).astype(f32)
    valid = valid_rows[:, None]
    betas = jnp.pad(beta_weight, ((0, 0), (0, 0), (0, HD - H)))
    gains = lambda at, which: norm_gains[at, which][None]
    square_sums = [jnp.sum(stream * stream * valid, axis=0)[None]]
    normed = root_norm(stream, gains(0, 0)).astype(bf16)
    ready = [tail, betas, normed, dcol, drow, valid, stream, *square_sums]
    parts_one = complete(finish(*launch(blocks[0], []), ready), [])
    coming = launch(blocks[1], parts_one[-2:])
    stored = []
    for at in range(LAYERS):
        normed_one = near(normed)
        qkv_full, out_full = spread(place, parts_one, sizes_one, [])
        projected, logits = project(tail, gains(at, 0), normed, qkv_full, betas[at], [])
        qn, kn, tinv, wu, step, pre, total = fwd_local(
            projected, conv_weight[at], logits, dcol, drow, normed_one[1:]
        )
        partner = other(total, "seq", 1)
        reads, local_out = fwd_read(qn, kn, wu, dcol, drow)
        pair = pair_state(pair_forward_kernel, place, total, partner)
        far = other(pair, "seq", 2)
        came = finish(*coming, [far, reads])
        state, mixed, attended = fwd_state(
            place, True, [partner], far, pre, reads, local_out, head_gain[at][None], [*came[1], *came[3]]
        )
        parts_two = complete(came, [attended])
        attended = near(attended)
        after_mix, normed, sums = branch(attended[0], out_full, stream, valid, gains(at, 1), False, [], 1)
        normed_two = near(normed)
        (gate_up_full,) = spread(place, parts_two, sizes_two, [*attended, normed])
        more = at + 1 < LAYERS
        if more:
            coming = launch(blocks[2 * at + 2], parts_two[3:5])
        activated, both = gated(normed, gate_up_full, [], 2)
        passed = []
        if more:
            came = finish(*coming, [activated, *normed_two])
            passed = came[3]
        new_stream, normed, more_sums = branch(
            activated, downs[at], after_mix, valid, gains((at + 1) % LAYERS, 0), not more, passed, 2
        )
        if more:
            parts_one = complete(came, [new_stream])
            tail = shifted(new_stream[rows - HALO :], "seq", 1)
            coming = launch(blocks[2 * at + 3], [*parts_one[-2:], tail])
        square_sums += [sums[:1], more_sums[:1], more_sums[1:]]
        stored.append(
            (
                qkv_full, out_full, gate_up_full, downs[at], stream, normed_one, attended, after_mix,
                normed_two, both, activated, (total, partner), mixed,
                (projected, conv_weight[at], logits, dcol, drow, tinv, wu, step, state, reads),
            )
        )
        stream = new_stream
    result = normed
    g = cotangent[0].astype(f32) * valid
    g_low = g.astype(bf16)
    small = []
    waiting = []
    downs = []
    result_qkv, result_out, result_gate = [], [], []
    for at in reversed(range(LAYERS)):
        (
            qkv_full, out_full, gate_up_full, down_full, stream, normed_one, attended, after_mix,
            normed_two, both, activated, states, mixed, kept,
        ) = stored[at]
        step, reads = kept[7], kept[9]
        started = []
        last_low = g_low
        if waiting:
            grad_down = contract_first(gate(activated, [scattered, waiting[0]]), g_low).astype(bf16)
            own, over_x, over_y, diag_a, diag_b = waiting
            over_x, over_y = merge(over_x, over_y, diag_a, diag_b, [grad_down])
            above = (own, other(over_x, "seq", 1), other(over_y, "seq", 2))
            block, over = gather_start(scattered, [over_x])
            started = [block]
        grad_gate_up = gated_back(g_low, down_full, both, [over_x, downs[-1]] if waiting else [], 2)
        grad_gate_up = near(grad_gate_up)
        g, g_low, gain_two = norm_back(
            grad_gate_up[0], gate_up_full, (), after_mix, g, gains(at, 1), started
        )
        branch_low = near(g_low)
        pairs_one = [(normed_two, grad_gate_up)]
        out_pair = (attended, branch_low)
        if waiting:
            pairs_one.append(out_pair)
        own, over_x, over_y, diag_a, diag_b = grad_pieces(place, pairs_one, [gain_two])
        diag_a, diag_b = other(diag_a, "seq", 1), other(diag_b, "seq", 2)
        done = [own]
        if waiting:
            reduced = total_of(*above, [own])
            above = scatter_chips(reduced)
            result_gate, passed = gather_settle(place, block, over, (size_gate,), at + 1, [], [own])
            done = [own, reduced, *passed]
        grad_heads = contract_last(branch_low[0], out_full).astype(bf16)
        grad_mixed, gain_head, total = bwd_local(
            grad_heads, mixed, reads, head_gain[at][None], step, dcol, done
        )
        partner = other(total, "seq", 1)
        if not waiting:
            grad_down = contract_first(gate(activated, [total]), last_low).astype(bf16)
        ordered = grad_down
        grad_down = lax.psum_scatter(grad_down, "fsdp", scatter_dimension=0, tiled=True)
        pair = pair_state(pair_backward_kernel, place, *states, total, partner, after=[ordered])
        gives = [partner, other(pair, "seq", 2)]
        over_x, over_y = merge(over_x, over_y, diag_a, diag_b, [gives[1], *result_gate])
        from_x, from_y = other(over_x, "seq", 1), other(over_y, "seq", 2)
        grad_proj, *parts, grad_logits = bwd_main(
            place, True, states[1:], gives, *kept, grad_mixed,
            [over_x, *branch_low[1:], *([above] if waiting else [])],
        )
        rim = shifted(jnp.concatenate(parts[:3], axis=1), "seq", -1)
        reduced = total_of(own, from_x, from_y, [grad_proj])
        scattered = scatter_chips(reduced)
        grad_proj = near(gate(grad_proj, [reduced]).at[rows - HALO :].add(rim))
        grad_beta = contract_first(grad_logits[:, :H], normed_one[0])
        grad_down = gate(grad_down, [reduced])
        grad_down = grad_down + other(grad_down, "seq", 1)
        g, g_low, gain_one = norm_back(
            grad_proj[0], qkv_full, (grad_logits, betas[at]), stream, g, gains(at, 0), [reduced]
        )
        pairs_two = [(normed_one, grad_proj)]
        started = [gain_one, grad_down]
        if waiting:
            block, over = gather_start(above, [reduced])
            started += [block]
        else:
            pairs_two.append(out_pair)
        grad_down = gate(grad_down, [gain_one])
        taken = other(grad_down, "seq", 2)
        own, over_x, over_y, diag_a, diag_b = grad_pieces(place, pairs_two, started)
        if waiting:
            (result_qkv, result_out), passed = gather_settle(
                place, block, over, (size_qkv, size_out), at + 1, [], [own]
            )
        downs.append(grad_down + gate(taken, [own]))
        waiting = own, over_x, over_y, other(diag_a, "seq", 1), other(diag_b, "seq", 2)
        small += [gain_one, gain_two, gain_head, *parts[3:6], grad_beta]
    small += [*square_sums[: 3 * LAYERS], jnp.broadcast_to(jnp.sum(valid_rows), (1, D))]
    packed, starts = small_rows(small)
    own, over_x, over_y, diag_a, diag_b = waiting
    over_x, over_y = merge(over_x, over_y, diag_a, diag_b, [packed, downs[-1], *passed])
    from_x, from_y = other(over_x, "seq", 1), other(over_y, "seq", 2)
    packed = sum_over(gate(packed, [over_x]), "fsdp")
    reduced = total_of(own, from_x, from_y, [packed, result_out])
    last = scatter_chips(reduced)
    packed = sum_over(gate(packed, [reduced]), "seq")
    block, over = gather_start(scattered, [reduced])
    (result_gate, result_out), _ = gather_settle(
        place, block, over, (size_gate, size_out), 0, [*result_gate, result_out], []
    )
    block, over = gather_start(last, [packed, result_gate])
    (result_qkv,), _ = gather_settle(place, block, over, (size_qkv,), 0, [result_qkv], [])
    summed = [small_part(packed, start, array.shape) for start, array in zip(starts, small)]
    of_layer = lambda at: summed[7 * (LAYERS - 1 - at) : 7 * (LAYERS - at)]
    by_layer = lambda pick: jnp.stack([pick(of_layer(at)) for at in range(LAYERS)])
    stats = jnp.concatenate(summed[7 * LAYERS : -1], axis=0)
    count = summed[-1][0, 0]
    rms_stats = jnp.sqrt(jnp.sum(stats, axis=1) / (jnp.maximum(count, 1.0) * D)).reshape(LAYERS, 3)
    return (
        result[None],
        g[None],
        by_layer(lambda arrays: jnp.concatenate(arrays[:2], axis=0)),
        by_layer(lambda arrays: arrays[2][0]),
        by_layer(lambda arrays: jnp.concatenate(arrays[3:6], axis=1)),
        by_layer(lambda arrays: arrays[6].T),
        result_qkv,
        result_out,
        result_gate,
        jnp.stack(downs[::-1]).astype(f32),
        rms_stats,
    )


def solution(mesh):
    axes = mesh.shape["seq"] == 4 and mesh.shape["fsdp"] == 8
    return jax.shard_map(
        on_device_axes if axes else on_device,
        mesh=mesh,
        in_specs=(
            P("fsdp", "seq", None),
            P("fsdp", None),
            P("fsdp", "seq"),
            P(),
            P(),
            P(),
            P(),
            P(None, "fsdp", None),
            P(None, "fsdp", None),
            P(None, "fsdp", None),
            P(None, "fsdp", None),
            P("fsdp", "seq", None),
        ),
        out_specs=(
            P("fsdp", "seq", None),
            P("fsdp", "seq", None),
            P(),
            P(),
            P(),
            P(),
            P(None, "fsdp", None),
            P(None, "fsdp", None),
            P(None, "fsdp", None),
            P(None, "fsdp", None),
            P(),
        ),
        check_vma=False,
    )
```

time: 1560 us -> 891 us (0.57)
  waiting for transfers between devices: 955 us -> 252 us
  Pallas kernels: 207 us -> 429 us
  matrix products: 211 us -> 22.6 us
  starting transfers between devices: 42.4 us -> 87.3 us
  blocking collectives: 38.1 us -> 0 us
    reduce_scatter x8 -> x6, waiting for transfers between devices: 396 us -> 5.18 us  [the longest x4 5.14 us: scatter_chips(): lax.psum_scatter(total, 'fsdp', scatter_dimension=0, axis_index_groups=co...]
    all_gather x8 -> x6, waiting for transfers between devices: 308 us -> 17.8 us  [the longest x4 17.8 us: gather_chips(): lax.all_gather(packed, 'fsdp', axis=0, axis_index_groups=core_groups(), t...]
    ppermute x0 -> x97, waiting for transfers between devices: none -> 226 us  [other(): lax.ppermute(block, axis, [(i, i ^ mask) for i in range(lax.axis_size(axi...]
    pallas_call x10 -> x84, Pallas kernels: 207 us -> 429 us  [the longest x4 52.8 us: grad_pieces(): pl.pallas_call(partial(grad_pieces_kernel, count=len(pairs)), grid_spec=p...]
    psum x2 -> x0, waiting for transfers between devices: 204 us -> none  [the longest x1 119 us: on_device(): lax.psum((jnp.stack(square_sums), jnp.sum(valid_rows), jnp.stack(gain_lis...]
    ppermute x0 -> x97, starting transfers between devices: none -> 75.6 us  [other(): lax.ppermute(block, axis, [(i, i ^ mask) for i in range(lax.axis_size(axi...]
    dot_general x10 -> x2, matrix products: 81.9 us -> 7.04 us  [contract_last(): lax.dot_general(left, right, (((1,), (1,)), ((), ())), preferred_element_...]
    dot_general x10 -> x0, matrix products: 66.3 us -> none  [the longest x2 22 us: on_device(): jnp.dot(normed_two, gate_up_full, preferred_element_type=jnp.float32)]
  transfers between devices with their start and end apart: 38 -> 113, of which waited for: 23 -> 52; matrix products, arithmetic and copies ran while one was open for 16% -> 6% of each run, Pallas kernels for 13% -> 43%
where the time goes in v2:
time: 891 us; the launch traced here: 890 us
  Pallas kernels  429 us (48%)
  waiting for transfers between devices  252 us (28%)
  starting transfers between devices  87.3 us (10%)
  local copies, waits for them, and re-layouts  54.8 us (6%)
  other arithmetic  28.9 us (3%)
  matrix products  22.6 us (3%)
  between operations  16 us (2%)
    ppermute x97, waiting for transfers between devices, other(): lax.ppermute(block, axis, [(i, i ^ mask) for i in range(lax.axis_size(axi...  226 us
    ppermute x97, starting transfers between devices, other(): lax.ppermute(block, axis, [(i, i ^ mask) for i in range(lax.axis_size(axi...  75.6 us
    pallas_call x4, Pallas kernels, grad_pieces(): pl.pallas_call(partial(grad_pieces_kernel, count=len(pairs)), grid_spec=p...  52.8 us
    pallas_call x4, Pallas kernels, norm_back(): pl.pallas_call(kernel, grid=(steps,), in_specs=[d_spec, pl.BlockSpec((D,...  51 us
    pallas_call x2, Pallas kernels, bwd_main(): pl.pallas_call(partial(bwd_main_kernel, len(moves), paired), grid=(H // T...  50.1 us
    unnamed x205, local copies, waits for them, and re-layouts  41.2 us
    pallas_call x2, Pallas kernels, gated(): pl.pallas_call(lambda *refs: act_kernel(*refs[:3], *refs[-2:]), grid=(ste...  36.6 us
    pallas_call x4, Pallas kernels, spread(): pl.pallas_call(partial(spread_kernel, sizes=sizes), in_specs=[SMEM] + [AN...  33.9 us
  transfers between devices with their start and end apart: 113, of which 52 were waited for; matrix products, arithmetic and copies ran while one was open for 6% of the time, Pallas kernels for 43%

profile of v2, /device:TPU:0, one launch (start us, length us, event | category | flops | bytes accessed | tf_op | source)
XLA Modules:
  0.0 890.4 jit_solution(3467695848956661427)
XLA Ops:
  23.3 17.7 %all-gather.9.cloned.1.call-done = bf16[512,1024]{1,0:T(8,128)(2,1)} async-done(((bf16[128,1024]{1,0:T(8,128)(2,1)}), bf16[512,1024]{1,0:T(8,128)(2,1)}) %all-gather.9.cloned.1.call-update) | async-done | bytes 1048592 | tf_op jit(solution)/shard_map/all_gather | solution.py:923
  51.8 14.3 %collective-permute-done.1.x_ref = bf16[512,1024]{1,0:T(8,128)(2,1)} collective-permute-done((bf16[512,1024]{1,0:T(8,128)(2,1)}, bf16[512,1024]{1,0:T(8,128)(2,1)}, u32[]{:S(2)}, u32[]{:S(2)}) %collective-permute-start.1) | collective-permute-done | bytes 1048608 | tf_op jit(solution)/shard_map/ppermute | solution.py:795
  72.6 10.6 %collective-permute-done.4 = bf16[256,1024]{1,0:T(8,128)(2,1)} collective-permute-done((bf16[256,1024]{1,0:T(8,128)(2,1)}, bf16[256,1024]{1,0:T(8,128)(2,1)}, u32[]{:S(2)}, u32[]{:S(2)}) %collective-permute-start.4) | collective-permute-done | bytes 524320 | tf_op jit(solution)/shard_map/ppermute | solution.py:795
  107.3 15.1 %delta_local.2 = (bf16[512,1024]{1,0:T(8,128)(2,1)}, bf16[512,1024]{1,0:T(8,128)(2,1)}, bf16[8,512,128]{2,1,0:T(8,128)(2,1)}, bf16[8,512,256]{2,1,0:T(8,128)(2,1...) custom-call(bf16[528,3072]{1,0:T(8,128)(2,1)} %get-tuple-element.187.q_ref.k_ref.v_ref.r, ...), custom_call_target="tpu_custom_call" | custom-call | bytes 53505000 | tf_op jit(solution)/shard_map/delta_local/pallas_call | solution.py:195
  123.4 13.3 %collective-permute-done.11.refs_2_.refs_0_ = bf16[8,128,256]{2,1,0:T(8,128)(2,1)S(1)} collective-permute-done((bf16[8,128,256]{2,1,0:T(8,128)(2,1)}, bf16[8,128,256]{2,1,0:T(8,128)(2,1)S(1)}, u32[]{:S(2)}, u32[]{:S(2)}) %collective-permute-start.11) | collective-permute-done | bytes 524320 | tf_op jit(solution)/shard_map/ppermute | solution.py:795
  190.6 24.1 %gated.2 = (bf16[512,2816]{1,0:T(8,128)(2,1)}, bf16[2,512,2816]{2,1,0:T(8,128)(2,1)}) custom-call(bf16[512,1024]{1,0:T(8,128)(2,1)} %get-tuple-element.203.refs_12_.refs_0_.refs_2_, bf16[1024,5632]{1,0:T(8,128)(2,1)} %bitcast.118, bf16[1024,5632]{1,0:T(8,128)(2,1)} %bitcast.119), custom_call_target="tpu_custom_call" | custom-call | bytes 33210000 | tf_op jit(solution)/shard_map/gated/pallas_call | solution.py:693
  261.7 15.2 %delta_local.3 = (bf16[512,1024]{1,0:T(8,128)(2,1)}, bf16[512,1024]{1,0:T(8,128)(2,1)}, bf16[8,512,128]{2,1,0:T(8,128)(2,1)}, bf16[8,512,256]{2,1,0:T(8,128)(2,1...) custom-call(bf16[528,3072]{1,0:T(8,128)(2,1)} %get-tuple-element.214.q_ref.k_ref.v_ref.r, ...), custom_call_target="tpu_custom_call" | custom-call | bytes 53505000 | tf_op jit(solution)/shard_map/delta_local/pallas_call | solution.py:195
  278.1 12.4 %collective-permute-done.35.refs_2_.refs_0_ = bf16[8,128,256]{2,1,0:T(8,128)(2,1)S(1)} collective-permute-done((bf16[8,128,256]{2,1,0:T(8,128)(2,1)}, bf16[8,128,256]{2,1,0:T(8,128)(2,1)S(1)}, u32[]{:S(2)}, u32[]{:S(2)}) %collective-permute-start.35) | collective-permute-done | bytes 524320 | tf_op jit(solution)/shard_map/ppermute | solution.py:795
  341.8 12.5 %gated.3 = (bf16[512,2816]{1,0:T(8,128)(2,1)}, bf16[2,512,2816]{2,1,0:T(8,128)(2,1)}) custom-call(bf16[512,1024]{1,0:T(8,128)(2,1)} %get-tuple-element.230.refs_12_.refs_0_, bf16[1024,5632]{1,0:T(8,128)(2,1)} %bitcast.121, bf16[1024,5632]{1,0:T(8,128)(2,1)} %bitcast.122), custom_call_target="tpu_custom_call" | custom-call | bytes 33210000 | tf_op jit(solution)/shard_map/gated/pallas_call | solution.py:693
  354.3 10.2 %gated_back.2.refs_0_.refs_2_ = bf16[2,512,2816]{2,1,0:T(8,128)(2,1)} custom-call(bf16[512,1024]{1,0:T(8,128)(2,1)} %get-tuple-element.334.refs_0_, bf16[2816,1024]{1,0:T(8,128)(2,1)} %bitcast.130, bf16[2,512,2816]{2,1,0:T(8,128)(2,1)} %get-tuple-element.234.refs_2_), custom_call_target="tpu_custom_call" | custom-call | bytes 29520000 | tf_op jit(solution)/shard_map/gated_back/pallas_call | solution.py:723
  374.0 14.4 %norm_back.4 = (f32[512,1024]{1,0:T(8,128)}, bf16[512,1024]{1,0:T(8,128)(2,1)}, f32[1,1024]{1,0:T(1,128)}) custom-call(bf16[2,512,2816]{2,1,0:T(8,128)(2,1)} %gated_back.2.refs_0_.refs_2_, bf16[1024,5632]{1,0:T(8,128)(2,1)} %bitcast.123, f32[512,1024]{1,0:T(8,128)} %get-tuple-element.232.refs_2_, f32[512,1024]{1,0:T(8,128)} %get-tuple-element.333.refs_3_, ...), custom_call_target="tpu_custom_call" | custom-call | bytes 33210000 | tf_op jit(solution)/shard_map/norm_back/pallas_call | solution.py:778
  391.9 13.9 %grad_pieces.4 = (bf16[512,1408]{1,0:T(8,128)(2,1)}, bf16[512,1408]{1,0:T(8,128)(2,1)}, bf16[512,1408]{1,0:T(8,128)(2,1)}, bf16[256,1408]{1,0:T(8,128)(2,1)}, bf16[256,1408]{1,0:T(8,128)(2,1)}) custom-call(s32[2]{0:T(128)} %pad_add_fusion.place_ref.refs_0_, bf16[512,1024]{1,0:T(8,128)(2,1)} %get-tuple-element.230.refs_12_.refs_0_, ...), custom_call_target="tpu_custom_call" | custom-call | bytes 44280000 | tf_op jit(solution)/shard_map/grad_pieces/pallas_call | solution.py:992
  422.8 21.1 %collective-permute-done.49.refs_4_.refs_1_ = bf16[8,128,128]{2,1,0:T(8,128)(2,1)S(1)} collective-permute-done((bf16[8,128,128]{2,1,0:T(8,128)(2,1)S(1)}, bf16[8,128,128]{2,1,0:T(8,128)(2,1)S(1)}, u32[]{:S(2)}, u32[]{:S(2)}) %collective-permute-start.49) | collective-permute-done | bytes 262176 | tf_op jit(solution)/shard_map/ppermute | solution.py:795
  463.5 25.1 %delta_back.2 = (bf16[512,3072]{1,0:T(8,128)(2,1)}, bf16[16,1024]{1,0:T(8,128)(2,1)}, bf16[16,1024]{1,0:T(8,128)(2,1)}, bf16[16,1024]{1,0:T(8,128)(2,1)}, f32[4,...) custom-call(s32[2]{0:T(128)} %pad_add_fusion.place_ref.refs_0_, ...), custom_call_target="tpu_custom_call" | custom-call | bytes 88560000 | tf_op jit(solution)/shard_map/delta_back/pallas_call | solution.py:542
  501.4 11.3 %norm_back.5 = (f32[512,1024]{1,0:T(8,128)}, bf16[512,1024]{1,0:T(8,128)(2,1)}, f32[1,1024]{1,0:T(1,128)}) custom-call(bf16[512,3072]{1,0:T(8,128)(2,1)} %fusion.5.refs_0_.refs_4_, bf16[1024,3072]{1,0:T(8,128)(2,1)} %bitcast.127, bf16[512,128]{1,0:T(8,128)(2,1)} %get-tuple-element.254.refs_2_, bf16[1024,128]{1,0:T(8,128)(2,1)} %get-tuple-element.335.refs_4_.refs_3_, ...), custom_call_target="tpu_custom_call" | custom-call | bytes 33210000 | tf_op jit(solution)/shard_map/norm_back/pallas_call | solution.py:778
  523.6 12.1 %grad_pieces.5 = (bf16[512,1024]{1,0:T(8,128)(2,1)}, bf16[512,1024]{1,0:T(8,128)(2,1)}, bf16[512,1024]{1,0:T(8,128)(2,1)}, bf16[256,1024]{1,0:T(8,128)(2,1)}, bf16[256,1024]{1,0:T(8,128)(2,1)}) custom-call(s32[2]{0:T(128)} %pad_add_fusion.place_ref.refs_0_, bf16[512,1024]{1,0:T(8,128)(2,1)} %get-tuple-element.210.refs_2_.refs_0_, ...), custom_call_target="tpu_custom_call" | custom-call | bytes 44280000 | tf_op jit(solution)/shard_map/grad_pieces/pallas_call | solution.py:992
  550.8 14.1 %collective-permute-done.60.b_ref = bf16[256,1024]{1,0:T(8,128)(2,1)S(1)} collective-permute-done((bf16[256,1024]{1,0:T(8,128)(2,1)}, bf16[256,1024]{1,0:T(8,128)(2,1)S(1)}, u32[]{:S(2)}, u32[]{:S(2)}) %collective-permute-start.60) | collective-permute-done | bytes 524320 | tf_op jit(solution)/shard_map/ppermute | solution.py:795
  573.0 10.0 %gated_back.3.refs_0_.refs_4_ = bf16[2,512,2816]{2,1,0:T(8,128)(2,1)} custom-call(bf16[512,1024]{1,0:T(8,128)(2,1)} %get-tuple-element.256.refs_0_, bf16[2816,1024]{1,0:T(8,128)(2,1)} %bitcast.129, bf16[2,512,2816]{2,1,0:T(8,128)(2,1)} %get-tuple-element.257.refs_2_, bf16[512,1024]{1,0:T(8,128)(2,1)} %get-tuple-element.264.refs_3_.refs_1_, ...), custom_call_target="tpu_custom_call" | custom-call | bytes 29520000 | tf_op jit(solution)/shard_map/gated_back/pallas_call | solution.py:723
  583.0 14.4 %norm_back.6 = (f32[512,1024]{1,0:T(8,128)}, bf16[512,1024]{1,0:T(8,128)(2,1)}, f32[1,1024]{1,0:T(1,128)}) custom-call(bf16[2,512,2816]{2,1,0:T(8,128)(2,1)} %gated_back.3.refs_0_.refs_4_, bf16[1024,5632]{1,0:T(8,128)(2,1)} %bitcast.120, f32[512,1024]{1,0:T(8,128)} %get-tuple-element.205.refs_2_, f32[512,1024]{1,0:T(8,128)} %get-tuple-element.265.refs_3_, ...), custom_call_target="tpu_custom_call" | custom-call | bytes 33210000 | tf_op jit(solution)/shard_map/norm_back/pallas_call | solution.py:778
  601.3 17.3 %grad_pieces.6 = (bf16[512,1664]{1,0:T(8,128)(2,1)}, bf16[512,1664]{1,0:T(8,128)(2,1)}, bf16[512,1664]{1,0:T(8,128)(2,1)}, bf16[256,1664]{1,0:T(8,128)(2,1)}, bf16[256,1664]{1,0:T(8,128)(2,1)}) custom-call(s32[2]{0:T(128)} %pad_add_fusion.place_ref.refs_0_, bf16[512,1024]{1,0:T(8,128)(2,1)} %get-tuple-element.203.refs_12_.refs_0_.refs_2_, ...), custom_call_target="tpu_custom_call" | custom-call | bytes 44280000 | tf_op jit(solution)/shard_map/grad_pieces/pallas_call | solution.py:992
  650.0 11.6 %collective-permute-done.68.refs_4_.refs_1_ = bf16[8,128,128]{2,1,0:T(8,128)(2,1)S(1)} collective-permute-done((bf16[8,128,128]{2,1,0:T(8,128)(2,1)}, bf16[8,128,128]{2,1,0:T(8,128)(2,1)S(1)}, u32[]{:S(2)}, u32[]{:S(2)}) %collective-permute-start.68) | collective-permute-done | bytes 262176 | tf_op jit(solution)/shard_map/ppermute | solution.py:795
  686.5 25.0 %delta_back.3 = (bf16[512,3072]{1,0:T(8,128)(2,1)}, bf16[16,1024]{1,0:T(8,128)(2,1)}, bf16[16,1024]{1,0:T(8,128)(2,1)}, bf16[16,1024]{1,0:T(8,128)(2,1)}, f32[4,...) custom-call(s32[2]{0:T(128)} %pad_add_fusion.place_ref.refs_0_, ...), custom_call_target="tpu_custom_call" | custom-call | bytes 88560000 | tf_op jit(solution)/shard_map/delta_back/pallas_call | solution.py:542
  731.7 11.1 %norm_back.7 = (f32[512,1024]{1,0:T(8,128)}, bf16[512,1024]{1,0:T(8,128)(2,1)}, f32[1,1024]{1,0:T(1,128)}) custom-call(bf16[512,3072]{1,0:T(8,128)(2,1)} %fusion.4.refs_0_.refs_2_, bf16[1024,3072]{1,0:T(8,128)(2,1)} %bitcast.125, bf16[512,128]{1,0:T(8,128)(2,1)} %get-tuple-element.290.refs_2_, bf16[1024,128]{1,0:T(8,128)(2,1)} %get-tuple-element.336.refs_4_.refs_3_, ...), custom_call_target="tpu_custom_call" | custom-call | bytes 33210000 | tf_op jit(solution)/shard_map/norm_back/pallas_call | solution.py:778
  774.6 12.2 %collective-permute-done.83.y_ref = bf16[128,1024]{1,0:T(8,128)(2,1)S(1)} collective-permute-done((bf16[128,1024]{1,0:T(8,128)(2,1)S(1)}, bf16[128,1024]{1,0:T(8,128)(2,1)S(1)}, u32[]{:S(2)}, u32[]{:S(2)}) %collective-permute-start.83) | collective-permute-done | bytes 262176 | tf_op jit(solution)/shard_map/ppermute | solution.py:795
  (561 shorter events, 515.5 us)
Async XLA Ops:
  10.2 75.8 %all-gather.11.cloned.1.call-start = ((), (), s32[]{:S(2)}) async-start(), calls=%async_computation.7 | async-start | bytes 1802240 | tf_op jit(solution)/shard_map/all_gather | solution.py:923
  13.4 159.0 %all-gather.13.cloned.1.call-start = ((), (), s32[]{:S(2)}) async-start(), calls=%async_computation.8 | async-start | bytes 1310720 | tf_op jit(solution)/shard_map/all_gather | solution.py:923
  14.1 205.9 %all-gather.17.cloned.1.call-start = ((), (), s32[]{:S(2)}) async-start(), calls=%async_computation.16 | async-start | bytes 6488064 | tf_op jit(solution)/shard_map/all_gather | solution.py:1325
  15.4 224.4 %all-gather.15.cloned.1.call-start = ((), (), s32[]{:S(2)}) async-start(), calls=%async_computation.9 | async-start | bytes 1802240 | tf_op jit(solution)/shard_map/all_gather | solution.py:923
  20.4 333.9 %all-gather.19.cloned.1.call-start = ((), (), s32[]{:S(2)}) async-start(), calls=%async_computation.17 | async-start | bytes 6488064 | tf_op jit(solution)/shard_map/all_gather | solution.py:1325
  84.5 416.1 %reduce-scatter.7.cloned.1.call-start = ((), (), s32[]{:S(2)}) async-start(), calls=%async_computation.10 | async-start | bytes 6488064 | tf_op jit(solution)/shard_map/reduce_scatter | solution.py:1445
  86.9 60.6 %collective-permute-start.13 = (bf16[512,1408]{1,0:T(8,128)(2,1)}, bf16[512,1408]{1,0:T(8,128)(2,1)S(1)}, u32[]{:S(2)}, u32[]{:S(2)}) collective-permute-start(bf16[512,1408]{1,0:T(8,128)(2,1)} %gate.25), channel_id=1, source_target_pairs={{0,1},{1,0},{2,3},{3,2},{4,5},{5,4},{6,7},{7,6},{8,9},{9,8},{10,11... | collective-permute-start | bytes 4325384 | tf_op jit(solution)/shard_map/ppermute | solution.py:795
  87.3 60.2 %collective-permute-start.14 = (bf16[512,1408]{1,0:T(8,128)(2,1)}, bf16[512,1408]{1,0:T(8,128)(2,1)}, u32[]{:S(2)}, u32[]{:S(2)}) collective-permute-start(bf16[512,1408]{1,0:T(8,128)(2,1)} %gate.25), channel_id=1, source_target_pairs={{0,8},{8,0},{16,24},{24,16},{1,9},{9,1},{17,25},{25,17},{2,10},{10... | collective-permute-start | bytes 4325384 | tf_op jit(solution)/shard_map/ppermute | solution.py:795
  87.9 59.6 %collective-permute-start.15 = (bf16[512,1408]{1,0:T(8,128)(2,1)}, bf16[512,1408]{1,0:T(8,128)(2,1)}, u32[]{:S(2)}, u32[]{:S(2)}) collective-permute-start(bf16[512,1408]{1,0:T(8,128)(2,1)} %gate.25), channel_id=1, source_target_pairs={{0,16},{8,24},{16,0},{24,8},{1,17},{9,25},{17,1},{25,9},{2,18},{10... | collective-permute-start | bytes 4325384 | tf_op jit(solution)/shard_map/ppermute | solution.py:795
  172.4 42.3 %collective-permute-start.23 = (bf16[512,1024]{1,0:T(8,128)(2,1)}, bf16[512,1024]{1,0:T(8,128)(2,1)}, u32[]{:S(2)}, u32[]{:S(2)}) collective-permute-start(bf16[512,1024]{1,0:T(8,128)(2,1)} %gate.28), channel_id=1, source_target_pairs={{0,8},{8,0},{16,24},{24,16},{1,9},{9,1},{17,25},{25,17},{2,10},{10... | collective-permute-start | bytes 3145736 | tf_op jit(solution)/shard_map/ppermute | solution.py:795
  172.7 42.0 %collective-permute-start.24 = (bf16[512,1024]{1,0:T(8,128)(2,1)}, bf16[512,1024]{1,0:T(8,128)(2,1)}, u32[]{:S(2)}, u32[]{:S(2)}) collective-permute-start(bf16[512,1024]{1,0:T(8,128)(2,1)} %gate.28), channel_id=1, source_target_pairs={{0,16},{8,24},{16,0},{24,8},{1,17},{9,25},{17,1},{25,9},{2,18},{10... | collective-permute-start | bytes 3145736 | tf_op jit(solution)/shard_map/ppermute | solution.py:795
  241.5 59.0 %collective-permute-start.37 = (bf16[512,1408]{1,0:T(8,128)(2,1)}, bf16[512,1408]{1,0:T(8,128)(2,1)S(1)}, u32[]{:S(2)}, u32[]{:S(2)}) collective-permute-start(bf16[512,1408]{1,0:T(8,128)(2,1)} %gate.31), channel_id=1, source_target_pairs={{0,1},{1,0},{2,3},{3,2},{4,5},{5,4},{6,7},{7,6},{8,9},{9,8},{10,11... | collective-permute-start | bytes 4325384 | tf_op jit(solution)/shard_map/ppermute | solution.py:795
  242.0 58.5 %collective-permute-start.38 = (bf16[512,1408]{1,0:T(8,128)(2,1)}, bf16[512,1408]{1,0:T(8,128)(2,1)S(1)}, u32[]{:S(2)}, u32[]{:S(2)}) collective-permute-start(bf16[512,1408]{1,0:T(8,128)(2,1)} %gate.31), channel_id=1, source_target_pairs={{0,8},{8,0},{16,24},{24,16},{1,9},{9,1},{17,25},{25,17},{2,10},{10... | collective-permute-start | bytes 4325384 | tf_op jit(solution)/shard_map/ppermute | solution.py:795
  244.3 56.2 %collective-permute-start.39 = (bf16[512,1408]{1,0:T(8,128)(2,1)}, bf16[512,1408]{1,0:T(8,128)(2,1)}, u32[]{:S(2)}, u32[]{:S(2)}) collective-permute-start(bf16[512,1408]{1,0:T(8,128)(2,1)} %gate.31), channel_id=1, source_target_pairs={{0,16},{8,24},{16,0},{24,8},{1,17},{9,25},{17,1},{25,9},{2,18},{10... | collective-permute-start | bytes 4325384 | tf_op jit(solution)/shard_map/ppermute | solution.py:795
  419.5 119.0 %reduce-scatter.9.cloned.1.call-start = ((), (), s32[]{:S(2)}) async-start(), calls=%async_computation.11 | async-start | bytes 1802240 | tf_op jit(solution)/shard_map/reduce_scatter | solution.py:927
  419.5 35.7 %collective-permute-start.51 = (bf16[256,1408]{1,0:T(8,128)(2,1)}, bf16[256,1408]{1,0:T(8,128)(2,1)S(1)}, u32[]{:S(2)}, u32[]{:S(2)}) collective-permute-start(bf16[256,1408]{1,0:T(8,128)(2,1)} %get-tuple-element.246), channel_id=1, source_target_pairs={{0,8},{8,0},{16,24},{24,16},{1,9},{9,1},{17,25},{25,17},{2,10},{10... | collective-permute-start | bytes 2162696 | tf_op jit(solution)/shard_map/ppermute | solution.py:795
  500.5 186.1 %reduce-scatter.11.cloned.1.call-start = ((), (), s32[]{:S(2)}) async-start(), calls=%async_computation.12 | async-start | bytes 1310720 | tf_op jit(solution)/shard_map/reduce_scatter | solution.py:927
  627.4 101.8 %reduce-scatter.13.cloned.1.call-start = ((), (), s32[]{:S(2)}) async-start(), calls=%async_computation.13 | async-start | bytes 6488064 | tf_op jit(solution)/shard_map/reduce_scatter | solution.py:1445
  628.0 202.0 %reduce-scatter.17.cloned.1.call-start = ((), (), s32[]{:S(2)}) async-start(), calls=%async_computation.15 | async-start | bytes 2129920 | tf_op jit(solution)/shard_map/reduce_scatter | solution.py:927
  631.3 47.4 %collective-permute-start.70 = (bf16[256,1664]{1,0:T(8,128)(2,1)}, bf16[256,1664]{1,0:T(8,128)(2,1)}, u32[]{:S(2)}, u32[]{:S(2)}) collective-permute-start(bf16[256,1664]{1,0:T(8,128)(2,1)} %get-tuple-element.280), channel_id=1, source_target_pairs={{0,8},{8,0},{16,24},{24,16},{1,9},{9,1},{17,25},{25,17},{2,10},{10... | collective-permute-start | bytes 2555912 | tf_op jit(solution)/shard_map/ppermute | solution.py:795
  632.1 46.7 %collective-permute-start.71 = (bf16[256,1664]{1,0:T(8,128)(2,1)}, bf16[256,1664]{1,0:T(8,128)(2,1)}, u32[]{:S(2)}, u32[]{:S(2)}) collective-permute-start(bf16[256,1664]{1,0:T(8,128)(2,1)} %get-tuple-element.281), channel_id=1, source_target_pairs={{0,16},{8,24},{16,0},{24,8},{1,17},{9,25},{17,1},{25,9},{2,18},{10... | collective-permute-start | bytes 2555912 | tf_op jit(solution)/shard_map/ppermute | solution.py:795
  683.6 37.5 %collective-permute-start.74 = (bf16[512,1664]{1,0:T(8,128)(2,1)}, bf16[512,1664]{1,0:T(8,128)(2,1)S(1)}, u32[]{:S(2)}, u32[]{:S(2)}) collective-permute-start(bf16[512,1664]{1,0:T(8,128)(2,1)} %get-tuple-element.284.refs_18_), channel_id=1, source_target_pairs={{0,8},{8,0},{16,24},{24,16},{1,9},{9,1},{17,25},{25,17},{2,10},{10... | collective-permute-start | bytes 5111816 | tf_op jit(solution)/shard_map/ppermute | solution.py:795
  684.9 36.2 %collective-permute-start.75 = (bf16[512,1664]{1,0:T(8,128)(2,1)}, bf16[512,1664]{1,0:T(8,128)(2,1)S(1)}, u32[]{:S(2)}, u32[]{:S(2)}) collective-permute-start(bf16[512,1664]{1,0:T(8,128)(2,1)} %get-tuple-element.286), channel_id=1, source_target_pairs={{0,16},{8,24},{16,0},{24,8},{1,17},{9,25},{17,1},{25,9},{2,18},{10... | collective-permute-start | bytes 5111816 | tf_op jit(solution)/shard_map/ppermute | solution.py:795
  729.2 135.0 %reduce-scatter.15.cloned.1.call-start = ((), (), s32[]{:S(2)}) async-start(), calls=%async_computation.14 | async-start | bytes 983040 | tf_op jit(solution)/shard_map/reduce_scatter | solution.py:927
  (191 other events, 1875.1 us)
Sparse Core Ops, SparseCore 0:
  10.4 30.6 all-gather.8
  42.6 34.4 all-gather.10
  78.6 26.7 all-gather.12
  107.0 59.9 all-gather.16
  168.3 33.6 all-gather.14
  203.5 59.2 all-gather.18
  419.6 64.4 reduce-scatter.6
  500.6 32.9 reduce-scatter.8
  627.5 27.1 reduce-scatter.10
  657.0 63.5 reduce-scatter.12
  729.3 37.3 reduce-scatter.16
  842.2 21.9 reduce-scatter.14

commit v3 on v2

--- a/solution.py
+++ b/solution.py
@@ -596,41 +596,6 @@
     )(place, *arrays, *after)
 
 
-def project_kernel(tail_ref, gain_ref, normed_ref, weight_ref, beta_ref, out_ref, logits_ref, low_tail):
-    @pl.when(pl.program_id(0) == 0)
-    def _():
-        tail = tail_ref[...]
-        scale = lax.rsqrt(jnp.mean(tail * tail, axis=-1, keepdims=True) + EPS_NORM)
-        low_tail[...] = (tail * scale * gain_ref[...]).astype(bf16)
-        logits_ref[...] = dot_nn(normed_ref[...], beta_ref[...]).astype(bf16)
-
-    out_ref[pl.ds(0, HALO), :] = dot_nn(low_tail[...], weight_ref[...]).astype(bf16)
-    out_ref[pl.ds(HALO, normed_ref.shape[0]), :] = dot_nn(normed_ref[...], weight_ref[...]).astype(bf16)
-
-
-def project(tail, gain, normed, weight, beta, after, steps=4):
-    rows, width = normed.shape[0], weight.shape[1]
-    sds = jax.ShapeDtypeStruct
-    return pl.pallas_call(
-        lambda *refs: project_kernel(*refs[:5], *refs[-3:]),
-        grid=(steps,),
-        in_specs=[
-            full_spec(tail.shape),
-            full_spec((1, D)),
-            full_spec(normed.shape),
-            pl.BlockSpec((D, width // steps), lambda j: (0, j)),
-            full_spec(beta.shape),
-        ]
-        + [pl.BlockSpec(memory_space=pl.ANY) for _ in after],
-        out_specs=[pl.BlockSpec((rows + HALO, width // steps), lambda j: (0, j)), full_spec((rows, beta.shape[1]))],
-        out_shape=[sds((rows + HALO, width), bf16), sds((rows, beta.shape[1]), bf16)],
-        scratch_shapes=[pltpu.VMEM((HALO, D), bf16)],
-        compiler_params=params(),
-        cost_estimate=cost(5, rows),
-        name="project",
-    )(tail, gain, normed, weight, beta, *after)
-
-
 def branch_kernel(x_ref, weight_ref, stream_ref, valid_ref, gain_ref, out_ref, normed_ref, sums_ref, total, *, last):
     step = pl.program_id(0)
 
@@ -678,35 +643,6 @@
     )(x, weight, stream, valid, gain, *after)
 
 
-def act_kernel(x_ref, gate_ref, up_ref, act_ref, both_ref):
-    gate = dot_nn(x_ref[...], gate_ref[...])
-    up = dot_nn(x_ref[...], up_ref[...])
-    act_ref[...] = (gate * sigmoid(gate) * up).astype(bf16)
-    both_ref[0] = gate.astype(bf16)
-    both_ref[1] = up.astype(bf16)
-
-
-def gated(x, weight, after, steps=11):
-    rows, half = x.shape[0], weight.shape[1] // 2
-    size = half // steps
-    sds = jax.ShapeDtypeStruct
-    return pl.pallas_call(
-        lambda *refs: act_kernel(*refs[:3], *refs[-2:]),
-        grid=(steps,),
-        in_specs=[
-            full_spec(x.shape),
-            pl.BlockSpec((D, size), lambda j: (0, j)),
-            pl.BlockSpec((D, size), lambda j: (0, steps + j)),
-        ]
-        + [pl.BlockSpec(memory_space=pl.ANY) for _ in after],
-        out_specs=[pl.BlockSpec((rows, size), lambda j: (0, j)), pl.BlockSpec((2, rows, size), lambda j: (0, 0, j))],
-        out_shape=[sds((rows, half), bf16), sds((2, rows, half), bf16)],
-        compiler_params=params(),
-        cost_estimate=cost(9, rows),
-        name="gated",
-    )(x, weight, weight, *after)
-
-
 def act_back_kernel(g_ref, down_ref, both_ref, out_ref):
     dact = dot_nt(g_ref[...], down_ref[...])
     gate, up = both_ref[0].astype(f32), both_ref[1].astype(f32)
@@ -850,33 +786,138 @@
     )(place, *weights, *after)
 
 
-def spread_kernel(place_ref, *refs, sizes):
-    pieces, outs, sems = refs[:10], refs[-len(sizes) - 1 : -1], refs[-1]
+def arrivals(place_ref, pieces, weights, sizes, sems):
     seq, core = place_ref[0], place_ref[1]
-    chips = outs[0].shape[0]
-    pairs = []
+    chips = weights[0].shape[0]
+    copies = {0: [], 1: [], 2: [], 3: []}
+    at = 0
     for own, (h, x, y, a, b) in ((core, pieces[:5]), (1 - core, pieces[5:])):
-        for piece, mask, at in ((h, 0, 0), (x, 1, 0), (y, 2, 0), (a, 3, 0), (b, 3, chips // 2)):
-            here = pl.ds(at, piece.shape[0])
-            for out_ref, start, size in zip(outs, offsets(sizes), sizes):
-                pairs.append((piece.at[:, :, pl.ds(start, size)], out_ref.at[here, own, :, aligned(seq ^ mask, size)]))
-    run_copies(pairs, sems)
-
-
-def spread(place, pieces, sizes, after):
+        for piece, mask, row in ((h, 0, 0), (x, 1, 0), (y, 2, 0), (a, 3, 0), (b, 3, chips // 2)):
+            here = pl.ds(row, piece.shape[0])
+            for weight, start, size in zip(weights, offsets(sizes), sizes):
+                copies[mask].append(
+                    pltpu.make_async_copy(
+                        piece.at[:, :, pl.ds(start, size)], weight.at[here, own, :, aligned(seq ^ mask, size)], sems.at[at]
+                    )
+                )
+                at += 1
+    return copies
+
+
+def columns_of(weight, quarter, size):
+    block = weight[:, :, :, aligned(quarter, size)]
+    return block.reshape(-1, size)
+
+
+def project_kernel(place_ref, tail_ref, gain_ref, normed_ref, beta_ref, *refs, sizes):
+    pieces, (out_ref, logits_ref, *full_refs) = refs[:10], refs[-9:-5]
+    weight, more, low_tail, sems_in, sems_out = refs[-5:]
+    copies = arrivals(place_ref, pieces, (weight, more), sizes, sems_in)
+    for mask in (0, 1, 2, 3):
+        for copy in copies[mask]:
+            copy.start()
+    tail = tail_ref[...]
+    scale = lax.rsqrt(jnp.mean(tail * tail, axis=-1, keepdims=True) + EPS_NORM)
+    low_tail[...] = (tail * scale * gain_ref[...]).astype(bf16)
+    logits_ref[...] = dot_nn(normed_ref[...], beta_ref[...]).astype(bf16)
+    sent = []
+    for mask in (0, 1, 2, 3):
+        for copy in copies[mask]:
+            copy.wait()
+        quarter = place_ref[0] ^ mask
+        columns = aligned(quarter, sizes[0])
+        sent.append(
+            pltpu.make_async_copy(
+                weight.at[:, :, :, columns], full_refs[0].at[:, :, :, columns], sems_out.at[mask]
+            )
+        )
+        sent[-1].start()
+        block = columns_of(weight, quarter, sizes[0])
+        out_ref[pl.ds(0, HALO), columns] = dot_nn(low_tail[...], block).astype(bf16)
+        out_ref[pl.ds(HALO, normed_ref.shape[0]), columns] = dot_nn(normed_ref[...], block).astype(bf16)
+    sent.append(pltpu.make_async_copy(more, full_refs[1], sems_out.at[4]))
+    sent[-1].start()
+    for copy in sent:
+        copy.wait()
+
+
+def project(place, tail, gain, normed, beta, pieces, sizes, after):
+    rows = normed.shape[0]
     chips = pieces[0].shape[0] // 128
     pieces = [piece.reshape(-1, 128, piece.shape[1]) for piece in pieces]
-    weights = pl.pallas_call(
-        partial(spread_kernel, sizes=sizes),
-        in_specs=[SMEM] + [ANY] * (len(pieces) + len(after)),
-        out_specs=[VMEM] * len(sizes),
-        out_shape=[jax.ShapeDtypeStruct((chips, 2, 128, size * 4), bf16) for size in sizes],
-        scratch_shapes=[pltpu.SemaphoreType.DMA((len(pieces) * len(sizes),))],
+    sds = jax.ShapeDtypeStruct
+    shapes = [(chips, 2, 128, 4 * size) for size in sizes]
+    out, logits, first, second = pl.pallas_call(
+        partial(project_kernel, sizes=sizes),
+        in_specs=[SMEM] + [VMEM] * 4 + [ANY] * (len(pieces) + len(after)),
+        out_specs=[VMEM, VMEM, ANY, ANY],
+        out_shape=[sds((rows + HALO, 4 * sizes[0]), bf16), sds((rows, beta.shape[1]), bf16)]
+        + [sds(shape, bf16) for shape in shapes],
+        scratch_shapes=[pltpu.VMEM(shape, bf16) for shape in shapes]
+        + [pltpu.VMEM((HALO, D), bf16), pltpu.SemaphoreType.DMA((20,)), pltpu.SemaphoreType.DMA((5,))],
         compiler_params=pltpu.CompilerParams(vmem_limit_bytes=VMEM_LIMIT),
-        cost_estimate=cost(7, 512),
-        name="spread_weights",
-    )(place, *pieces, *after)
-    return [weight.reshape(-1, weight.shape[3]) for weight in weights]
+        cost_estimate=cost(10, rows),
+        name="project",
+    )(place, tail, gain, normed, beta, *pieces, *after)
+    return out, logits, first.reshape(D, -1), second.reshape(D, -1)
+
+
+def gated_kernel(place_ref, x_ref, *refs, size):
+    pieces, (act_ref, both_ref, full_ref) = refs[:10], refs[-9:-6]
+    weight, act, both, sems_in, sems_out, sems_act = refs[-6:]
+    copies = arrivals(place_ref, pieces, (weight,), (size,), sems_in)
+    order = (0, 2, 1, 3)
+    for mask in order:
+        for copy in copies[mask]:
+            copy.start()
+    sent = []
+    for turn in (0, 1):
+        for mask in order[2 * turn : 2 * turn + 2]:
+            for copy in copies[mask]:
+                copy.wait()
+            columns = aligned(place_ref[0] ^ mask, size)
+            sent.append(
+                pltpu.make_async_copy(weight.at[:, :, :, columns], full_ref.at[:, :, :, columns], sems_out.at[mask])
+            )
+            sent[-1].start()
+        half = lax.rem(place_ref[0] ^ turn, 2)
+        gate_block = dot_nn(x_ref[...], columns_of(weight, half, size))
+        up_block = dot_nn(x_ref[...], columns_of(weight, half + 2, size))
+        act[turn] = (gate_block * sigmoid(gate_block) * up_block).astype(bf16)
+        both[turn, 0] = gate_block.astype(bf16)
+        both[turn, 1] = up_block.astype(bf16)
+        columns = aligned(half, size)
+        sent.append(pltpu.make_async_copy(act.at[turn], act_ref.at[:, columns], sems_act.at[2 * turn]))
+        sent.append(pltpu.make_async_copy(both.at[turn], both_ref.at[:, :, columns], sems_act.at[2 * turn + 1]))
+        for copy in sent[-2:]:
+            copy.start()
+    for copy in sent:
+        copy.wait()
+
+
+def gated(place, x, pieces, size, after):
+    rows = x.shape[0]
+    chips = pieces[0].shape[0] // 128
+    pieces = [piece.reshape(-1, 128, piece.shape[1]) for piece in pieces]
+    sds = jax.ShapeDtypeStruct
+    act, both, full = pl.pallas_call(
+        partial(gated_kernel, size=size),
+        in_specs=[SMEM, VMEM] + [ANY] * (len(pieces) + len(after)),
+        out_specs=[ANY] * 3,
+        out_shape=[sds((rows, 2 * size), bf16), sds((2, rows, 2 * size), bf16), sds((chips, 2, 128, 4 * size), bf16)],
+        scratch_shapes=[
+            pltpu.VMEM((chips, 2, 128, 4 * size), bf16),
+            pltpu.VMEM((2, rows, size), bf16),
+            pltpu.VMEM((2, 2, rows, size), bf16),
+            pltpu.SemaphoreType.DMA((10,)),
+            pltpu.SemaphoreType.DMA((4,)),
+            pltpu.SemaphoreType.DMA((4,)),
+        ],
+        compiler_params=pltpu.CompilerParams(vmem_limit_bytes=VMEM_LIMIT),
+        cost_estimate=cost(15, rows),
+        name="gated",
+    )(place, x, *pieces, *after)
+    return act, both, full.reshape(D, -1)
 
 
 def gate(array, after):
@@ -1352,16 +1393,17 @@
     stored = []
     for at in range(LAYERS):
         normed_one = near(normed)
-        qkv_full, out_full = spread(place, parts_one, sizes_one, [])
-        projected, logits = project(tail, gains(at, 0), normed, qkv_full, betas[at], [])
+        projected, logits, qkv_full, out_full = project(
+            place, tail, gains(at, 0), normed, betas[at], parts_one, sizes_one, []
+        )
         qn, kn, tinv, wu, step, pre, total = fwd_local(
             projected, conv_weight[at], logits, dcol, drow, normed_one[1:]
         )
         partner = other(total, "seq", 1)
         reads, local_out = fwd_read(qn, kn, wu, dcol, drow)
-        pair = pair_state(pair_forward_kernel, place, total, partner)
+        pair = pair_state(pair_forward_kernel, place, total, partner, after=[reads])
         far = other(pair, "seq", 2)
-        came = finish(*coming, [far, reads])
+        came = finish(*coming, [far])
         state, mixed, attended = fwd_state(
             place, True, [partner], far, pre, reads, local_out, head_gain[at][None], [*came[1], *came[3]]
         )
@@ -1369,11 +1411,10 @@
         attended = near(attended)
         after_mix, normed, sums = branch(attended[0], out_full, stream, valid, gains(at, 1), False, [], 1)
         normed_two = near(normed)
-        (gate_up_full,) = spread(place, parts_two, sizes_two, [*attended, normed])
         more = at + 1 < LAYERS
         if more:
             coming = launch(blocks[2 * at + 2], parts_two[3:5])
-        activated, both = gated(normed, gate_up_full, [], 2)
+        activated, both, gate_up_full = gated(place, normed, parts_two, size_gate, attended[1:])
         passed = []
         if more:
             came = finish(*coming, [activated, *normed_two])
@@ -1390,7 +1431,7 @@
             (
                 qkv_full, out_full, gate_up_full, downs[at], stream, normed_one, attended, after_mix,
                 normed_two, both, activated, (total, partner), mixed,
-                (projected, conv_weight[at], logits, dcol, drow, tinv, wu, step, state, reads),
+                new_stream, (projected, conv_weight[at], logits, dcol, drow, tinv, wu, step, state, reads),
             )
         )
         stream = new_stream
@@ -1399,16 +1440,14 @@
     g_low = g.astype(bf16)
     small = []
     waiting = []
-    downs = []
     result_qkv, result_out, result_gate = [], [], []
     for at in reversed(range(LAYERS)):
         (
             qkv_full, out_full, gate_up_full, down_full, stream, normed_one, attended, after_mix,
-            normed_two, both, activated, states, mixed, kept,
+            normed_two, both, activated, states, mixed, leaving, kept,
         ) = stored[at]
         step, reads = kept[7], kept[9]
         started = []
-        last_low = g_low
         if waiting:
             grad_down = contract_first(gate(activated, [scattered, waiting[0]]), g_low).astype(bf16)
             own, over_x, over_y, diag_a, diag_b = waiting
@@ -1416,7 +1455,10 @@
             above = (own, other(over_x, "seq", 1), other(over_y, "seq", 2))
             block, over = gather_start(scattered, [over_x])
             started = [block]
-        grad_gate_up = gated_back(g_low, down_full, both, [over_x, downs[-1]] if waiting else [], 2)
+        else:
+            grad_down = contract_first(activated, g_low).astype(bf16)
+        grad_gate_up = gated_back(g_low, down_full, both, [over_x] if waiting else [grad_down], 2)
+        grad_down = lax.psum_scatter(grad_down, "fsdp", scatter_dimension=0, tiled=True)
         grad_gate_up = near(grad_gate_up)
         g, g_low, gain_two = norm_back(
             grad_gate_up[0], gate_up_full, (), after_mix, g, gains(at, 1), started
@@ -1424,67 +1466,70 @@
         branch_low = near(g_low)
         pairs_one = [(normed_two, grad_gate_up)]
         out_pair = (attended, branch_low)
+        ready = [gain_two]
         if waiting:
             pairs_one.append(out_pair)
-        own, over_x, over_y, diag_a, diag_b = grad_pieces(place, pairs_one, [gain_two])
+            reduced = total_of(*above, [gain_two])
+            above = scatter_chips(reduced)
+            ready += [reduced]
+        own, over_x, over_y, diag_a, diag_b = grad_pieces(place, pairs_one, ready)
         diag_a, diag_b = other(diag_a, "seq", 1), other(diag_b, "seq", 2)
         done = [own]
         if waiting:
-            reduced = total_of(*above, [own])
-            above = scatter_chips(reduced)
             result_gate, passed = gather_settle(place, block, over, (size_gate,), at + 1, [], [own])
-            done = [own, reduced, *passed]
+            done += passed
         grad_heads = contract_last(branch_low[0], out_full).astype(bf16)
         grad_mixed, gain_head, total = bwd_local(
             grad_heads, mixed, reads, head_gain[at][None], step, dcol, done
         )
         partner = other(total, "seq", 1)
-        if not waiting:
-            grad_down = contract_first(gate(activated, [total]), last_low).astype(bf16)
-        ordered = grad_down
-        grad_down = lax.psum_scatter(grad_down, "fsdp", scatter_dimension=0, tiled=True)
-        pair = pair_state(pair_backward_kernel, place, *states, total, partner, after=[ordered])
+        fillers = result_gate if waiting else [leaving]
+        pair = pair_state(pair_backward_kernel, place, *states, total, partner, after=fillers)
         gives = [partner, other(pair, "seq", 2)]
-        over_x, over_y = merge(over_x, over_y, diag_a, diag_b, [gives[1], *result_gate])
+        over_x, over_y = merge(over_x, over_y, diag_a, diag_b, [gives[1]])
         from_x, from_y = other(over_x, "seq", 1), other(over_y, "seq", 2)
         grad_proj, *parts, grad_logits = bwd_main(
             place, True, states[1:], gives, *kept, grad_mixed,
             [over_x, *branch_low[1:], *([above] if waiting else [])],
         )
         rim = shifted(jnp.concatenate(parts[:3], axis=1), "seq", -1)
-        reduced = total_of(own, from_x, from_y, [grad_proj])
+        reduced = total_of(own, from_x, from_y, [grad_proj, grad_down])
         scattered = scatter_chips(reduced)
         grad_proj = near(gate(grad_proj, [reduced]).at[rows - HALO :].add(rim))
         grad_beta = contract_first(grad_logits[:, :H], normed_one[0])
-        grad_down = gate(grad_down, [reduced])
-        grad_down = grad_down + other(grad_down, "seq", 1)
         g, g_low, gain_one = norm_back(
             grad_proj[0], qkv_full, (grad_logits, betas[at]), stream, g, gains(at, 0), [reduced]
         )
         pairs_two = [(normed_one, grad_proj)]
-        started = [gain_one, grad_down]
+        started = [gain_one]
+        small += [gain_one, gain_two, gain_head, *parts[3:6], grad_beta]
         if waiting:
+            grad_down = gate(grad_down, [reduced])
+            grad_down = grad_down + gate(other(grad_down, "seq", 1), [gain_one])
+            down_above = down_above + gate(other(gate(down_above, [reduced]), "seq", 2), [gain_one])
+            above_far = other(down_above, "seq", 1)
             block, over = gather_start(above, [reduced])
-            started += [block]
+            small += [*square_sums[: 3 * LAYERS], jnp.broadcast_to(jnp.sum(valid_rows), (1, D))]
+            packed, starts = small_rows(small)
+            started += [grad_down, down_above, packed]
+            packed_near = other(packed, "fsdp", 1)
+            down_far = other(grad_down, "seq", 2)
         else:
             pairs_two.append(out_pair)
-        grad_down = gate(grad_down, [gain_one])
-        taken = other(grad_down, "seq", 2)
+            down_above = grad_down
         own, over_x, over_y, diag_a, diag_b = grad_pieces(place, pairs_two, started)
         if waiting:
-            (result_qkv, result_out), passed = gather_settle(
-                place, block, over, (size_qkv, size_out), at + 1, [], [own]
-            )
-        downs.append(grad_down + gate(taken, [own]))
+            settled, _ = gather_settle(place, block, over, (size_qkv, size_out), at + 1, [], [own])
+            result_qkv, result_out = settled
         waiting = own, over_x, over_y, other(diag_a, "seq", 1), other(diag_b, "seq", 2)
-        small += [gain_one, gain_two, gain_head, *parts[3:6], grad_beta]
-    small += [*square_sums[: 3 * LAYERS], jnp.broadcast_to(jnp.sum(valid_rows), (1, D))]
-    packed, starts = small_rows(small)
     own, over_x, over_y, diag_a, diag_b = waiting
-    over_x, over_y = merge(over_x, over_y, diag_a, diag_b, [packed, downs[-1], *passed])
+    packed = packed + gate(packed_near, [own])
+    packed = packed + other(packed, "fsdp", 2)
+    downs = [grad_down + gate(down_far, [own]), down_above + gate(above_far, [own])]
+    over_x, over_y = merge(over_x, over_y, diag_a, diag_b, [packed, *downs])
     from_x, from_y = other(over_x, "seq", 1), other(over_y, "seq", 2)
-    packed = sum_over(gate(packed, [over_x]), "fsdp")
-    reduced = total_of(own, from_x, from_y, [packed, result_out])
+    packed = packed + other(gate(packed, [over_x]), "fsdp", 4)
+    reduced = total_of(own, from_x, from_y, [packed])
     last = scatter_chips(reduced)
     packed = sum_over(gate(packed, [reduced]), "seq")
     block, over = gather_start(scattered, [reduced])
@@ -1509,7 +1554,7 @@
         result_qkv,
         result_out,
         result_gate,
-        jnp.stack(downs[::-1]).astype(f32),
+        jnp.stack(downs).astype(f32),
         rms_stats,
     )
 

time: 891 us -> 822 us (0.923)
  waiting for transfers between devices: 252 us -> 214 us
  Pallas kernels: 429 us -> 393 us
    ppermute x97, waiting for transfers between devices: 226 us -> 182 us  [other(): lax.ppermute(block, axis, [(i, i ^ mask) for i in range(lax.axis_size(axi...]
    pallas_call x8 -> x4, Pallas kernels: 88.1 us -> 50.5 us  [the longest x2 26.8 us: gated(): pl.pallas_call(partial(gated_kernel, size=size), in_specs=[SMEM, VMEM] +...]
    unnamed x205 -> x213, local copies, waits for them, and re-layouts: 41.2 us -> 41.5 us
  transfers between devices with their start and end apart: 113 -> 113, of which waited for: 52 -> 47; matrix products, arithmetic and copies ran while one was open for 6% -> 7% of each run, Pallas kernels for 43% -> 47%
where the time goes in v3:
time: 822 us; the launch traced here: 814 us
  Pallas kernels  393 us (48%)
  waiting for transfers between devices  214 us (26%)
  starting transfers between devices  86.4 us (11%)
  local copies, waits for them, and re-layouts  55.1 us (7%)
  other arithmetic  27.9 us (3%)
  matrix products  21.2 us (3%)
  between operations  16.1 us (2%)
    ppermute x97, waiting for transfers between devices, other(): lax.ppermute(block, axis, [(i, i ^ mask) for i in range(lax.axis_size(axi...  182 us
    ppermute x97, starting transfers between devices, other(): lax.ppermute(block, axis, [(i, i ^ mask) for i in range(lax.axis_size(axi...  74.9 us
    pallas_call x4, Pallas kernels, grad_pieces(): pl.pallas_call(partial(grad_pieces_kernel, count=len(pairs)), grid_spec=p...  53 us
    pallas_call x4, Pallas kernels, norm_back(): pl.pallas_call(kernel, grid=(steps,), in_specs=[d_spec, pl.BlockSpec((D,...  51 us
    pallas_call x2, Pallas kernels, bwd_main(): pl.pallas_call(partial(bwd_main_kernel, len(moves), paired), grid=(H // T...  50 us
    unnamed x213, local copies, waits for them, and re-layouts  41.5 us
    pallas_call x2, Pallas kernels, fwd_local(): pl.pallas_call(fwd_local_kernel, grid=(H // TOGETHER,), in_specs=[col_spe...  30.9 us
    pallas_call x4, Pallas kernels, branch(): pl.pallas_call(lambda *refs: branch_kernel(*refs[:5], *refs[-4:], last=la...  30.4 us
  transfers between devices with their start and end apart: 113, of which 47 were waited for; matrix products, arithmetic and copies ran while one was open for 7% of the time, Pallas kernels for 47%

profile of v3, /device:TPU:0, one launch (start us, length us, event | category | flops | bytes accessed | tf_op | source)
XLA Modules:
  0.0 813.5 jit_solution(14984828228106171589)
XLA Ops:
  23.2 17.8 %all-gather.9.cloned.1.call-done = bf16[512,1024]{1,0:T(8,128)(2,1)} async-done(((bf16[128,1024]{1,0:T(8,128)(2,1)}), bf16[512,1024]{1,0:T(8,128)(2,1)}) %all-gather.9.cloned.1.call-update) | async-done | bytes 1048592 | tf_op jit(solution)/shard_map/all_gather | solution.py:964
  51.7 14.3 %collective-permute-done.1.x_ref = bf16[512,1024]{1,0:T(8,128)(2,1)} collective-permute-done((bf16[512,1024]{1,0:T(8,128)(2,1)}, bf16[512,1024]{1,0:T(8,128)(2,1)}, u32[]{:S(2)}, u32[]{:S(2)}) %collective-permute-start.1) | collective-permute-done | bytes 1048608 | tf_op jit(solution)/shard_map/ppermute | solution.py:731
  72.6 10.6 %collective-permute-done.4 = bf16[256,1024]{1,0:T(8,128)(2,1)} collective-permute-done((bf16[256,1024]{1,0:T(8,128)(2,1)}, bf16[256,1024]{1,0:T(8,128)(2,1)}, u32[]{:S(2)}, u32[]{:S(2)}) %collective-permute-start.4) | collective-permute-done | bytes 524320 | tf_op jit(solution)/shard_map/ppermute | solution.py:731
  89.7 11.9 %project.2 = (bf16[528,3072]{1,0:T(8,128)(2,1)}, bf16[512,128]{1,0:T(8,128)(2,1)}, bf16[4,2,128,3072]{3,2,1,0:T(8,128)(2,1)}, bf16[4,2,128,1024]{3,2,1,0:T(8,128)(2,1)}) custom-call(s32[2]{0:T(128)} %pad_add_fusion.place_ref.refs_0_, f32[16,1024]{1,0:T(8,128)} %convert_element_type.54.refs_1_.tail_ref, ...), custom_call_target="tpu_custom_call" | custom-call | bytes 36900000 | tf_op jit(solution)/shard_map/project/pallas_call | solution.py:850
  102.6 15.4 %delta_local.2 = (bf16[512,1024]{1,0:T(8,128)(2,1)}, bf16[512,1024]{1,0:T(8,128)(2,1)}, bf16[8,512,128]{2,1,0:T(8,128)(2,1)}, bf16[8,512,256]{2,1,0:T(8,128)(2,1...) custom-call(bf16[528,3072]{1,0:T(8,128)(2,1)} %get-tuple-element.189.q_ref.k_ref.v_ref.r, ...), custom_call_target="tpu_custom_call" | custom-call | bytes 53505000 | tf_op jit(solution)/shard_map/delta_local/pallas_call | solution.py:195
  176.7 13.3 %gated.2 = (bf16[512,2816]{1,0:T(8,128)(2,1)}, bf16[2,512,2816]{2,1,0:T(8,128)(2,1)}, bf16[4,2,128,5632]{3,2,1,0:T(8,128)(2,1)}) custom-call(s32[2]{0:T(128)} %pad_add_fusion.place_ref.refs_0_, bf16[512,1024]{1,0:T(8,128)(2,1)} %get-tuple-element.205.x_ref.refs_2_.refs_0_, bf16[4,128,1408]{2,1,0:T(8,128)(2,1)} %bitcast.136, ...), custom_call_target="tpu_custom_call" | custom-call | bytes 55350000 | tf_op jit(solution)/shard_map/gated/pallas_call | solution.py:903
  198.8 9.3 %branch.5 = (f32[512,1024]{1,0:T(8,128)}, bf16[512,1024]{1,0:T(8,128)(2,1)}, f32[2,1024]{1,0:T(2,128)}) custom-call(bf16[512,2816]{1,0:T(8,128)(2,1)} %get-tuple-element.206.refs_1_.refs_0_, bf16[2816,1024]{1,0:T(8,128)(2,1)} %bitcast.118, f32[512,1024]{1,0:T(8,128)} %get-tuple-element.207.refs_2_, f32[512,1]{1,0:T(8,128)} %copy.78.refs_6_.refs_3_, ...), custom_call_target="tpu_custom_call" | custom-call | bytes 18450000 | tf_op jit(solution)/shard_map/branch/pallas_call | solution.py:626
  223.5 11.8 %project.3 = (bf16[528,3072]{1,0:T(8,128)(2,1)}, bf16[512,128]{1,0:T(8,128)(2,1)}, bf16[4,2,128,3072]{3,2,1,0:T(8,128)(2,1)}, bf16[4,2,128,1024]{3,2,1,0:T(8,128)(2,1)}) custom-call(s32[2]{0:T(128)} %pad_add_fusion.place_ref.refs_0_, f32[16,1024]{1,0:T(8,128)} %copy-done.83, f32[1,1024]{1,0:T(1,128)} %get-tuple-element.361.refs_4_.gain_ref.refs_6_, ...), custom_call_target="tpu_custom_call" | custom-call | bytes 36900000 | tf_op jit(solution)/shard_map/project/pallas_call | solution.py:850
  235.3 15.5 %delta_local.3 = (bf16[512,1024]{1,0:T(8,128)(2,1)}, bf16[512,1024]{1,0:T(8,128)(2,1)}, bf16[8,512,128]{2,1,0:T(8,128)(2,1)}, bf16[8,512,256]{2,1,0:T(8,128)(2,1...) custom-call(bf16[528,3072]{1,0:T(8,128)(2,1)} %get-tuple-element.215.q_ref.k_ref.v_ref.r, ...), custom_call_target="tpu_custom_call" | custom-call | bytes 53505000 | tf_op jit(solution)/shard_map/delta_local/pallas_call | solution.py:195
  309.6 13.5 %gated.3 = (bf16[512,2816]{1,0:T(8,128)(2,1)}, bf16[2,512,2816]{2,1,0:T(8,128)(2,1)}, bf16[4,2,128,5632]{3,2,1,0:T(8,128)(2,1)}) custom-call(s32[2]{0:T(128)} %pad_add_fusion.place_ref.refs_0_, bf16[512,1024]{1,0:T(8,128)(2,1)} %get-tuple-element.231.x_ref.refs_0_, bf16[4,128,1408]{2,1,0:T(8,128)(2,1)} %bitcast.135, bf16[4,128,1408]{2,1,0:T(8,128)(2,1)} %bitcast.137, ...), custom_call_target="tpu_custom_call" | custom-call | bytes 55350000 | tf_op jit(solution)/shard_map/gated/pallas_call | solution.py:903
  330.1 10.7 %gated_back.2.refs_0_.refs_2_ = bf16[2,512,2816]{2,1,0:T(8,128)(2,1)} custom-call(bf16[512,1024]{1,0:T(8,128)(2,1)} %get-tuple-element.340.refs_0_, bf16[2816,1024]{1,0:T(8,128)(2,1)} %bitcast.120, bf16[2,512,2816]{2,1,0:T(8,128)(2,1)} %get-tuple-element.235.refs_2_, bf16[2816,1024]{1,0:T(8,128)(2,1)} %convolution_convert_fusion.1.refs_3_), custom_call_target="tpu_custom_call" | custom-call | bytes 29520000 | tf_op jit(solution)/shard_map/gated_back/pallas_call | solution.py:659
  341.3 14.4 %norm_back.4 = (f32[512,1024]{1,0:T(8,128)}, bf16[512,1024]{1,0:T(8,128)(2,1)}, f32[1,1024]{1,0:T(1,128)}) custom-call(bf16[2,512,2816]{2,1,0:T(8,128)(2,1)} %gated_back.2.refs_0_.refs_2_, bf16[1024,5632]{1,0:T(8,128)(2,1)} %bitcast.125, f32[512,1024]{1,0:T(8,128)} %get-tuple-element.233.refs_2_, f32[512,1024]{1,0:T(8,128)} %get-tuple-element.339.refs_3_, ...), custom_call_target="tpu_custom_call" | custom-call | bytes 33210000 | tf_op jit(solution)/shard_map/norm_back/pallas_call | solution.py:714
  356.7 14.1 %grad_pieces.4 = (bf16[512,1408]{1,0:T(8,128)(2,1)}, bf16[512,1408]{1,0:T(8,128)(2,1)}, bf16[512,1408]{1,0:T(8,128)(2,1)}, bf16[256,1408]{1,0:T(8,128)(2,1)}, bf16[256,1408]{1,0:T(8,128)(2,1)}) custom-call(s32[2]{0:T(128)} %pad_add_fusion.place_ref.refs_0_, bf16[512,1024]{1,0:T(8,128)(2,1)} %get-tuple-element.231.x_ref.refs_0_, ...), custom_call_target="tpu_custom_call" | custom-call | bytes 44280000 | tf_op jit(solution)/shard_map/grad_pieces/pallas_call | solution.py:1033
  414.2 25.0 %delta_back.2 = (bf16[512,3072]{1,0:T(8,128)(2,1)}, bf16[16,1024]{1,0:T(8,128)(2,1)}, bf16[16,1024]{1,0:T(8,128)(2,1)}, bf16[16,1024]{1,0:T(8,128)(2,1)}, f32[4,...) custom-call(s32[2]{0:T(128)} %pad_add_fusion.place_ref.refs_0_, ...), custom_call_target="tpu_custom_call" | custom-call | bytes 88560000 | tf_op jit(solution)/shard_map/delta_back/pallas_call | solution.py:542
  450.7 11.2 %norm_back.5 = (f32[512,1024]{1,0:T(8,128)}, bf16[512,1024]{1,0:T(8,128)(2,1)}, f32[1,1024]{1,0:T(1,128)}) custom-call(bf16[512,3072]{1,0:T(8,128)(2,1)} %fusion.5.refs_0_.refs_4_, bf16[1024,3072]{1,0:T(8,128)(2,1)} %bitcast.131, bf16[512,128]{1,0:T(8,128)(2,1)} %get-tuple-element.258.refs_2_, bf16[1024,128]{1,0:T(8,128)(2,1)} %get-tuple-element.341.beta_ref.refs_3_, ...), custom_call_target="tpu_custom_call" | custom-call | bytes 33210000 | tf_op jit(solution)/shard_map/norm_back/pallas_call | solution.py:714
  463.6 12.0 %grad_pieces.5 = (bf16[512,1024]{1,0:T(8,128)(2,1)}, bf16[512,1024]{1,0:T(8,128)(2,1)}, bf16[512,1024]{1,0:T(8,128)(2,1)}, bf16[256,1024]{1,0:T(8,128)(2,1)}, bf16[256,1024]{1,0:T(8,128)(2,1)}) custom-call(s32[2]{0:T(128)} %pad_add_fusion.place_ref.refs_0_, bf16[512,1024]{1,0:T(8,128)(2,1)} %get-tuple-element.212.normed_ref.refs_0_, ...), custom_call_target="tpu_custom_call" | custom-call | bytes 44280000 | tf_op jit(solution)/shard_map/grad_pieces/pallas_call | solution.py:1033
  499.2 10.1 %gated_back.3.refs_0_.refs_4_ = bf16[2,512,2816]{2,1,0:T(8,128)(2,1)} custom-call(bf16[512,1024]{1,0:T(8,128)(2,1)} %get-tuple-element.260.refs_0_, bf16[2816,1024]{1,0:T(8,128)(2,1)} %bitcast.119, bf16[2,512,2816]{2,1,0:T(8,128)(2,1)} %get-tuple-element.261.refs_2_, bf16[512,1024]{1,0:T(8,128)(2,1)} %get-tuple-element.268.refs_3_.refs_1_), custom_call_target="tpu_custom_call" | custom-call | bytes 29520000 | tf_op jit(solution)/shard_map/gated_back/pallas_call | solution.py:659
  509.3 14.2 %norm_back.6 = (f32[512,1024]{1,0:T(8,128)}, bf16[512,1024]{1,0:T(8,128)(2,1)}, f32[1,1024]{1,0:T(1,128)}) custom-call(bf16[2,512,2816]{2,1,0:T(8,128)(2,1)} %gated_back.3.refs_0_.refs_4_, bf16[1024,5632]{1,0:T(8,128)(2,1)} %bitcast.124, f32[512,1024]{1,0:T(8,128)} %get-tuple-element.207.refs_2_, f32[512,1024]{1,0:T(8,128)} %get-tuple-element.270.refs_3_, ...), custom_call_target="tpu_custom_call" | custom-call | bytes 33210000 | tf_op jit(solution)/shard_map/norm_back/pallas_call | solution.py:714
  540.7 17.4 %grad_pieces.6 = (bf16[512,1664]{1,0:T(8,128)(2,1)}, bf16[512,1664]{1,0:T(8,128)(2,1)}, bf16[512,1664]{1,0:T(8,128)(2,1)}, bf16[256,1664]{1,0:T(8,128)(2,1)}, bf16[256,1664]{1,0:T(8,128)(2,1)}) custom-call(s32[2]{0:T(128)} %pad_add_fusion.place_ref.refs_0_, bf16[512,1024]{1,0:T(8,128)(2,1)} %get-tuple-element.205.x_ref.refs_2_.refs_0_, ...), custom_call_target="tpu_custom_call" | custom-call | bytes 44280000 | tf_op jit(solution)/shard_map/grad_pieces/pallas_call | solution.py:1033
  609.7 25.0 %delta_back.3 = (bf16[512,3072]{1,0:T(8,128)(2,1)}, bf16[16,1024]{1,0:T(8,128)(2,1)}, bf16[16,1024]{1,0:T(8,128)(2,1)}, bf16[16,1024]{1,0:T(8,128)(2,1)}, f32[4,...) custom-call(s32[2]{0:T(128)} %pad_add_fusion.place_ref.refs_0_, ...), custom_call_target="tpu_custom_call" | custom-call | bytes 88560000 | tf_op jit(solution)/shard_map/delta_back/pallas_call | solution.py:542
  636.8 10.7 %collective-permute-done.72.x_ref = bf16[512,1664]{1,0:T(8,128)(2,1)S(1)} collective-permute-done((bf16[512,1664]{1,0:T(8,128)(2,1)}, bf16[512,1664]{1,0:T(8,128)(2,1)S(1)}, u32[]{:S(2)}, u32[]{:S(2)}) %collective-permute-start.72) | collective-permute-done | bytes 1703968 | tf_op jit(solution)/shard_map/ppermute | solution.py:731
  661.8 11.1 %norm_back.7 = (f32[512,1024]{1,0:T(8,128)}, bf16[512,1024]{1,0:T(8,128)(2,1)}, f32[1,1024]{1,0:T(1,128)}) custom-call(bf16[512,3072]{1,0:T(8,128)(2,1)} %fusion.4.refs_0_.refs_2_, bf16[1024,3072]{1,0:T(8,128)(2,1)} %bitcast.130, bf16[512,128]{1,0:T(8,128)(2,1)} %get-tuple-element.296.refs_2_, bf16[1024,128]{1,0:T(8,128)(2,1)} %get-tuple-element.342.beta_ref.refs_3_, ...), custom_call_target="tpu_custom_call" | custom-call | bytes 33210000 | tf_op jit(solution)/shard_map/norm_back/pallas_call | solution.py:714
  686.5 9.5 %grad_pieces.7 = (bf16[512,768]{1,0:T(8,128)(2,1)}, bf16[512,768]{1,0:T(8,128)(2,1)}, bf16[512,768]{1,0:T(8,128)(2,1)}, bf16[256,768]{1,0:T(8,128)(2,1)}, bf16[256,768]{1,0:T(8,128)(2,1)}) custom-call(s32[2]{0:T(128)} %pad_add_fusion.place_ref.refs_0_, bf16[512,1024]{1,0:T(8,128)(2,1)} %multiply_convert_fusion.refs_3_.normed_ref.refs_0_, ...), custom_call_target="tpu_custom_call" | custom-call | bytes 44280000 | tf_op jit(solution)/shard_map/grad_pieces/pallas_call | solution.py:1033
  717.1 10.0 %collective-permute-done.84 = f32[56,1024]{1,0:T(8,128)S(1)} collective-permute-done((f32[56,1024]{1,0:T(8,128)}, f32[56,1024]{1,0:T(8,128)S(1)}, u32[]{:S(2)}, u32[]{:S(2)}) %collective-permute-start.84) | collective-permute-done | bytes 229408 | tf_op jit(solution)/shard_map/ppermute | solution.py:731
  (565 shorter events, 468.6 us)
Async XLA Ops:
  10.2 75.7 %all-gather.11.cloned.1.call-start = ((), (), s32[]{:S(2)}) async-start(), calls=%async_computation.7 | async-start | bytes 1802240 | tf_op jit(solution)/shard_map/all_gather | solution.py:964
  13.3 154.7 %all-gather.13.cloned.1.call-start = ((), (), s32[]{:S(2)}) async-start(), calls=%async_computation.8 | async-start | bytes 1310720 | tf_op jit(solution)/shard_map/all_gather | solution.py:964
  14.0 184.8 %all-gather.17.cloned.1.call-start = ((), (), s32[]{:S(2)}) async-start(), calls=%async_computation.16 | async-start | bytes 6488064 | tf_op jit(solution)/shard_map/all_gather | solution.py:1366
  15.4 202.7 %all-gather.15.cloned.1.call-start = ((), (), s32[]{:S(2)}) async-start(), calls=%async_computation.9 | async-start | bytes 1802240 | tf_op jit(solution)/shard_map/all_gather | solution.py:964
  15.4 35.6 %collective-permute-start = (bf16[16,1024]{1,0:T(8,128)(2,1)S(1)}, bf16[16,1024]{1,0:T(8,128)(2,1)S(1)}, u32[]{:S(2)}, u32[]{:S(2)}) collective-permute-start(bf16[16,1024]{1,0:T(8,128)(2,1)S(1)} %slice_bitcast_fusion.6), channel_id=1, source_target_pairs={{0,8},{8,16},{16,24},{1,9},{9,17},{17,25},{2,10},{10,18},{18,26},{... | collective-permute-start | bytes 98312 | tf_op jit(solution)/shard_map/ppermute | solution.py:1166
  20.3 309.7 %all-gather.19.cloned.1.call-start = ((), (), s32[]{:S(2)}) async-start(), calls=%async_computation.17 | async-start | bytes 6488064 | tf_op jit(solution)/shard_map/all_gather | solution.py:1366
  85.0 359.6 %reduce-scatter.7.cloned.1.call-start = ((), (), s32[]{:S(2)}) async-start(), calls=%async_computation.10 | async-start | bytes 6488064 | tf_op jit(solution)/shard_map/reduce_scatter | solution.py:1461
  86.7 56.4 %collective-permute-start.13 = (bf16[512,1408]{1,0:T(8,128)(2,1)}, bf16[512,1408]{1,0:T(8,128)(2,1)S(1)}, u32[]{:S(2)}, u32[]{:S(2)}) collective-permute-start(bf16[512,1408]{1,0:T(8,128)(2,1)} %gate.25), channel_id=1, source_target_pairs={{0,1},{1,0},{2,3},{3,2},{4,5},{5,4},{6,7},{7,6},{8,9},{9,8},{10,11... | collective-permute-start | bytes 4325384 | tf_op jit(solution)/shard_map/ppermute | solution.py:731
  87.2 55.9 %collective-permute-start.14 = (bf16[512,1408]{1,0:T(8,128)(2,1)}, bf16[512,1408]{1,0:T(8,128)(2,1)}, u32[]{:S(2)}, u32[]{:S(2)}) collective-permute-start(bf16[512,1408]{1,0:T(8,128)(2,1)} %gate.25), channel_id=1, source_target_pairs={{0,8},{8,0},{16,24},{24,16},{1,9},{9,1},{17,25},{25,17},{2,10},{10... | collective-permute-start | bytes 4325384 | tf_op jit(solution)/shard_map/ppermute | solution.py:731
  87.8 55.3 %collective-permute-start.15 = (bf16[512,1408]{1,0:T(8,128)(2,1)}, bf16[512,1408]{1,0:T(8,128)(2,1)}, u32[]{:S(2)}, u32[]{:S(2)}) collective-permute-start(bf16[512,1408]{1,0:T(8,128)(2,1)} %gate.25), channel_id=1, source_target_pairs={{0,16},{8,24},{16,0},{24,8},{1,17},{9,25},{17,1},{25,9},{2,18},{10... | collective-permute-start | bytes 4325384 | tf_op jit(solution)/shard_map/ppermute | solution.py:731
  219.7 57.1 %collective-permute-start.37 = (bf16[512,1408]{1,0:T(8,128)(2,1)}, bf16[512,1408]{1,0:T(8,128)(2,1)S(1)}, u32[]{:S(2)}, u32[]{:S(2)}) collective-permute-start(bf16[512,1408]{1,0:T(8,128)(2,1)} %gate.31), channel_id=1, source_target_pairs={{0,1},{1,0},{2,3},{3,2},{4,5},{5,4},{6,7},{7,6},{8,9},{9,8},{10,11... | collective-permute-start | bytes 4325384 | tf_op jit(solution)/shard_map/ppermute | solution.py:731
  220.2 56.6 %collective-permute-start.38 = (bf16[512,1408]{1,0:T(8,128)(2,1)}, bf16[512,1408]{1,0:T(8,128)(2,1)S(1)}, u32[]{:S(2)}, u32[]{:S(2)}) collective-permute-start(bf16[512,1408]{1,0:T(8,128)(2,1)} %gate.31), channel_id=1, source_target_pairs={{0,8},{8,0},{16,24},{24,16},{1,9},{9,1},{17,25},{25,17},{2,10},{10... | collective-permute-start | bytes 4325384 | tf_op jit(solution)/shard_map/ppermute | solution.py:731
  222.6 54.2 %collective-permute-start.39 = (bf16[512,1408]{1,0:T(8,128)(2,1)}, bf16[512,1408]{1,0:T(8,128)(2,1)}, u32[]{:S(2)}, u32[]{:S(2)}) collective-permute-start(bf16[512,1408]{1,0:T(8,128)(2,1)} %gate.31), channel_id=1, source_target_pairs={{0,16},{8,24},{16,0},{24,8},{1,17},{9,25},{17,1},{25,9},{2,18},{10... | collective-permute-start | bytes 4325384 | tf_op jit(solution)/shard_map/ppermute | solution.py:731
  330.0 153.6 %reduce-scatter.9.cloned.1.call-start = ((), (), s32[]{:S(2)}) async-start(), calls=%async_computation.11 | async-start | bytes 1802240 | tf_op jit(solution)/shard_map/reduce_scatter | solution.py:968
  370.8 35.1 %collective-permute-start.51 = (bf16[256,1408]{1,0:T(8,128)(2,1)}, bf16[256,1408]{1,0:T(8,128)(2,1)S(1)}, u32[]{:S(2)}, u32[]{:S(2)}) collective-permute-start(bf16[256,1408]{1,0:T(8,128)(2,1)} %get-tuple-element.249), channel_id=1, source_target_pairs={{0,8},{8,0},{16,24},{24,16},{1,9},{9,1},{17,25},{25,17},{2,10},{10... | collective-permute-start | bytes 2162696 | tf_op jit(solution)/shard_map/ppermute | solution.py:731
  371.3 34.7 %collective-permute-start.52 = (bf16[256,1408]{1,0:T(8,128)(2,1)}, bf16[256,1408]{1,0:T(8,128)(2,1)}, u32[]{:S(2)}, u32[]{:S(2)}) collective-permute-start(bf16[256,1408]{1,0:T(8,128)(2,1)} %get-tuple-element.250), channel_id=1, source_target_pairs={{0,16},{8,24},{16,0},{24,8},{1,17},{9,25},{17,1},{25,9},{2,18},{10... | collective-permute-start | bytes 2162696 | tf_op jit(solution)/shard_map/ppermute | solution.py:731
  450.7 159.0 %reduce-scatter.11.cloned.1.call-start = ((), (), s32[]{:S(2)}) async-start(), calls=%async_computation.12 | async-start | bytes 1310720 | tf_op jit(solution)/shard_map/reduce_scatter | solution.py:968
  528.7 118.7 %reduce-scatter.13.cloned.1.call-start = ((), (), s32[]{:S(2)}) async-start(), calls=%async_computation.13 | async-start | bytes 6488064 | tf_op jit(solution)/shard_map/reduce_scatter | solution.py:1461
  529.3 211.1 %reduce-scatter.17.cloned.1.call-start = ((), (), s32[]{:S(2)}) async-start(), calls=%async_computation.15 | async-start | bytes 2129920 | tf_op jit(solution)/shard_map/reduce_scatter | solution.py:968
  558.1 45.3 %collective-permute-start.70 = (bf16[256,1664]{1,0:T(8,128)(2,1)}, bf16[256,1664]{1,0:T(8,128)(2,1)S(1)}, u32[]{:S(2)}, u32[]{:S(2)}) collective-permute-start(bf16[256,1664]{1,0:T(8,128)(2,1)} %get-tuple-element.287), channel_id=1, source_target_pairs={{0,8},{8,0},{16,24},{24,16},{1,9},{9,1},{17,25},{25,17},{2,10},{10... | collective-permute-start | bytes 2555912 | tf_op jit(solution)/shard_map/ppermute | solution.py:731
  558.6 44.8 %collective-permute-start.71 = (bf16[256,1664]{1,0:T(8,128)(2,1)}, bf16[256,1664]{1,0:T(8,128)(2,1)}, u32[]{:S(2)}, u32[]{:S(2)}) collective-permute-start(bf16[256,1664]{1,0:T(8,128)(2,1)} %get-tuple-element.288), channel_id=1, source_target_pairs={{0,16},{8,24},{16,0},{24,8},{1,17},{9,25},{17,1},{25,9},{2,18},{10... | collective-permute-start | bytes 2555912 | tf_op jit(solution)/shard_map/ppermute | solution.py:731
  608.5 39.0 %collective-permute-start.72 = (bf16[512,1664]{1,0:T(8,128)(2,1)}, bf16[512,1664]{1,0:T(8,128)(2,1)S(1)}, u32[]{:S(2)}, u32[]{:S(2)}) collective-permute-start(bf16[512,1664]{1,0:T(8,128)(2,1)} %get-tuple-element.289.refs_18_), channel_id=1, source_target_pairs={{0,8},{8,0},{16,24},{24,16},{1,9},{9,1},{17,25},{25,17},{2,10},{10... | collective-permute-start | bytes 5111816 | tf_op jit(solution)/shard_map/ppermute | solution.py:731
  609.2 38.3 %collective-permute-start.73 = (bf16[512,1664]{1,0:T(8,128)(2,1)}, bf16[512,1664]{1,0:T(8,128)(2,1)S(1)}, u32[]{:S(2)}, u32[]{:S(2)}) collective-permute-start(bf16[512,1664]{1,0:T(8,128)(2,1)} %get-tuple-element.291), channel_id=1, source_target_pairs={{0,16},{8,24},{16,0},{24,8},{1,17},{9,25},{17,1},{25,9},{2,18},{10... | collective-permute-start | bytes 5111816 | tf_op jit(solution)/shard_map/ppermute | solution.py:731
  655.3 132.1 %reduce-scatter.15.cloned.1.call-start = ((), (), s32[]{:S(2)}) async-start(), calls=%async_computation.14 | async-start | bytes 983040 | tf_op jit(solution)/shard_map/reduce_scatter | solution.py:968
  (194 other events, 1738.1 us)
Sparse Core Ops, SparseCore 0:
  10.3 30.6 all-gather.8
  42.5 34.4 all-gather.10
  78.6 26.8 all-gather.12
  107.0 59.9 all-gather.16
  168.4 34.4 all-gather.14
  204.3 59.2 all-gather.18
  330.1 63.7 reduce-scatter.6
  450.8 32.7 reduce-scatter.8
  528.9 25.0 reduce-scatter.10
  556.2 63.5 reduce-scatter.12
  655.5 36.2 reduce-scatter.16
  765.5 21.8 reduce-scatter.14

commit v4 on v3

--- a/solution.py
+++ b/solution.py
@@ -1401,9 +1401,9 @@
         )
         partner = other(total, "seq", 1)
         reads, local_out = fwd_read(qn, kn, wu, dcol, drow)
-        pair = pair_state(pair_forward_kernel, place, total, partner, after=[reads])
+        came = finish(*coming, [reads])
+        pair = pair_state(pair_forward_kernel, place, total, partner, after=came[3])
         far = other(pair, "seq", 2)
-        came = finish(*coming, [far])
         state, mixed, attended = fwd_state(
             place, True, [partner], far, pre, reads, local_out, head_gain[at][None], [*came[1], *came[3]]
         )

time: 822 us -> 818 us (level)
    unnamed x213 -> x209, local copies, waits for them, and re-layouts: 41.5 us -> 42.4 us
  transfers between devices with their start and end apart: 113 -> 113, of which waited for: 47 -> 43; matrix products, arithmetic and copies ran while one was open for 7% -> 8% of each run, Pallas kernels for 47% -> 47%
where the time goes in v4:
time: 818 us; the launch traced here: 809 us
  Pallas kernels  393 us (48%)
  waiting for transfers between devices  210 us (26%)
  starting transfers between devices  83.5 us (10%)
  local copies, waits for them, and re-layouts  56.8 us (7%)
  other arithmetic  28.5 us (3%)
  matrix products  21.3 us (3%)
  between operations  16.1 us (2%)
    ppermute x97, waiting for transfers between devices, other(): lax.ppermute(block, axis, [(i, i ^ mask) for i in range(lax.axis_size(axi...  178 us
    ppermute x97, starting transfers between devices, other(): lax.ppermute(block, axis, [(i, i ^ mask) for i in range(lax.axis_size(axi...  72.8 us
    pallas_call x4, Pallas kernels, grad_pieces(): pl.pallas_call(partial(grad_pieces_kernel, count=len(pairs)), grid_spec=p...  53 us
    pallas_call x4, Pallas kernels, norm_back(): pl.pallas_call(kernel, grid=(steps,), in_specs=[d_spec, pl.BlockSpec((D,...  51 us
    pallas_call x2, Pallas kernels, bwd_main(): pl.pallas_call(partial(bwd_main_kernel, len(moves), paired), grid=(H // T...  50 us
    unnamed x209, local copies, waits for them, and re-layouts  42.4 us
    pallas_call x2, Pallas kernels, fwd_local(): pl.pallas_call(fwd_local_kernel, grid=(H // TOGETHER,), in_specs=[col_spe...  31 us
    pallas_call x4, Pallas kernels, branch(): pl.pallas_call(lambda *refs: branch_kernel(*refs[:5], *refs[-4:], last=la...  30.3 us
  transfers between devices with their start and end apart: 113, of which 43 were waited for; matrix products, arithmetic and copies ran while one was open for 8% of the time, Pallas kernels for 47%

profile of v4, /device:TPU:0, one launch (start us, length us, event | category | flops | bytes accessed | tf_op | source)
XLA Modules:
  0.0 809.2 jit_solution(3003048806417636529)
XLA Ops:
  24.4 16.5 %all-gather.9.cloned.1.call-done = bf16[512,1024]{1,0:T(8,128)(2,1)} async-done(((bf16[128,1024]{1,0:T(8,128)(2,1)}), bf16[512,1024]{1,0:T(8,128)(2,1)}) %all-gather.9.cloned.1.call-update) | async-done | bytes 1048592 | tf_op jit(solution)/shard_map/all_gather | solution.py:964
  51.1 15.0 %collective-permute-done.1.x_ref = bf16[512,1024]{1,0:T(8,128)(2,1)} collective-permute-done((bf16[512,1024]{1,0:T(8,128)(2,1)}, bf16[512,1024]{1,0:T(8,128)(2,1)}, u32[]{:S(2)}, u32[]{:S(2)}) %collective-permute-start.1) | collective-permute-done | bytes 1048608 | tf_op jit(solution)/shard_map/ppermute | solution.py:731
  72.5 10.5 %collective-permute-done.4 = bf16[256,1024]{1,0:T(8,128)(2,1)S(1)} collective-permute-done((bf16[256,1024]{1,0:T(8,128)(2,1)}, bf16[256,1024]{1,0:T(8,128)(2,1)S(1)}, u32[]{:S(2)}, u32[]{:S(2)}) %collective-permute-start.4) | collective-permute-done | bytes 524320 | tf_op jit(solution)/shard_map/ppermute | solution.py:731
  94.9 11.7 %project.2 = (bf16[528,3072]{1,0:T(8,128)(2,1)}, bf16[512,128]{1,0:T(8,128)(2,1)}, bf16[4,2,128,3072]{3,2,1,0:T(8,128)(2,1)}, bf16[4,2,128,1024]{3,2,1,0:T(8,128)(2,1)}) custom-call(s32[2]{0:T(128)} %pad_add_fusion.place_ref.refs_0_, f32[16,1024]{1,0:T(8,128)} %convert_element_type.54.refs_1_.tail_ref, ...), custom_call_target="tpu_custom_call" | custom-call | bytes 36900000 | tf_op jit(solution)/shard_map/project/pallas_call | solution.py:850
  106.7 15.5 %delta_local.2 = (bf16[512,1024]{1,0:T(8,128)(2,1)}, bf16[512,1024]{1,0:T(8,128)(2,1)}, bf16[8,512,128]{2,1,0:T(8,128)(2,1)}, bf16[8,512,256]{2,1,0:T(8,128)(2,1...) custom-call(bf16[528,3072]{1,0:T(8,128)(2,1)} %get-tuple-element.189.q_ref.k_ref.v_ref.r, ...), custom_call_target="tpu_custom_call" | custom-call | bytes 53505000 | tf_op jit(solution)/shard_map/delta_local/pallas_call | solution.py:195
  134.1 11.8 %collective-permute-done.11.refs_2_.refs_0_ = bf16[8,128,256]{2,1,0:T(8,128)(2,1)S(1)} collective-permute-done((bf16[8,128,256]{2,1,0:T(8,128)(2,1)}, bf16[8,128,256]{2,1,0:T(8,128)(2,1)S(1)}, u32[]{:S(2)}, u32[]{:S(2)}) %collective-permute-start.11) | collective-permute-done | bytes 524320 | tf_op jit(solution)/shard_map/ppermute | solution.py:731
  175.6 13.4 %gated.2 = (bf16[512,2816]{1,0:T(8,128)(2,1)}, bf16[2,512,2816]{2,1,0:T(8,128)(2,1)}, bf16[4,2,128,5632]{3,2,1,0:T(8,128)(2,1)}) custom-call(s32[2]{0:T(128)} %pad_add_fusion.place_ref.refs_0_, bf16[512,1024]{1,0:T(8,128)(2,1)} %get-tuple-element.205.x_ref.refs_2_.refs_0_, bf16[4,128,1408]{2,1,0:T(8,128)(2,1)} %bitcast.136, ...), custom_call_target="tpu_custom_call" | custom-call | bytes 55350000 | tf_op jit(solution)/shard_map/gated/pallas_call | solution.py:903
  227.2 11.9 %project.3 = (bf16[528,3072]{1,0:T(8,128)(2,1)}, bf16[512,128]{1,0:T(8,128)(2,1)}, bf16[4,2,128,3072]{3,2,1,0:T(8,128)(2,1)}, bf16[4,2,128,1024]{3,2,1,0:T(8,128)(2,1)}) custom-call(s32[2]{0:T(128)} %pad_add_fusion.place_ref.refs_0_, f32[16,1024]{1,0:T(8,128)} %copy-done.81, f32[1,1024]{1,0:T(1,128)} %get-tuple-element.361.refs_4_.gain_ref.refs_6_, ...), custom_call_target="tpu_custom_call" | custom-call | bytes 36900000 | tf_op jit(solution)/shard_map/project/pallas_call | solution.py:850
  239.1 15.5 %delta_local.3 = (bf16[512,1024]{1,0:T(8,128)(2,1)}, bf16[512,1024]{1,0:T(8,128)(2,1)}, bf16[8,512,128]{2,1,0:T(8,128)(2,1)}, bf16[8,512,256]{2,1,0:T(8,128)(2,1...) custom-call(bf16[528,3072]{1,0:T(8,128)(2,1)} %get-tuple-element.215.q_ref.k_ref.v_ref.r, ...), custom_call_target="tpu_custom_call" | custom-call | bytes 53505000 | tf_op jit(solution)/shard_map/delta_local/pallas_call | solution.py:195
  266.4 12.4 %collective-permute-done.35.refs_2_.refs_0_ = bf16[8,128,256]{2,1,0:T(8,128)(2,1)S(1)} collective-permute-done((bf16[8,128,256]{2,1,0:T(8,128)(2,1)}, bf16[8,128,256]{2,1,0:T(8,128)(2,1)S(1)}, u32[]{:S(2)}, u32[]{:S(2)}) %collective-permute-start.35) | collective-permute-done | bytes 524320 | tf_op jit(solution)/shard_map/ppermute | solution.py:731
  304.5 13.5 %gated.3 = (bf16[512,2816]{1,0:T(8,128)(2,1)}, bf16[2,512,2816]{2,1,0:T(8,128)(2,1)}, bf16[4,2,128,5632]{3,2,1,0:T(8,128)(2,1)}) custom-call(s32[2]{0:T(128)} %pad_add_fusion.place_ref.refs_0_, bf16[512,1024]{1,0:T(8,128)(2,1)} %get-tuple-element.231.x_ref.refs_0_, bf16[4,128,1408]{2,1,0:T(8,128)(2,1)} %bitcast.135, bf16[4,128,1408]{2,1,0:T(8,128)(2,1)} %bitcast.137, ...), custom_call_target="tpu_custom_call" | custom-call | bytes 55350000 | tf_op jit(solution)/shard_map/gated/pallas_call | solution.py:903
  324.9 10.6 %gated_back.2.refs_0_.refs_2_ = bf16[2,512,2816]{2,1,0:T(8,128)(2,1)} custom-call(bf16[512,1024]{1,0:T(8,128)(2,1)} %get-tuple-element.340.refs_0_, bf16[2816,1024]{1,0:T(8,128)(2,1)} %bitcast.120, bf16[2,512,2816]{2,1,0:T(8,128)(2,1)} %get-tuple-element.235.refs_2_, bf16[2816,1024]{1,0:T(8,128)(2,1)} %convolution_convert_fusion.1.refs_3_), custom_call_target="tpu_custom_call" | custom-call | bytes 29520000 | tf_op jit(solution)/shard_map/gated_back/pallas_call | solution.py:659
  336.0 14.5 %norm_back.4 = (f32[512,1024]{1,0:T(8,128)}, bf16[512,1024]{1,0:T(8,128)(2,1)}, f32[1,1024]{1,0:T(1,128)}) custom-call(bf16[2,512,2816]{2,1,0:T(8,128)(2,1)} %gated_back.2.refs_0_.refs_2_, bf16[1024,5632]{1,0:T(8,128)(2,1)} %bitcast.125, f32[512,1024]{1,0:T(8,128)} %get-tuple-element.233.refs_2_, f32[512,1024]{1,0:T(8,128)} %get-tuple-element.339.refs_3_, ...), custom_call_target="tpu_custom_call" | custom-call | bytes 33210000 | tf_op jit(solution)/shard_map/norm_back/pallas_call | solution.py:714
  351.5 14.1 %grad_pieces.4 = (bf16[512,1408]{1,0:T(8,128)(2,1)}, bf16[512,1408]{1,0:T(8,128)(2,1)}, bf16[512,1408]{1,0:T(8,128)(2,1)}, bf16[256,1408]{1,0:T(8,128)(2,1)}, bf16[256,1408]{1,0:T(8,128)(2,1)}) custom-call(s32[2]{0:T(128)} %pad_add_fusion.place_ref.refs_0_, bf16[512,1024]{1,0:T(8,128)(2,1)} %get-tuple-element.231.x_ref.refs_0_, ...), custom_call_target="tpu_custom_call" | custom-call | bytes 44280000 | tf_op jit(solution)/shard_map/grad_pieces/pallas_call | solution.py:1033
  408.7 25.0 %delta_back.2 = (bf16[512,3072]{1,0:T(8,128)(2,1)}, bf16[16,1024]{1,0:T(8,128)(2,1)}, bf16[16,1024]{1,0:T(8,128)(2,1)}, bf16[16,1024]{1,0:T(8,128)(2,1)}, f32[4,...) custom-call(s32[2]{0:T(128)} %pad_add_fusion.place_ref.refs_0_, ...), custom_call_target="tpu_custom_call" | custom-call | bytes 88560000 | tf_op jit(solution)/shard_map/delta_back/pallas_call | solution.py:542
  446.1 11.2 %norm_back.5 = (f32[512,1024]{1,0:T(8,128)}, bf16[512,1024]{1,0:T(8,128)(2,1)}, f32[1,1024]{1,0:T(1,128)}) custom-call(bf16[512,3072]{1,0:T(8,128)(2,1)} %fusion.5.refs_0_.refs_4_, bf16[1024,3072]{1,0:T(8,128)(2,1)} %bitcast.131, bf16[512,128]{1,0:T(8,128)(2,1)} %get-tuple-element.258.refs_2_, bf16[1024,128]{1,0:T(8,128)(2,1)} %get-tuple-element.341.beta_ref.refs_3_, ...), custom_call_target="tpu_custom_call" | custom-call | bytes 33210000 | tf_op jit(solution)/shard_map/norm_back/pallas_call | solution.py:714
  458.9 12.0 %grad_pieces.5 = (bf16[512,1024]{1,0:T(8,128)(2,1)}, bf16[512,1024]{1,0:T(8,128)(2,1)}, bf16[512,1024]{1,0:T(8,128)(2,1)}, bf16[256,1024]{1,0:T(8,128)(2,1)}, bf16[256,1024]{1,0:T(8,128)(2,1)}) custom-call(s32[2]{0:T(128)} %pad_add_fusion.place_ref.refs_0_, bf16[512,1024]{1,0:T(8,128)(2,1)} %get-tuple-element.212.normed_ref.refs_0_, ...), custom_call_target="tpu_custom_call" | custom-call | bytes 44280000 | tf_op jit(solution)/shard_map/grad_pieces/pallas_call | solution.py:1033
  494.7 10.1 %gated_back.3.refs_0_.refs_4_ = bf16[2,512,2816]{2,1,0:T(8,128)(2,1)} custom-call(bf16[512,1024]{1,0:T(8,128)(2,1)} %get-tuple-element.260.refs_0_, bf16[2816,1024]{1,0:T(8,128)(2,1)} %bitcast.119, bf16[2,512,2816]{2,1,0:T(8,128)(2,1)} %get-tuple-element.261.refs_2_, bf16[512,1024]{1,0:T(8,128)(2,1)} %get-tuple-element.268.refs_3_.refs_1_), custom_call_target="tpu_custom_call" | custom-call | bytes 29520000 | tf_op jit(solution)/shard_map/gated_back/pallas_call | solution.py:659
  504.8 14.2 %norm_back.6 = (f32[512,1024]{1,0:T(8,128)}, bf16[512,1024]{1,0:T(8,128)(2,1)}, f32[1,1024]{1,0:T(1,128)}) custom-call(bf16[2,512,2816]{2,1,0:T(8,128)(2,1)} %gated_back.3.refs_0_.refs_4_, bf16[1024,5632]{1,0:T(8,128)(2,1)} %bitcast.124, f32[512,1024]{1,0:T(8,128)} %get-tuple-element.207.refs_2_, f32[512,1024]{1,0:T(8,128)} %get-tuple-element.270.refs_3_, ...), custom_call_target="tpu_custom_call" | custom-call | bytes 33210000 | tf_op jit(solution)/shard_map/norm_back/pallas_call | solution.py:714
  536.3 17.3 %grad_pieces.6 = (bf16[512,1664]{1,0:T(8,128)(2,1)}, bf16[512,1664]{1,0:T(8,128)(2,1)}, bf16[512,1664]{1,0:T(8,128)(2,1)}, bf16[256,1664]{1,0:T(8,128)(2,1)}, bf16[256,1664]{1,0:T(8,128)(2,1)}) custom-call(s32[2]{0:T(128)} %pad_add_fusion.place_ref.refs_0_, bf16[512,1024]{1,0:T(8,128)(2,1)} %get-tuple-element.205.x_ref.refs_2_.refs_0_, ...), custom_call_target="tpu_custom_call" | custom-call | bytes 44280000 | tf_op jit(solution)/shard_map/grad_pieces/pallas_call | solution.py:1033
  605.2 25.0 %delta_back.3 = (bf16[512,3072]{1,0:T(8,128)(2,1)}, bf16[16,1024]{1,0:T(8,128)(2,1)}, bf16[16,1024]{1,0:T(8,128)(2,1)}, bf16[16,1024]{1,0:T(8,128)(2,1)}, f32[4,...) custom-call(s32[2]{0:T(128)} %pad_add_fusion.place_ref.refs_0_, ...), custom_call_target="tpu_custom_call" | custom-call | bytes 88560000 | tf_op jit(solution)/shard_map/delta_back/pallas_call | solution.py:542
  632.3 10.7 %collective-permute-done.72.x_ref = bf16[512,1664]{1,0:T(8,128)(2,1)S(1)} collective-permute-done((bf16[512,1664]{1,0:T(8,128)(2,1)}, bf16[512,1664]{1,0:T(8,128)(2,1)S(1)}, u32[]{:S(2)}, u32[]{:S(2)}) %collective-permute-start.72) | collective-permute-done | bytes 1703968 | tf_op jit(solution)/shard_map/ppermute | solution.py:731
  657.4 11.1 %norm_back.7 = (f32[512,1024]{1,0:T(8,128)}, bf16[512,1024]{1,0:T(8,128)(2,1)}, f32[1,1024]{1,0:T(1,128)}) custom-call(bf16[512,3072]{1,0:T(8,128)(2,1)} %fusion.4.refs_0_.refs_2_, bf16[1024,3072]{1,0:T(8,128)(2,1)} %bitcast.130, bf16[512,128]{1,0:T(8,128)(2,1)} %get-tuple-element.296.refs_2_, bf16[1024,128]{1,0:T(8,128)(2,1)} %get-tuple-element.342.beta_ref.refs_3_, ...), custom_call_target="tpu_custom_call" | custom-call | bytes 33210000 | tf_op jit(solution)/shard_map/norm_back/pallas_call | solution.py:714
  712.8 9.9 %collective-permute-done.84 = f32[56,1024]{1,0:T(8,128)S(1)} collective-permute-done((f32[56,1024]{1,0:T(8,128)}, f32[56,1024]{1,0:T(8,128)S(1)}, u32[]{:S(2)}, u32[]{:S(2)}) %collective-permute-start.84) | collective-permute-done | bytes 229408 | tf_op jit(solution)/shard_map/ppermute | solution.py:731
  (561 shorter events, 459.6 us)
Async XLA Ops:
  10.2 74.1 %all-gather.11.cloned.1.call-start = ((), (), s32[]{:S(2)}) async-start(), calls=%async_computation.7 | async-start | bytes 1802240 | tf_op jit(solution)/shard_map/all_gather | solution.py:964
  13.2 152.2 %all-gather.13.cloned.1.call-start = ((), (), s32[]{:S(2)}) async-start(), calls=%async_computation.8 | async-start | bytes 1310720 | tf_op jit(solution)/shard_map/all_gather | solution.py:964
  14.0 182.5 %all-gather.17.cloned.1.call-start = ((), (), s32[]{:S(2)}) async-start(), calls=%async_computation.16 | async-start | bytes 6488064 | tf_op jit(solution)/shard_map/all_gather | solution.py:1366
  15.3 198.6 %all-gather.15.cloned.1.call-start = ((), (), s32[]{:S(2)}) async-start(), calls=%async_computation.9 | async-start | bytes 1802240 | tf_op jit(solution)/shard_map/all_gather | solution.py:964
  15.4 35.0 %collective-permute-start = (bf16[16,1024]{1,0:T(8,128)(2,1)S(1)}, bf16[16,1024]{1,0:T(8,128)(2,1)S(1)}, u32[]{:S(2)}, u32[]{:S(2)}) collective-permute-start(bf16[16,1024]{1,0:T(8,128)(2,1)S(1)} %slice_bitcast_fusion.6), channel_id=1, source_target_pairs={{0,8},{8,16},{16,24},{1,9},{9,17},{17,25},{2,10},{10,18},{18,26},{... | collective-permute-start | bytes 98312 | tf_op jit(solution)/shard_map/ppermute | solution.py:1166
  20.3 304.6 %all-gather.19.cloned.1.call-start = ((), (), s32[]{:S(2)}) async-start(), calls=%async_computation.17 | async-start | bytes 6488064 | tf_op jit(solution)/shard_map/all_gather | solution.py:1366
  87.2 39.5 %collective-permute-start.12 = (bf16[512,1408]{1,0:T(8,128)(2,1)}, bf16[512,1408]{1,0:T(8,128)(2,1)}, u32[]{:S(2)}, u32[]{:S(2)}) collective-permute-start(bf16[512,1408]{1,0:T(8,128)(2,1)} %gate.25), channel_id=1, source_target_pairs={{0,8},{8,0},{16,24},{24,16},{1,9},{9,1},{17,25},{25,17},{2,10},{10... | collective-permute-start | bytes 4325384 | tf_op jit(solution)/shard_map/ppermute | solution.py:731
  87.8 38.9 %collective-permute-start.13 = (bf16[512,1408]{1,0:T(8,128)(2,1)}, bf16[512,1408]{1,0:T(8,128)(2,1)}, u32[]{:S(2)}, u32[]{:S(2)}) collective-permute-start(bf16[512,1408]{1,0:T(8,128)(2,1)} %gate.25), channel_id=1, source_target_pairs={{0,16},{8,24},{16,0},{24,8},{1,17},{9,25},{17,1},{25,9},{2,18},{10... | collective-permute-start | bytes 4325384 | tf_op jit(solution)/shard_map/ppermute | solution.py:731
  88.7 38.0 %collective-permute-start.14 = (bf16[512,1408]{1,0:T(8,128)(2,1)}, bf16[512,1408]{1,0:T(8,128)(2,1)S(1)}, u32[]{:S(2)}, u32[]{:S(2)}) collective-permute-start(bf16[512,1408]{1,0:T(8,128)(2,1)} %gate.25), channel_id=1, source_target_pairs={{0,1},{1,0},{2,3},{3,2},{4,5},{5,4},{6,7},{7,6},{8,9},{9,8},{10,11... | collective-permute-start | bytes 4325384 | tf_op jit(solution)/shard_map/ppermute | solution.py:731
  88.8 350.7 %reduce-scatter.7.cloned.1.call-start = ((), (), s32[]{:S(2)}) async-start(), calls=%async_computation.10 | async-start | bytes 6488064 | tf_op jit(solution)/shard_map/reduce_scatter | solution.py:1461
  217.3 42.0 %collective-permute-start.36 = (bf16[512,1408]{1,0:T(8,128)(2,1)}, bf16[512,1408]{1,0:T(8,128)(2,1)S(1)}, u32[]{:S(2)}, u32[]{:S(2)}) collective-permute-start(bf16[512,1408]{1,0:T(8,128)(2,1)} %gate.31), channel_id=1, source_target_pairs={{0,8},{8,0},{16,24},{24,16},{1,9},{9,1},{17,25},{25,17},{2,10},{10... | collective-permute-start | bytes 4325384 | tf_op jit(solution)/shard_map/ppermute | solution.py:731
  219.6 39.6 %collective-permute-start.37 = (bf16[512,1408]{1,0:T(8,128)(2,1)}, bf16[512,1408]{1,0:T(8,128)(2,1)}, u32[]{:S(2)}, u32[]{:S(2)}) collective-permute-start(bf16[512,1408]{1,0:T(8,128)(2,1)} %gate.31), channel_id=1, source_target_pairs={{0,16},{8,24},{16,0},{24,8},{1,17},{9,25},{17,1},{25,9},{2,18},{10... | collective-permute-start | bytes 4325384 | tf_op jit(solution)/shard_map/ppermute | solution.py:731
  221.0 38.3 %collective-permute-start.38 = (bf16[512,1408]{1,0:T(8,128)(2,1)}, bf16[512,1408]{1,0:T(8,128)(2,1)S(1)}, u32[]{:S(2)}, u32[]{:S(2)}) collective-permute-start(bf16[512,1408]{1,0:T(8,128)(2,1)} %gate.31), channel_id=1, source_target_pairs={{0,1},{1,0},{2,3},{3,2},{4,5},{5,4},{6,7},{7,6},{8,9},{9,8},{10,11... | collective-permute-start | bytes 4325384 | tf_op jit(solution)/shard_map/ppermute | solution.py:731
  324.8 154.3 %reduce-scatter.9.cloned.1.call-start = ((), (), s32[]{:S(2)}) async-start(), calls=%async_computation.11 | async-start | bytes 1802240 | tf_op jit(solution)/shard_map/reduce_scatter | solution.py:968
  365.6 35.2 %collective-permute-start.51 = (bf16[256,1408]{1,0:T(8,128)(2,1)}, bf16[256,1408]{1,0:T(8,128)(2,1)S(1)}, u32[]{:S(2)}, u32[]{:S(2)}) collective-permute-start(bf16[256,1408]{1,0:T(8,128)(2,1)} %get-tuple-element.249), channel_id=1, source_target_pairs={{0,8},{8,0},{16,24},{24,16},{1,9},{9,1},{17,25},{25,17},{2,10},{10... | collective-permute-start | bytes 2162696 | tf_op jit(solution)/shard_map/ppermute | solution.py:731
  367.0 33.8 %collective-permute-start.52 = (bf16[256,1408]{1,0:T(8,128)(2,1)}, bf16[256,1408]{1,0:T(8,128)(2,1)}, u32[]{:S(2)}, u32[]{:S(2)}) collective-permute-start(bf16[256,1408]{1,0:T(8,128)(2,1)} %get-tuple-element.250), channel_id=1, source_target_pairs={{0,16},{8,24},{16,0},{24,8},{1,17},{9,25},{17,1},{25,9},{2,18},{10... | collective-permute-start | bytes 2162696 | tf_op jit(solution)/shard_map/ppermute | solution.py:731
  446.0 159.2 %reduce-scatter.11.cloned.1.call-start = ((), (), s32[]{:S(2)}) async-start(), calls=%async_computation.12 | async-start | bytes 1310720 | tf_op jit(solution)/shard_map/reduce_scatter | solution.py:968
  524.3 118.7 %reduce-scatter.13.cloned.1.call-start = ((), (), s32[]{:S(2)}) async-start(), calls=%async_computation.13 | async-start | bytes 6488064 | tf_op jit(solution)/shard_map/reduce_scatter | solution.py:1461
  524.9 211.1 %reduce-scatter.17.cloned.1.call-start = ((), (), s32[]{:S(2)}) async-start(), calls=%async_computation.15 | async-start | bytes 2129920 | tf_op jit(solution)/shard_map/reduce_scatter | solution.py:968
  553.6 45.3 %collective-permute-start.70 = (bf16[256,1664]{1,0:T(8,128)(2,1)}, bf16[256,1664]{1,0:T(8,128)(2,1)S(1)}, u32[]{:S(2)}, u32[]{:S(2)}) collective-permute-start(bf16[256,1664]{1,0:T(8,128)(2,1)} %get-tuple-element.287), channel_id=1, source_target_pairs={{0,8},{8,0},{16,24},{24,16},{1,9},{9,1},{17,25},{25,17},{2,10},{10... | collective-permute-start | bytes 2555912 | tf_op jit(solution)/shard_map/ppermute | solution.py:731
  554.2 44.8 %collective-permute-start.71 = (bf16[256,1664]{1,0:T(8,128)(2,1)}, bf16[256,1664]{1,0:T(8,128)(2,1)}, u32[]{:S(2)}, u32[]{:S(2)}) collective-permute-start(bf16[256,1664]{1,0:T(8,128)(2,1)} %get-tuple-element.288), channel_id=1, source_target_pairs={{0,16},{8,24},{16,0},{24,8},{1,17},{9,25},{17,1},{25,9},{2,18},{10... | collective-permute-start | bytes 2555912 | tf_op jit(solution)/shard_map/ppermute | solution.py:731
  604.0 39.0 %collective-permute-start.72 = (bf16[512,1664]{1,0:T(8,128)(2,1)}, bf16[512,1664]{1,0:T(8,128)(2,1)S(1)}, u32[]{:S(2)}, u32[]{:S(2)}) collective-permute-start(bf16[512,1664]{1,0:T(8,128)(2,1)} %get-tuple-element.289.refs_18_), channel_id=1, source_target_pairs={{0,8},{8,0},{16,24},{24,16},{1,9},{9,1},{17,25},{25,17},{2,10},{10... | collective-permute-start | bytes 5111816 | tf_op jit(solution)/shard_map/ppermute | solution.py:731
  604.7 38.3 %collective-permute-start.73 = (bf16[512,1664]{1,0:T(8,128)(2,1)}, bf16[512,1664]{1,0:T(8,128)(2,1)S(1)}, u32[]{:S(2)}, u32[]{:S(2)}) collective-permute-start(bf16[512,1664]{1,0:T(8,128)(2,1)} %get-tuple-element.291), channel_id=1, source_target_pairs={{0,16},{8,24},{16,0},{24,8},{1,17},{9,25},{17,1},{25,9},{2,18},{10... | collective-permute-start | bytes 5111816 | tf_op jit(solution)/shard_map/ppermute | solution.py:731
  650.9 132.1 %reduce-scatter.15.cloned.1.call-start = ((), (), s32[]{:S(2)}) async-start(), calls=%async_computation.14 | async-start | bytes 983040 | tf_op jit(solution)/shard_map/reduce_scatter | solution.py:968
  (192 other events, 1855.0 us)
Sparse Core Ops, SparseCore 0:
  10.3 30.6 all-gather.8
  42.5 34.4 all-gather.10
  78.6 26.7 all-gather.12
  106.9 60.7 all-gather.16
  169.1 33.3 all-gather.14
  204.0 59.2 all-gather.18
  325.0 64.0 reduce-scatter.6
  446.2 32.8 reduce-scatter.8
  524.4 24.6 reduce-scatter.10
  551.4 63.5 reduce-scatter.12
  651.1 36.2 reduce-scatter.16
  761.1 21.9 reduce-scatter.14
